TPU v7x, 32 devices: a whole 2x2x4 slice. The times are simulated.
32 devices in a mesh: seq: 8 (over z, x), mp: 4 (over y, core).
Axes of the slice: x: 2, y: 2, z: 4, core: 2. Of those that a mesh axis runs over, the one named last changes fastest.
Arguments:
- inputs: bfloat16 [8192, 7168], P('seq')
- norm_gain: float32 [7168], replicated, may hold values from 0.1 to 1.9
- qkv_weight: bfloat16 [7168, 3, 3584], P('seq', None, 'mp'), may hold values from -0.0625 to 0.0625
- adapter_down: bfloat16 [7168, 128], P('seq'), may hold values from -0.0625 to 0.0625
- adapter_up: bfloat16 [3, 128, 3584], P(None, None, 'mp'), may hold values from -0.5 to 0.5
- out_weight: bfloat16 [3584, 3584], P('mp', 'seq'), may hold values from -0.5 to 0.5
- cache_keys: bfloat16 [16, 256, 3584], P('seq', None, 'mp')
- cache_values: bfloat16 [16, 256, 3584], P('seq', None, 'mp'), may hold values from -6 to 6
- cache_lengths: int32 [4], replicated, may hold values from 1 to 1024, 2560 in all
- block_perm: int32 [16], replicated, may hold values from 0 to 15, each once
Outputs:
- block_out: bfloat16 [8192, 3584], P('seq', 'mp')
Inputs may be any that keep to these rules, and one draw needn't show every extreme that they name: `cache_lengths`: each request has at least one cached position, and some request fills all of its 4 blocks. `block_perm`: each logical block appears once.
All inputs are finite; a program needn't handle non-finite values.
Results may differ from a plain program's by a relative error of at most 0.025.
Values may be sent and summed in bfloat16 or wider, within the bound.
No kernel may reach another device: no remote copies, remote signals or barrier semaphores. Data moves between devices by JAX's collectives and lax.ppermute only.
A program may use at most 384 MiB of HBM per device.

v0:
```python
import jax
import jax.numpy as jnp
from jax import lax
from jax.sharding import PartitionSpec as P

HD = 224
REQS = 4
QLEN = 2048


lowest = -1e30


def lookup(small_table, positions_of):
    hits = positions_of[..., None] == jnp.arange(small_table.shape[0], dtype=jnp.int32)
    return jnp.sum(jnp.where(hits, small_table, 0), axis=-1)


def query_meta(token_index, lengths):
    request = token_index // QLEN
    return (request, lookup(lengths, request) + token_index % QLEN)


def key_meta(row_index, layout, permutation, lengths):
    cache_rows, block_size, tok_dev, max_blocks = layout
    rows_dev = cache_rows + tok_dev
    device = row_index // rows_dev
    local_row = row_index % rows_dev
    block_index = (
        device * (cache_rows // block_size) + jnp.minimum(local_row, cache_rows - 1) // block_size
    )
    logical = lookup(permutation, block_index)
    request = logical // max_blocks
    position = logical % max_blocks * block_size + local_row % block_size
    cached_live = position < lookup(lengths, request)
    new_req, new_pos = query_meta(device * tok_dev + local_row - cache_rows, lengths)
    in_cache = local_row < cache_rows
    key_req = jnp.where(in_cache, jnp.where(cached_live, request, -1), new_req)
    return (key_req, jnp.where(in_cache, position, new_pos))


def attend(softmax_state, queries, query_info, key_rows, value_rows, key_info, head_dim):
    query_req, query_pos = query_info
    key_req, key_pos = key_info
    visible = (key_req[None, :] == query_req[:, None]) & (key_pos[None, :] <= query_pos[:, None])
    query_count = queries.shape[0]
    key_count = key_rows.shape[0]
    head_count = queries.shape[1] // head_dim
    summed, largest, weight_sum = softmax_state
    scores = jnp.einsum(
        "qhd,khd->hqk",
        queries.reshape(query_count, head_count, head_dim),
        key_rows.reshape(key_count, head_count, head_dim),
        preferred_element_type=jnp.float32,
    ) * head_dim ** (-0.5)
    scores = jnp.where(visible[None], scores, lowest)
    new_largest = jnp.maximum(largest, jnp.max(scores, axis=-1))
    weights = jnp.where(visible[None], jnp.exp(scores - new_largest[..., None]), 0.0)
    weight_sum = jnp.sum(weights, axis=-1)
    summed = jnp.einsum(
        "hqk,khd->hqd",
        weights.astype(jnp.bfloat16),
        value_rows.reshape(key_count, head_count, head_dim),
        preferred_element_type=jnp.float32,
    )
    return (summed, new_largest, weight_sum)


def per_device(
    inputs,
    norm_gain,
    qkv_weight,
    adapter_down,
    adapter_up,
    out_weight,
    cache_keys,
    cache_values,
    cache_lengths,
    block_perm,
):
    tok_dev = inputs.shape[0]
    widened = inputs.astype(jnp.float32)
    normed = (
        widened * lax.rsqrt(jnp.mean(widened * widened, axis=-1, keepdims=True) + 1e-05) * norm_gain
    ).astype(jnp.bfloat16)
    head_width = qkv_weight.shape[2]
    weight_rows = lax.all_gather(qkv_weight, "seq", axis=0, tiled=True)
    down_rows = lax.all_gather(adapter_down, "seq", axis=0, tiled=True)
    main_part = jnp.einsum("tr,rkc->ktc", normed, weight_rows, preferred_element_type=jnp.float32)
    low_rank = jnp.dot(normed, down_rows, preferred_element_type=jnp.float32)
    main_part, low_rank = (main_part, low_rank)
    low_rank = low_rank.astype(jnp.bfloat16)
    projected = (
        main_part
        + jnp.einsum("tr,krc->ktc", low_rank, adapter_up, preferred_element_type=jnp.float32)
    ).astype(jnp.bfloat16)
    queries = projected[0]
    new_keys = projected[1]
    new_values = projected[2]
    cycle_index = lax.axis_index("seq")
    cache_rows = cache_keys.shape[0] * cache_keys.shape[1]
    layout = (cache_rows, cache_keys.shape[1], tok_dev, block_perm.shape[0] // REQS)
    key_rows = jnp.concatenate([cache_keys.reshape(cache_rows, head_width), new_keys], axis=0)
    value_rows = jnp.concatenate([cache_values.reshape(cache_rows, head_width), new_values], axis=0)
    token_ids = jnp.arange(tok_dev, dtype=jnp.int32)
    own_info = query_meta(cycle_index * tok_dev + token_ids, cache_lengths)
    head_count = head_width // HD
    softmax_state = (
        jnp.zeros((head_count, tok_dev, HD), jnp.float32),
        jnp.full((head_count, tok_dev), lowest, jnp.float32),
        jnp.zeros((head_count, tok_dev), jnp.float32),
    )
    pieces = (
        lax.all_gather(key_rows, "seq", axis=0, tiled=True),
        lax.all_gather(value_rows, "seq", axis=0, tiled=True),
    )
    row_ids = jnp.arange(pieces[0].shape[0], dtype=jnp.int32)
    key_info = key_meta(row_ids, layout, block_perm, cache_lengths)
    softmax_state = attend(softmax_state, queries, own_info, pieces[0], pieces[1], key_info, HD)
    summed, largest, weight_sum = softmax_state
    attended = (
        (summed / weight_sum[..., None])
        .transpose(1, 0, 2)
        .reshape(tok_dev, head_width)
        .astype(jnp.bfloat16)
    )
    partial_value = jnp.dot(
        attended,
        lax.all_gather(out_weight, "seq", axis=1, tiled=True),
        preferred_element_type=jnp.float32,
    )
    return lax.psum_scatter(
        partial_value.astype(jnp.bfloat16), "mp", scatter_dimension=1, tiled=True
    )


def solution(mesh):
    in_specs = (
        P("seq", None),
        P(),
        P("seq", None, "mp"),
        P("seq", None),
        P(None, None, "mp"),
        P("mp", "seq"),
        P("seq", None, "mp"),
        P("seq", None, "mp"),
        P(),
        P(),
    )
    out_specs = P("seq", "mp")
    return jax.shard_map(
        per_device, mesh=mesh, in_specs=in_specs, out_specs=out_specs, check_vma=False
    )
```

profile of v0, /device:TPU:0, one launch (start us, length us, event | category | flops | bytes accessed | tf_op | source)
XLA Modules:
  0.0 1864.4 jit_solution(12091383622664191776)
XLA Ops:
  6.5 0.0 copy-start
  6.5 0.0 copy-start.3
  6.5 0.0 copy-start.6
  6.5 0.0 all-gather.6.cloned.1.call-start
  6.5 7.7 copy.19
  14.2 0.0 all-gather.6.cloned.1.call-update
  14.2 0.0 all-gather.8.cloned.1.call-start
  14.3 0.7 all-gather.8.cloned.1.call-update
  15.0 0.0 all-gather.10.cloned.1.call-start
  15.0 8.1 fusion.6
  23.1 0.0 copy-done.3
  23.1 0.7 copy.24
  23.9 724.3 %all-gather.6.cloned.1.call-done = bf16[7168,3,896]{0,2,1:T(8,128)(2,1)} async-done(((bf16[896,3,896]{0,2,1:T(8,128)(2,1)}), bf16[7168,3,896]{0,2,1:T(8,128)(2,1)}) %all-gather.6.cloned.1.call-update) | async-done | bytes 38535184 | tf_op jit(solution)/shard_map/all_gather | solution.py:87
  748.2 0.0 copy-done.6
  748.2 49.8 %fusion.9 = f32[1024,3,896]{0,2,1:T(8,128)} fusion(bf16[7168,3,896]{0,2,1:T(8,128)(2,1)} %all-gather.6.cloned.1.call-done, bf16[1024,7168]{1,0:T(8,128)(2,1)} %param.10, f32[7168]{0:T(1024)S(1)} %copy-done.6, f32[1024]{0:T(1024)S(1)} %add_rsqrt_fusion), kind=kOutput, calls=%fused_computation.13 | convolution fusion | flops 39489372160 | bytes 64258048 | tf_op jit(solution)/shard_map/tr,rkc->ktc/dot_general | solution.py:89
  798.0 0.0 all-gather.8.cloned.1.call-done
  798.0 0.0 copy-done
  798.0 15.5 fusion.11
  813.5 0.0 copy-start.5
  813.5 0.0 copy-start.4
  813.5 4.5 slice_bitcast_fusion.1
  818.0 1.7 pad_maximum_fusion
  819.8 0.0 all-gather.10.cloned.1.call-update
  819.8 0.0 all-gather.12.cloned.1.call-start
  819.9 1.5 copy.25
  821.3 1.7 pad_maximum_fusion.1
  823.1 0.0 copy-start.2
  823.1 0.0 all-gather.12.cloned.1.call-update
  823.1 0.0 all-gather.14.cloned.1.call-start
  823.1 0.5 all-gather.14.cloned.1.call-update
  823.7 0.3 reduce-scatter.4.cloned.1.call-start
  823.9 0.1 fusion.28
  824.0 0.0 copy-done.5
  824.0 0.2 select_reduce_fusion
  824.3 0.1 add_select_fusion.1
  824.4 0.0 copy-done.4
  824.4 0.1 select_reduce_fusion.3
  824.5 0.3 select_reduce_fusion.2
  824.8 0.1 select_select_fusion
  825.0 13.1 compare_and_fusion
  838.0 403.4 %all-gather.10.cloned.1.call-done = bf16[12288,896]{0,1:T(8,128)(2,1)} async-done(((bf16[1536,896]{0,1:T(8,128)(2,1)}), bf16[12288,896]{0,1:T(8,128)(2,1)}) %all-gather.10.cloned.1.call-update) | async-done | bytes 22020112 | tf_op jit(solution)/shard_map/all_gather | solution.py:114
  1241.4 0.0 copy-done.2
  1241.4 79.3 %fusion = (f32[4,1024]{1,0:T(4,128)S(1)}, f32[4,1024,12288]{2,1,0:T(8,128)}) fusion(pred[1024,12288]{1,0:T(8,128)(4,1)} %compare_and_fusion, bf16[1024,4,224]{0,2,1:T(8,128)(2,1)S(1)} %bitcast.36, bf16[12288,4,224]{0,2,1:T(8,128)(2,1)} %bitcast.40), kind=kOutput, calls=%fused_computation.2 | convolution fusion | flops 22699569152 | bytes 237780992 | tf_op jit(solution)/shard_map/qhd,khd->hqk/dot_general | solution.py:50
  1320.7 65.2 %fusion.1 = f32[4,1024]{1,0:T(4,128)S(1)} fusion(f32[4,1024,12288]{2,1,0:T(8,128)} %get-tuple-element.13, f32[4,1024]{1,0:T(4,128)S(1)} %broadcast_maximum_fusion, pred[1024,12288]{1,0:T(8,128)(4,1)} %compare_and_fusion), kind=kLoop, calls=%fused_computation.3 | loop fusion | flops 251654144 | bytes 213942272 | tf_op jit(solution)/shard_map/reduce_sum | solution.py:59
  1385.8 278.4 %all-gather.12.cloned.1.call-done = bf16[12288,896]{0,1:T(8,128)(2,1)} async-done(((bf16[1536,896]{0,1:T(8,128)(2,1)}), bf16[12288,896]{0,1:T(8,128)(2,1)}) %all-gather.12.cloned.1.call-update) | async-done | bytes 22020112 | tf_op jit(solution)/shard_map/all_gather | solution.py:115
  1664.2 83.7 %fusion.15 = bf16[1024,4,224]{0,2,1:T(8,128)(2,1)S(1)} fusion(bf16[12288,4,224]{0,2,1:T(8,128)(2,1)} %bitcast.41, f32[4,1024,12288]{2,1,0:T(8,128)} %get-tuple-element.13, f32[4,1024]{1,0:T(4,128)S(1)} %broadcast_maximum_fusion, pred[1024,12288]{1,0:T(8,128)(4,1)} %compare_and_fusion, f32[1024,4]{0,1:T(4,128)S(1)} %bitcast.39), kind=kOutput, calls=%fused_computation.20 | convolution fusion | flops 22802071552 | bytes 237797376 | tf_op jit(solution)/shard_map/hqk,khd->hqd/dot_general | solution.py:60
  1747.9 19.0 %all-gather.14.cloned.1.call-done = bf16[896,3584]{0,1:T(8,128)(2,1)} async-done(((bf16[896,448]{0,1:T(8,128)(2,1)}), bf16[896,3584]{0,1:T(8,128)(2,1)}) %all-gather.14.cloned.1.call-update) | async-done | bytes 6422544 | tf_op jit(solution)/shard_map/all_gather | solution.py:129
  1766.9 0.0 copy-start.1
  1766.9 12.8 convolution_convert_fusion
  1779.7 10.4 copy.26
  1790.1 0.0 reduce-scatter.4.cloned.1.call-update
  1790.1 63.7 %reduce-scatter.4.cloned.1.call-done = bf16[896,1024]{1,0:T(8,128)(2,1)} async-done(((bf16[3584,1024]{1,0:T(8,128)(2,1)}), bf16[896,1024]{1,0:T(8,128)(2,1)}) %reduce-scatter.4.cloned.1.call-update) | async-done | bytes 1835024
  1853.8 3.8 copy.27
  1857.6 0.0 copy-done.1
  (4 shorter events, 0.0 us)
Async XLA Ops:
  6.5 791.5 %copy-start = (bf16[3,128,896]{2,1,0:T(8,128)(2,1)S(1)}, bf16[3,128,896]{2,1,0:T(8,128)(2,1)}, u32[]{:S(2)}) copy-start(bf16[3,128,896]{2,1,0:T(8,128)(2,1)} %param.14) | copy-start | bytes 2064388
  6.5 16.6 copy-start.3
  6.5 741.7 %copy-start.6 = (f32[7168]{0:T(1024)S(1)}, f32[7168]{0:T(1024)}, u32[]{:S(2)}) copy-start(f32[7168]{0:T(1024)} %param.11) | copy-start | bytes 86020
  6.5 741.7 %all-gather.6.cloned.1.call-start = ((), (), s32[]{:S(2)}) async-start(), calls=%async_computation.1 | async-start | bytes 43352064 | tf_op jit(solution)/shard_map/all_gather | solution.py:87
  14.2 783.8 %all-gather.8.cloned.1.call-start = ((), (), s32[]{:S(2)}) async-start(), calls=%async_computation.2 | async-start | bytes 2064384 | tf_op jit(solution)/shard_map/all_gather | solution.py:88
  15.0 1226.4 %all-gather.10.cloned.1.call-start = ((), (), s32[]{:S(2)}) async-start(), calls=%async_computation.3 | async-start | bytes 24772608 | tf_op jit(solution)/shard_map/all_gather | solution.py:114
  813.5 10.5 copy-start.5
  813.5 10.8 copy-start.4
  819.8 844.4 %all-gather.12.cloned.1.call-start = ((), (), s32[]{:S(2)}) async-start(), calls=%async_computation.4 | async-start | bytes 24772608 | tf_op jit(solution)/shard_map/all_gather | solution.py:115
  823.1 418.3 %copy-start.2 = (bf16[1,1024,896]{1,2,0:T(8,128)(2,1)S(1)}, bf16[1,1024,896]{1,2,0:T(8,128)(2,1)}, u32[]{:S(2)}) copy-start(bf16[1,1024,896]{1,2,0:T(8,128)(2,1)} %get-tuple-element.9) | copy-start | bytes 5505028
  823.1 943.8 %all-gather.14.cloned.1.call-start = ((), (), s32[]{:S(2)}) async-start(), calls=%async_computation.5 | async-start | bytes 7225344 | tf_op jit(solution)/shard_map/all_gather | solution.py:129
  823.7 1030.1 %reduce-scatter.4.cloned.1.call-start = ((), (), s32[]{:S(2)}) async-start(), calls=%async_computation.6 | async-start | bytes 9175040
  1766.9 90.7 %copy-start.1 = (bf16[3,128,896]{2,1,0:T(8,128)(2,1)S(1)}, bf16[3,128,896]{2,1,0:T(8,128)(2,1)}, u32[]{:S(2)}) copy-start(bf16[3,128,896]{2,1,0:T(8,128)(2,1)} %param.14) | copy-start | bytes 2064388
Sparse Core Ops, SparseCore 0:
  14.3 733.8 all-gather.5
  750.4 46.2 all-gather.7
  819.9 421.4 all-gather.9
  1242.8 421.4 all-gather.11
  1666.3 100.5 all-gather.13
  1790.2 63.5 reduce-scatter.3
where the time goes:
time: 1870 us; the launch traced here: 1860 us
  waiting for transfers between devices  1490 us (80%)
  matrix products  241 us (13%)
  other arithmetic  90.8 us (5%)
  local copies, waits for them, and re-layouts  28.5 us (2%)
    all_gather x1, waiting for transfers between devices, per_device(): weight_rows = lax.all_gather(qkv_weight, 'seq', axis=0, tiled=True)  724 us
    all_gather x1, waiting for transfers between devices, per_device(): lax.all_gather(key_rows, 'seq', axis=0, tiled=True)  403 us
    all_gather x1, waiting for transfers between devices, per_device(): lax.all_gather(value_rows, 'seq', axis=0, tiled=True)  278 us
    dot_general x1, matrix products, attend(): jnp.einsum('hqk,khd->hqd', weights.astype(jnp.bfloat16), value_rows.resha...  83.7 us
    dot_general x1, matrix products, attend(): jnp.einsum('qhd,khd->hqk', queries.reshape(query_count, head_count, head_...  79.3 us
    reduce_sum x1, other arithmetic, attend(): weight_sum = jnp.sum(weights, axis=-1)  65.2 us
    unnamed x7, waiting for transfers between devices  65 us
    dot_general x1, matrix products, per_device(): jnp.einsum('tr,rkc->ktc', normed, weight_rows, preferred_element_type=jnp...  49.8 us
  transfers between devices with their start and end apart: 6, of which 5 were waited for; matrix products, arithmetic and copies ran while one was open for 16% of the time, Pallas kernels for 0%

commit v1 on v0

--- a/solution.py
+++ b/solution.py
@@ -1,6 +1,8 @@
 import jax
 import jax.numpy as jnp
 from jax import lax
+from jax.experimental import pallas as pl
+from jax.experimental.pallas import tpu as pltpu
 from jax.sharding import PartitionSpec as P
 
 HD = 224
@@ -134,6 +136,239 @@
     )
 
 
+CHUNK = 256
+RANK = 128
+LOG2E = 1.4426950408889634
+
+
+def swap(array, axis, size, bit):
+    return lax.ppermute(array, axis, [(i, i ^ bit) for i in range(size)])
+
+
+def pick(array, index, axis=0):
+    return lax.dynamic_index_in_dim(array, index, axis, keepdims=False)
+
+
+def attention_kernel(
+    chunk_table, cache_table, lengths, projected_ref, cache_ref, out_ref, total_ref
+):
+    request = pl.program_id(0)
+    tile = pl.program_id(1)
+    factor = HD ** (-0.5) * LOG2E
+
+    def chunk_of(number, part):
+        return projected_ref[chunk_table[request * 8 + number], pl.ds(part * HD, HD), :]
+
+    queries = jnp.concatenate([chunk_of(2 * tile, 0), chunk_of(2 * tile + 1, 0)], axis=1)
+    width = 2 * CHUNK
+    total_ref[...] = jnp.zeros_like(total_ref)
+
+    def step(state, keys, values, visible):
+        largest, weight_sum = state
+        scores = lax.dot_general(
+            keys, queries, (((0,), (0,)), ((), ())), preferred_element_type=jnp.float32
+        )
+        if visible is not None:
+            scores = jnp.where(visible, scores, lowest)
+        new_largest = jnp.maximum(largest, jnp.max(scores, axis=0, keepdims=True))
+        weights = jnp.exp2((scores - new_largest) * factor)
+        fade = jnp.exp2((largest - new_largest) * factor)
+        weight_sum = weight_sum * fade + jnp.sum(weights, axis=0, keepdims=True)
+        total_ref[...] = total_ref[...] * fade + jnp.dot(
+            values, weights.astype(jnp.bfloat16), preferred_element_type=jnp.float32
+        )
+        return (new_largest, weight_sum)
+
+    key_row = lax.broadcasted_iota(jnp.int32, (CHUNK, width), 0)
+    query_column = lax.broadcasted_iota(jnp.int32, (CHUNK, width), 1)
+
+    def new_step(number, state):
+        return step(state, chunk_of(number, 1), chunk_of(number, 2), None)
+
+    def own_step(number, state):
+        visible = key_row + number * CHUNK <= query_column + tile * width
+        return step(state, chunk_of(number, 1), chunk_of(number, 2), visible)
+
+    length = lengths[request]
+
+    def cache_step(number, state):
+        entry = cache_table[request * 4 + number]
+        start = pl.multiple_of((entry % 2) * CHUNK, CHUNK)
+        keys = cache_ref[entry // 2, pl.ds(0, HD), pl.ds(start, CHUNK)]
+        values = cache_ref[entry // 2, pl.ds(HD, HD), pl.ds(start, CHUNK)]
+        return step(state, keys, values, key_row + number * CHUNK < length)
+
+    state = (jnp.full((1, width), lowest, jnp.float32), jnp.zeros((1, width), jnp.float32))
+    state = own_step(2 * tile, state)
+    state = own_step(2 * tile + 1, state)
+    state = lax.fori_loop(0, 2 * tile, new_step, state)
+    state = lax.fori_loop(0, pl.cdiv(length, CHUNK), cache_step, state)
+    out_ref[...] = (total_ref[...] / state[1]).astype(jnp.bfloat16)[None]
+
+
+def attention(projected, cached, chunk_table, cache_table, lengths):
+    return pl.pallas_call(
+        attention_kernel,
+        grid_spec=pltpu.PrefetchScalarGridSpec(
+            num_scalar_prefetch=3,
+            grid=(2, QLEN // (2 * CHUNK)),
+            in_specs=[
+                pl.BlockSpec(projected.shape, lambda r, i, *_: (0, 0, 0)),
+                pl.BlockSpec(cached.shape, lambda r, i, *_: (0, 0, 0)),
+            ],
+            out_specs=pl.BlockSpec((1, HD, 2 * CHUNK), lambda r, i, *_: (r, 0, i)),
+            scratch_shapes=[pltpu.VMEM((HD, 2 * CHUNK), jnp.float32)],
+        ),
+        out_shape=jax.ShapeDtypeStruct((2, HD, QLEN), jnp.bfloat16),
+        compiler_params=pltpu.CompilerParams(vmem_limit_bytes=48 * 2**20),
+        cost_estimate=pl.CostEstimate(
+            flops=2 * 2 * 2 * QLEN * QLEN * 256,
+            bytes_accessed=2 * projected.size,
+            transcendentals=2 * QLEN * QLEN,
+        ),
+    )(chunk_table, cache_table, lengths, projected, cached)
+
+
+def per_device_paired(
+    inputs,
+    norm_gain,
+    qkv_weight,
+    adapter_down,
+    adapter_up,
+    out_weight,
+    cache_keys,
+    cache_values,
+    cache_lengths,
+    block_perm,
+):
+    tok_dev, width = inputs.shape
+    rows = qkv_weight.shape[0]
+    seq = lax.axis_index("seq")
+    mp = lax.axis_index("mp")
+    plane, side = seq // 2, seq % 2
+    role = plane % 2
+
+    def over_z(array, bit):
+        return swap(array, "seq", 8, 2 * bit)
+
+    def over_x(array):
+        return swap(array, "seq", 8, 1)
+
+    def over_y(array):
+        return swap(array, "mp", 4, 2)
+
+    def over_core(array):
+        return swap(array, "mp", 4, 1)
+
+    widened = inputs.astype(jnp.float32)
+    normed = (
+        widened * lax.rsqrt(jnp.mean(widened * widened, axis=-1, keepdims=True) + 1e-05) * norm_gain
+    ).astype(jnp.bfloat16)
+
+    turned = qkv_weight.reshape(rows, 3, 4, HD).transpose(2, 1, 3, 0).reshape(2, 2, 3 * HD, rows)
+    kept = pick(turned, side, 1)
+    from_x = over_x(pick(turned, 1 - side, 1))
+    weight_blocks = [[pick(kept, role), pick(from_x, role)]]
+    for bit in (1, 2, 3):
+        other = role ^ (bit & 1)
+        weight_blocks.append(
+            [over_z(pick(kept, other), bit), over_z(pick(from_x, other), bit)]
+        )
+    weight_rows = jnp.zeros((3 * HD, width), jnp.bfloat16)
+    for bit in range(4):
+        for other_side in range(2):
+            source = (seq ^ (2 * bit)) ^ other_side
+            weight_rows = lax.dynamic_update_slice(
+                weight_rows, weight_blocks[bit][other_side], (0, source * rows)
+            )
+
+    def turned_cache(cache):
+        blocks, size, _ = cache.shape
+        return cache.reshape(blocks * size, 4, HD).transpose(1, 2, 0)
+
+    cached = jnp.concatenate([turned_cache(cache_keys), turned_cache(cache_values)], axis=1)
+    cached = cached.reshape(2, 2, 2 * HD, cached.shape[2])
+    kept_cache = pick(cached, side, 1)
+    cache_from_x = over_x(pick(cached, 1 - side, 1))
+    cache_blocks = [pick(kept_cache, role), pick(cache_from_x, role)]
+    for bit in (1, 2, 3):
+        other = role ^ (bit & 1)
+        cache_blocks += [
+            over_z(pick(kept_cache, other), bit),
+            over_z(pick(cache_from_x, other), bit),
+        ]
+    cached_rows = jnp.stack(cache_blocks)
+
+    part = lax.dynamic_slice_in_dim(normed, mp * CHUNK, CHUNK, 0)
+    part_x = over_x(part)
+    part_z = over_z(part, 1)
+    part_zx = over_x(part_z)
+
+    def completed(piece):
+        across = over_y(piece)
+        return jnp.concatenate([piece, over_core(piece), across, over_core(across)], axis=0)
+
+    token_sets = [normed, completed(part_x), completed(part_z), completed(part_zx)]
+
+    down_share = lax.dynamic_slice_in_dim(adapter_down, mp * (rows // 4), rows // 4, 0)
+    down_rows = lax.all_gather(down_share, ("seq", "mp"), axis=0, tiled=True)
+    up = adapter_up.reshape(3, RANK, 4, HD).transpose(2, 0, 3, 1).reshape(4, 3 * HD, RANK)
+    up = pick(up, 2 * role + side)
+
+    def project(tokens):
+        low_rank = jnp.dot(tokens, down_rows, preferred_element_type=jnp.float32)
+        low_rank = low_rank.astype(jnp.bfloat16)
+        nt = (((1,), (1,)), ((), ()))
+        main_part = lax.dot_general(weight_rows, tokens, nt, preferred_element_type=jnp.float32)
+        extra = lax.dot_general(up, low_rank, nt, preferred_element_type=jnp.float32)
+        result = (main_part + extra).astype(jnp.bfloat16)
+        return result.reshape(3 * HD, 4, CHUNK).transpose(1, 0, 2)
+
+    projected = jnp.concatenate([project(tokens) for tokens in token_sets], axis=0)
+
+    place = jnp.arange(8, dtype=jnp.int32)
+    other_side = (place // 4) ^ side
+    chunk_table = jnp.concatenate(
+        [
+            other_side * 4 + jnp.where(other_side == 1, (place % 4) ^ mp, place % 4),
+            8 + other_side * 4 + ((place % 4) ^ mp),
+        ]
+    ).astype(jnp.int32)
+    requests = jnp.stack([plane, plane ^ 1])
+    lengths = lookup(cache_lengths, requests)
+    logical = requests[:, None] * 4 + jnp.arange(4, dtype=jnp.int32)[None, :]
+    hits = logical[..., None] == block_perm
+    physical = jnp.sum(
+        jnp.where(hits, jnp.arange(block_perm.shape[0], dtype=jnp.int32), 0), axis=-1
+    ).reshape(8)
+    source = (physical // 2) ^ seq
+    cache_table = (source * 2 + physical % 2).astype(jnp.int32)
+
+    attended = attention(projected, cached_rows, chunk_table, cache_table, lengths)
+
+    received = over_z(attended[1], 1)
+    pair = jnp.where(
+        role == 0, jnp.stack([attended[0], received]), jnp.stack([received, attended[0]])
+    ).reshape(2, HD, 2, tok_dev)
+    mine = pick(pair, side, 2)
+    theirs = over_x(pick(pair, 1 - side, 2))
+    heads = jnp.where(
+        side == 0, jnp.stack([mine, theirs], axis=1), jnp.stack([theirs, mine], axis=1)
+    ).reshape(4 * HD, tok_dev)
+
+    out_rows = lax.all_gather(out_weight, "seq", axis=1, tiled=True)
+    partial_value = lax.dot_general(
+        heads, out_rows, (((0,), (0,)), ((), ())), preferred_element_type=jnp.float32
+    ).astype(jnp.bfloat16)
+    partial_value = partial_value.reshape(tok_dev, 2, 2, -1)
+    core, row = mp % 2, mp // 2
+    both = pick(partial_value, core, 2).astype(jnp.float32) + over_core(
+        pick(partial_value, 1 - core, 2)
+    ).astype(jnp.float32)
+    sent = over_y(pick(both, 1 - row, 1).astype(jnp.bfloat16))
+    return (pick(both, row, 1) + sent.astype(jnp.float32)).astype(jnp.bfloat16)
+
+
 def solution(mesh):
     in_specs = (
         P("seq", None),
@@ -148,6 +383,7 @@
         P(),
     )
     out_specs = P("seq", "mp")
+    paired = mesh.shape["seq"] == 8 and mesh.shape["mp"] == 4
     return jax.shard_map(
-        per_device, mesh=mesh, in_specs=in_specs, out_specs=out_specs, check_vma=False
-    )
+        per_device_paired if paired else per_device, mesh=mesh, in_specs=in_specs, out_specs=out_specs, check_vma=False
+    )

time: 1870 us -> 987 us (0.53)
  waiting for transfers between devices: 1490 us -> 563 us
  local copies, waits for them, and re-layouts: 28.5 us -> 153 us
  matrix products: 241 us -> 130 us
  other arithmetic: 90.8 us -> 37.5 us
  starting transfers between devices: 0.42 us -> 41.9 us
  Pallas kernels: 0 us -> 38.1 us
    all_gather x5 -> x2, waiting for transfers between devices: 1430 us -> 0.02 us  [the longest x1 0.02 us: per_device_paired(): out_rows = lax.all_gather(out_weight, 'seq', axis=1, tiled=True)]
    ppermute x0 -> x30, waiting for transfers between devices: none -> 563 us  [swap(): return lax.ppermute(array, axis, [(i, i ^ bit) for i in range(size)])]
    dot_general x5 -> x9, matrix products: 241 us -> 130 us  [the longest x4 70.2 us: project(): lax.dot_general(weight_rows, tokens, nt, preferred_element_type=jnp.float32)]
    unnamed x7 -> x2, waiting for transfers between devices: 65 us -> 0.03 us
    reduce_sum x2, other arithmetic: 73.2 us -> 8.32 us  [the longest x1 8.11 us: per_device_paired(): jnp.mean(widened * widened, axis=-1, keepdims=True) + 1e-05]
    ppermute x0 -> x30, starting transfers between devices: none -> 41.9 us  [swap(): return lax.ppermute(array, axis, [(i, i ^ bit) for i in range(size)])]
    pallas_call x0 -> x1, Pallas kernels: none -> 38.1 us  [attention(): pl.pallas_call(attention_kernel, grid_spec=pltpu.PrefetchScalarGridSpec(n...]
    unnamed x17 -> x49, local copies, waits for them, and re-layouts: 21.9 us -> 51 us
  transfers between devices with their start and end apart: 6 -> 32, of which waited for: 5 -> 13; matrix products, arithmetic and copies ran while one was open for 16% -> 26% of each run, Pallas kernels for 0% -> 4%
where the time goes in v1:
time: 987 us; the launch traced here: 978 us
  waiting for transfers between devices  563 us (57%)
  local copies, waits for them, and re-layouts  153 us (16%)
  matrix products  130 us (13%)
  starting transfers between devices  41.9 us (4%)
  Pallas kernels  38.1 us (4%)
  other arithmetic  37.5 us (4%)
  between operations  14.3 us (1%)
    ppermute x30, waiting for transfers between devices, swap(): return lax.ppermute(array, axis, [(i, i ^ bit) for i in range(size)])  563 us
    dot_general x4, matrix products, project(): lax.dot_general(weight_rows, tokens, nt, preferred_element_type=jnp.float32)  70.2 us
    unnamed x49, local copies, waits for them, and re-layouts  51 us
    dot_general x4, matrix products, project(): lax.dot_general(up, low_rank, nt, preferred_element_type=jnp.float32)  47.3 us
    ppermute x30, starting transfers between devices, swap(): return lax.ppermute(array, axis, [(i, i ^ bit) for i in range(size)])  41.9 us
    pallas_call x1, Pallas kernels, attention(): pl.pallas_call(attention_kernel, grid_spec=pltpu.PrefetchScalarGridSpec(n...  38.1 us
    dynamic_slice x2, local copies, waits for them, and re-layouts, pick(): return lax.dynamic_index_in_dim(array, index, axis, keepdims=False)  20.2 us
  transfers between devices with their start and end apart: 32, of which 13 were waited for; matrix products, arithmetic and copies ran while one was open for 26% of the time, Pallas kernels for 4%

profile of v1, /device:TPU:0, one launch (start us, length us, event | category | flops | bytes accessed | tf_op | source)
XLA Modules:
  0.0 977.6 jit_solution(15060732672244556035)
XLA Ops:
  8.2 3.0 reshape.126
  12.0 3.0 reshape.127
  18.8 3.0 collective-permute-start.20
  21.8 2.5 collective-permute-start.24
  24.3 7.6 copy.31
  31.9 4.9 copy.32
  36.7 3.3 dynamic-slice_bitcast_fusion
  43.2 8.1 fusion
  51.5 14.8 %fusion.2 = bf16[1024,7168]{1,0:T(8,128)(2,1)} fusion(bf16[1024,7168]{1,0:T(8,128)(2,1)} %param.10, f32[7168]{0:T(1024)S(1)} %copy-done.13, f32[1024]{0:T(1024)S(1)} %add_rsqrt_fusion), kind=kLoop, calls=%fused_computation.4 | loop fusion | flops 29360128 | bytes 29392896 | tf_op jit(solution)/shard_map/convert_element_type | solution.py:266
  68.8 4.8 broadcast_in_dim.31
  73.6 2.5 constant_dynamic-update-slice_fusion.19
  76.1 4.1 constant_dynamic-slice_fusion.2
  80.3 45.1 %collective-permute-done.19 = bf16[2,448,512]{2,1,0:T(8,128)(2,1)} collective-permute-done((bf16[2,448,512]{2,1,0:T(8,128)(2,1)}, bf16[2,448,512]{2,1,0:T(8,128)(2,1)}, u32[]{:S(2)}, u32[]{:S(2)}) %collective-permute-start.19) | collective-permute-done | bytes 917536 | tf_op jit(solution)/shard_map/ppermute | solution.py:145
  128.1 2.3 collective-permute-start.23
  131.4 38.3 %collective-permute-done.21 = bf16[448,512]{1,0:T(8,128)(2,1)S(1)} collective-permute-done((bf16[448,512]{1,0:T(8,128)(2,1)S(1)}, bf16[448,512]{1,0:T(8,128)(2,1)S(1)}, u32[]{:S(2)}, u32[]{:S(2)}) %collective-permute-start.21) | collective-permute-done | bytes 458784 | tf_op jit(solution)/shard_map/ppermute | solution.py:145
  169.8 3.0 collective-permute-start.3
  172.8 2.4 dynamic-slice_bitcast_fusion.1
  179.9 86.9 %collective-permute-done.25 = bf16[448,512]{1,0:T(8,128)(2,1)S(1)} collective-permute-done((bf16[448,512]{1,0:T(8,128)(2,1)S(1)}, bf16[448,512]{1,0:T(8,128)(2,1)S(1)}, u32[]{:S(2)}, u32[]{:S(2)}) %collective-permute-start.25) | collective-permute-done | bytes 458784 | tf_op jit(solution)/shard_map/ppermute | solution.py:145
  266.8 6.8 collective-permute-start.11
  276.6 3.0 constant_dynamic-update-slice_fusion.18
  279.6 2.8 collective-permute-start.5
  285.6 4.1 collective-permute-done.2
  289.7 3.6 collective-permute-start.4
  293.3 12.2 %fusion.8 = f32[672,1024]{1,0:T(8,128)} fusion(bf16[1024,7168]{1,0:T(8,128)(2,1)} %fusion.2, bf16[7168,128]{1,0:T(8,128)(2,1)} %all-gather.3.cloned.1.call-done, bf16[4,672,128]{2,1,0:T(8,128)(2,1)S(1)} %bitcast.134, s32[]{:T(128)S(6)} %select_n.194), kind=kOutput, calls=%fused_computation.37 | convolution fusion | flops 2055340032 | bytes 19439620 | tf_op jit(solution)/shard_map/dot_general | solution.py:323
  305.5 2.4 constant_dynamic-update-slice_fusion.16
  309.1 132.8 %collective-permute-done.4 = bf16[672,896]{1,0:T(8,128)(2,1)} collective-permute-done((bf16[672,896]{1,0:T(8,128)(2,1)}, bf16[672,896]{1,0:T(8,128)(2,1)}, u32[]{:S(2)}, u32[]{:S(2)}) %collective-permute-start.4) | collective-permute-done | bytes 1204256 | tf_op jit(solution)/shard_map/ppermute | solution.py:145
  441.8 2.6 constant_dynamic-update-slice_fusion.14
  444.4 2.5 constant_dynamic-update-slice_fusion.13
  446.9 2.5 constant_dynamic-update-slice_fusion.12
  451.6 18.0 %add_convert_fusion.3 = bf16[672,1024]{1,0:T(8,128)(2,1)} fusion(f32[672,1024]{1,0:T(8,128)} %fusion.8, bf16[672,7168]{1,0:T(8,128)(2,1)} %constant_dynamic-update-slice_fusion.12, bf16[1024,7168]{1,0:T(8,128)(2,1)} %fusion.2), kind=kOutput, calls=%fused_computation.16 | convolution fusion | flops 9866379264 | bytes 28442624 | tf_op jit(solution)/shard_map/dot_general | solution.py:322
  469.7 4.1 constant_dynamic-update-slice_fusion.3
  473.7 4.1 constant_dynamic-update-slice_fusion.7
  477.8 54.0 %collective-permute-done.9 = bf16[256,7168]{1,0:T(8,128)(2,1)S(1)} collective-permute-done((bf16[256,7168]{1,0:T(8,128)(2,1)}, bf16[256,7168]{1,0:T(8,128)(2,1)S(1)}, u32[]{:S(2)}, u32[]{:S(2)}) %collective-permute-start.9) | collective-permute-done | bytes 3670048 | tf_op jit(solution)/shard_map/ppermute | solution.py:145
  533.0 4.1 constant_dynamic-update-slice_fusion.11
  538.5 72.1 %collective-permute-done.13 = bf16[256,7168]{1,0:T(8,128)(2,1)} collective-permute-done((bf16[256,7168]{1,0:T(8,128)(2,1)}, bf16[256,7168]{1,0:T(8,128)(2,1)}, u32[]{:S(2)}, u32[]{:S(2)}) %collective-permute-start.13) | collective-permute-done | bytes 3670048 | tf_op jit(solution)/shard_map/ppermute | solution.py:145
  614.7 2.1 constant_dynamic-update-slice_fusion.6
  616.8 4.1 constant_dynamic-update-slice_fusion.5
  623.2 11.7 %fusion.7 = f32[672,1024]{1,0:T(8,128)} fusion(bf16[1024,7168]{1,0:T(8,128)(2,1)} %constant_dynamic-update-slice_fusion, bf16[7168,128]{1,0:T(8,128)(2,1)S(1)} %copy-done.4, bf16[4,672,128]{2,1,0:T(8,128)(2,1)S(1)} %bitcast.135, s32[]{:T(128)S(6)} %select_n.194), kind=kOutput, calls=%fused_computation.35 | convolution fusion | flops 2055340032 | bytes 19439620 | tf_op jit(solution)/shard_map/dot_general | solution.py:323
  634.9 4.2 constant_dynamic-update-slice_fusion.4
  639.1 11.6 %fusion.6 = f32[672,1024]{1,0:T(8,128)} fusion(bf16[1024,7168]{1,0:T(8,128)(2,1)} %constant_dynamic-update-slice_fusion.4, bf16[7168,128]{1,0:T(8,128)(2,1)S(1)} %copy-done.4, bf16[4,672,128]{2,1,0:T(8,128)(2,1)S(1)} %bitcast.136, s32[]{:T(128)S(6)} %select_n.194), kind=kOutput, calls=%fused_computation.33 | convolution fusion | flops 2055340032 | bytes 19439620 | tf_op jit(solution)/shard_map/dot_general | solution.py:323
  650.7 38.1 %collective-permute-done.17 = bf16[256,7168]{1,0:T(8,128)(2,1)} collective-permute-done((bf16[256,7168]{1,0:T(8,128)(2,1)}, bf16[256,7168]{1,0:T(8,128)(2,1)}, u32[]{:S(2)}, u32[]{:S(2)}) %collective-permute-start.17) | collective-permute-done | bytes 3670048 | tf_op jit(solution)/shard_map/ppermute | solution.py:145
  688.8 17.8 %add_convert_fusion.2 = bf16[672,1024]{1,0:T(8,128)(2,1)} fusion(f32[672,1024]{1,0:T(8,128)} %fusion.7, bf16[672,7168]{1,0:T(8,128)(2,1)} %constant_dynamic-update-slice_fusion.12, bf16[1024,7168]{1,0:T(8,128)(2,1)} %constant_dynamic-update-slice_fusion), kind=kOutput, calls=%fused_computation.15 | convolution fusion | flops 9866379264 | bytes 28442624 | tf_op jit(solution)/shard_map/dot_general | solution.py:322
  706.6 4.1 constant_dynamic-update-slice_fusion.10
  710.7 4.2 constant_dynamic-update-slice_fusion.9
  714.9 17.7 %add_convert_fusion.1 = bf16[672,1024]{1,0:T(8,128)(2,1)} fusion(f32[672,1024]{1,0:T(8,128)} %fusion.6, bf16[672,7168]{1,0:T(8,128)(2,1)} %constant_dynamic-update-slice_fusion.12, bf16[1024,7168]{1,0:T(8,128)(2,1)} %constant_dynamic-update-slice_fusion.4), kind=kOutput, calls=%fused_computation.14 | convolution fusion | flops 9866379264 | bytes 28442624 | tf_op jit(solution)/shard_map/dot_general | solution.py:322
  732.6 2.6 bitcast_bitcast_fusion.2
  735.2 2.1 constant_dynamic-update-slice_fusion.8
  737.4 11.7 %fusion.5 = f32[672,1024]{1,0:T(8,128)} fusion(bf16[1024,7168]{1,0:T(8,128)(2,1)} %constant_dynamic-update-slice_fusion.8, bf16[7168,128]{1,0:T(8,128)(2,1)S(1)} %copy-done.4, bf16[4,672,128]{2,1,0:T(8,128)(2,1)} %bitcast.137, s32[]{:T(128)S(6)} %select_n.194), kind=kOutput, calls=%fused_computation.31 | convolution fusion | flops 2055340032 | bytes 19439620 | tf_op jit(solution)/shard_map/dot_general | solution.py:323
  749.1 16.7 %add_convert_fusion = bf16[672,1024]{1,0:T(8,128)(2,1)S(1)} fusion(f32[672,1024]{1,0:T(8,128)} %fusion.5, bf16[672,7168]{1,0:T(8,128)(2,1)} %constant_dynamic-update-slice_fusion.12, bf16[1024,7168]{1,0:T(8,128)(2,1)} %constant_dynamic-update-slice_fusion.8), kind=kOutput, calls=%fused_computation.13 | convolution fusion | flops 9866379264 | bytes 28442624 | tf_op jit(solution)/shard_map/dot_general | solution.py:322
  767.1 3.0 pad_maximum_fusion.projected_ref
  771.2 38.1 %shard_map.100 = bf16[2,224,2048]{2,1,0:T(8,128)(2,1)S(1)} custom-call(s32[16]{0:T(128)S(1)} %pad_add_fusion.chunk_table, s32[8]{0:T(128)S(1)} %fusion.22.cache_table, s32[2]{0:T(128)S(1)} %fusion.21.lengths, bf16[16,672,256]{2,1,0:T(8,128)(2,1)} %pad_maximum_fusion.projected_ref, bf16[8,448,512]{2,1,0:T(8,128)(2,1)S(1)} %copy-done.3), custom_call_target="tpu_custom_call" | custom-call | flops 8589934592 | bytes 5505024 | tf_op jit(solution)/shard_map/pallas_call | solution.py:210
  809.4 3.9 collective-permute-start.26
  813.4 21.1 %collective-permute-done.26 = bf16[224,2048]{1,0:T(8,128)(2,1)} collective-permute-done((bf16[224,2048]{1,0:T(8,128)(2,1)S(1)}, bf16[224,2048]{1,0:T(8,128)(2,1)}, u32[]{:S(2)}, u32[]{:S(2)}) %collective-permute-start.26) | collective-permute-done | bytes 917536 | tf_op jit(solution)/shard_map/ppermute | solution.py:145
  834.4 3.0 stack.69
  838.9 21.6 %collective-permute-done.27 = bf16[2,224,1024]{2,1,0:T(8,128)(2,1)S(1)} collective-permute-done((bf16[2,224,1024]{2,1,0:T(8,128)(2,1)S(1)}, bf16[2,224,1024]{2,1,0:T(8,128)(2,1)S(1)}, u32[]{:S(2)}, u32[]{:S(2)}) %collective-permute-start.27) | collective-permute-done | bytes 917536 | tf_op jit(solution)/shard_map/ppermute | solution.py:145
  861.0 12.7 %convolution_convert_fusion = bf16[1024,3584]{1,0:T(8,128)(2,1)} fusion(bf16[896,1024]{1,0:T(8,128)(2,1)S(1)} %bitcast.138, bf16[896,3584]{0,1:T(8,128)(2,1)} %all-gather.5.cloned.1.call-done), kind=kOutput, calls=%fused_computation.5 | convolution fusion | flops 6580338688 | bytes 15597568 | tf_op jit(solution)/shard_map/dot_general | solution.py:360
  873.7 15.4 %reshape.124 = bf16[1024,2,2,896]{3,2,1,0:T(2,128)(2,1)} reshape(bf16[1024,3584]{1,0:T(8,128)(2,1)} %convolution_convert_fusion) | data formatting | bytes 14680064 | tf_op jit(solution)/shard_map/reshape | solution.py:363
  889.0 17.7 %constant_dynamic-slice_fusion.1 = (bf16[1024,2,1,896]{3,2,1,0:T(2,128)(2,1)}, bf16[1024,2,1,896]{3,2,1,0:T(2,128)(2,1)S(1)}) fusion(bf16[1024,2,2,896]{3,2,1,0:T(2,128)(2,1)} %reshape.124, s32[]{:T(128)S(6)} %select_n.201, s32[]{:T(128)S(6)} %select_n.202), kind=kLoop, calls=%fused_computation.79 | loop fusion | bytes 14680072 | tf_op jit(solution)/shard_map/jit(dynamic_index_in_dim)/dynamic_slice | solution.py:149
  906.8 2.5 copy.65
  909.3 6.7 collective-permute-done.28
  916.0 4.9 convert_add_fusion
  920.9 2.9 copy-done.5
  925.6 40.6 %collective-permute-done.29 = bf16[1024,896]{1,0:T(8,128)(2,1)} collective-permute-done((bf16[1024,896]{1,0:T(8,128)(2,1)S(1)}, bf16[1024,896]{1,0:T(8,128)(2,1)}, u32[]{:S(2)}, u32[]{:S(2)}) %collective-permute-start.29) | collective-permute-done | bytes 1835040 | tf_op jit(solution)/shard_map/ppermute | solution.py:145
  966.2 4.2 fusion.3
  (117 shorter events, 44.9 us)
Async XLA Ops:
  6.5 0.9 copy-start
  6.5 286.7 %all-gather.3.cloned.1.call-start = ((), (), s32[]{:S(2)}) async-start(), calls=%async_computation | async-start | bytes 1892352 | tf_op jit(solution)/shard_map/all_gather | solution.py:314
  8.1 852.8 %all-gather.5.cloned.1.call-start = ((), (), s32[]{:S(2)}) async-start(), calls=%async_computation.1 | async-start | bytes 7225344 | tf_op jit(solution)/shard_map/all_gather | solution.py:359
  18.8 109.3 %collective-permute-start.20 = (bf16[448,512]{1,0:T(8,128)(2,1)}, bf16[448,512]{1,0:T(8,128)(2,1)}, u32[]{:S(2)}, u32[]{:S(2)}) collective-permute-start(bf16[448,512]{1,0:T(8,128)(2,1)} %get-tuple-element.18), channel_id=1, source_target_pairs={{0,8},{4,12},{8,0},{12,4},{16,24},{20,28},{24,16},{28,20},{1,9},{5... | collective-permute-start | bytes 1376264 | tf_op jit(solution)/shard_map/ppermute | solution.py:145
  21.8 156.0 %collective-permute-start.24 = (bf16[448,512]{1,0:T(8,128)(2,1)}, bf16[448,512]{1,0:T(8,128)(2,1)}, u32[]{:S(2)}, u32[]{:S(2)}) collective-permute-start(bf16[448,512]{1,0:T(8,128)(2,1)} %get-tuple-element.18), channel_id=1, source_target_pairs={{0,24},{4,28},{8,16},{12,20},{16,8},{20,12},{24,0},{28,4},{1,25},{... | collective-permute-start | bytes 1376264 | tf_op jit(solution)/shard_map/ppermute | solution.py:145
  40.0 129.8 %collective-permute-start = (bf16[2,672,896]{2,1,0:T(8,128)(2,1)}, bf16[2,672,896]{2,1,0:T(8,128)(2,1)}, u32[]{:S(2)}, u32[]{:S(2)}) collective-permute-start(bf16[2,672,896]{2,1,0:T(8,128)(2,1)} %dynamic-slice_bitcast_fusion), channel_id=1, source_target_pairs={{0,4},{4,0},{8,12},{12,8},{16,20},{20,16},{24,28},{28,24},{1,5},{5... | collective-permute-start | bytes 7225352 | tf_op jit(solution)/shard_map/ppermute | solution.py:145
  42.5 82.9 %collective-permute-start.19 = (bf16[2,448,512]{2,1,0:T(8,128)(2,1)}, bf16[2,448,512]{2,1,0:T(8,128)(2,1)}, u32[]{:S(2)}, u32[]{:S(2)}) collective-permute-start(bf16[2,448,512]{2,1,0:T(8,128)(2,1)} %dynamic-slice_bitcast_fusion.7), channel_id=1, source_target_pairs={{0,4},{4,0},{8,12},{12,8},{16,20},{20,16},{24,28},{28,24},{1,5},{5... | collective-permute-start | bytes 2752520 | tf_op jit(solution)/shard_map/ppermute | solution.py:145
  43.1 132.2 %collective-permute-start.22 = (bf16[448,512]{1,0:T(8,128)(2,1)}, bf16[448,512]{1,0:T(8,128)(2,1)}, u32[]{:S(2)}, u32[]{:S(2)}) collective-permute-start(bf16[448,512]{1,0:T(8,128)(2,1)} %get-tuple-element.17), channel_id=1, source_target_pairs={{0,16},{4,20},{8,24},{12,28},{16,0},{20,4},{24,8},{28,12},{1,17},{... | collective-permute-start | bytes 1376264 | tf_op jit(solution)/shard_map/ppermute | solution.py:145
  43.2 8.3 copy-start.13
  51.5 14.9 %copy-start.14 = (s32[16]{0:T(128)S(1)}, s32[16]{0:T(128)}, u32[]{:S(2)}) copy-start(s32[16]{0:T(128)} %param.19) | copy-start | bytes 196
  51.5 15.1 %copy-start.12 = (bf16[3,128,896]{2,1,0:T(8,128)(2,1)S(1)}, bf16[3,128,896]{2,1,0:T(8,128)(2,1)}, u32[]{:S(2)}) copy-start(bf16[3,128,896]{2,1,0:T(8,128)(2,1)} %param.14) | copy-start | bytes 2064388
  51.5 15.7 %copy-start.15 = (s32[4]{0:T(128)S(1)}, s32[4]{0:T(128)}, u32[]{:S(2)}) copy-start(s32[4]{0:T(128)} %param.18) | copy-start | bytes 52
  67.0 572.0 %copy-start.7 = (bf16[4,3,224,128]{3,2,1,0:T(8,128)(2,1)}, bf16[4,3,224,128]{3,2,1,0:T(8,128)(2,1)S(1)}, u32[]{:S(2)}) copy-start(bf16[4,3,224,128]{3,2,1,0:T(8,128)(2,1)S(1)} %copy.34) | copy-start | bytes 2064388
  126.7 43.0 %collective-permute-start.21 = (bf16[448,512]{1,0:T(8,128)(2,1)S(1)}, bf16[448,512]{1,0:T(8,128)(2,1)S(1)}, u32[]{:S(2)}, u32[]{:S(2)}) collective-permute-start(bf16[448,512]{1,0:T(8,128)(2,1)S(1)} %get-tuple-element.21), channel_id=1, source_target_pairs={{0,8},{4,12},{8,0},{12,4},{16,24},{20,28},{24,16},{28,20},{1,9},{5... | collective-permute-start | bytes 1376264 | tf_op jit(solution)/shard_map/ppermute | solution.py:145
  128.1 48.6 %collective-permute-start.23 = (bf16[448,512]{1,0:T(8,128)(2,1)S(1)}, bf16[448,512]{1,0:T(8,128)(2,1)S(1)}, u32[]{:S(2)}, u32[]{:S(2)}) collective-permute-start(bf16[448,512]{1,0:T(8,128)(2,1)S(1)} %get-tuple-element.19), channel_id=1, source_target_pairs={{0,16},{4,20},{8,24},{12,28},{16,0},{20,4},{24,8},{28,12},{1,17},{... | collective-permute-start | bytes 1376264 | tf_op jit(solution)/shard_map/ppermute | solution.py:145
  169.8 109.8 %collective-permute-start.1 = (bf16[672,896]{1,0:T(8,128)(2,1)S(1)}, bf16[672,896]{1,0:T(8,128)(2,1)S(1)}, u32[]{:S(2)}, u32[]{:S(2)}) collective-permute-start(bf16[672,896]{1,0:T(8,128)(2,1)S(1)} %dynamic-slice_bitcast_fusion.2), channel_id=1, source_target_pairs={{0,8},{4,12},{8,0},{12,4},{16,24},{20,28},{24,16},{28,20},{1,9},{5... | collective-permute-start | bytes 3612680 | tf_op jit(solution)/shard_map/ppermute | solution.py:145
  169.8 113.7 %collective-permute-start.3 = (bf16[672,896]{1,0:T(8,128)(2,1)S(1)}, bf16[672,896]{1,0:T(8,128)(2,1)S(1)}, u32[]{:S(2)}, u32[]{:S(2)}) collective-permute-start(bf16[672,896]{1,0:T(8,128)(2,1)S(1)} %get-tuple-element.8), channel_id=1, source_target_pairs={{0,16},{4,20},{8,24},{12,28},{16,0},{20,4},{24,8},{28,12},{1,17},{... | collective-permute-start | bytes 3612680 | tf_op jit(solution)/shard_map/ppermute | solution.py:145
  175.3 91.5 %collective-permute-start.25 = (bf16[448,512]{1,0:T(8,128)(2,1)S(1)}, bf16[448,512]{1,0:T(8,128)(2,1)S(1)}, u32[]{:S(2)}, u32[]{:S(2)}) collective-permute-start(bf16[448,512]{1,0:T(8,128)(2,1)S(1)} %get-tuple-element.21), channel_id=1, source_target_pairs={{0,24},{4,28},{8,16},{12,20},{16,8},{20,12},{24,0},{28,4},{1,25},{... | collective-permute-start | bytes 1376264 | tf_op jit(solution)/shard_map/ppermute | solution.py:145
  176.7 113.0 %collective-permute-start.2 = (bf16[672,896]{1,0:T(8,128)(2,1)}, bf16[672,896]{1,0:T(8,128)(2,1)}, u32[]{:S(2)}, u32[]{:S(2)}) collective-permute-start(bf16[672,896]{1,0:T(8,128)(2,1)} %dynamic-slice_bitcast_fusion.1), channel_id=1, source_target_pairs={{0,8},{4,12},{8,0},{12,4},{16,24},{20,28},{24,16},{28,20},{1,9},{5... | collective-permute-start | bytes 3612680 | tf_op jit(solution)/shard_map/ppermute | solution.py:145
  177.8 271.6 %collective-permute-start.7 = (bf16[256,7168]{1,0:T(8,128)(2,1)}, bf16[256,7168]{1,0:T(8,128)(2,1)}, u32[]{:S(2)}, u32[]{:S(2)}) collective-permute-start(bf16[256,7168]{1,0:T(8,128)(2,1)} %constant_dynamic-slice_fusion.2), channel_id=1, source_target_pairs={{0,4},{4,0},{8,12},{12,8},{16,20},{20,16},{24,28},{28,24},{1,5},{5... | collective-permute-start | bytes 11010056 | tf_op jit(solution)/shard_map/ppermute | solution.py:145
  266.8 184.1 %collective-permute-start.11 = (bf16[256,7168]{1,0:T(8,128)(2,1)}, bf16[256,7168]{1,0:T(8,128)(2,1)}, u32[]{:S(2)}, u32[]{:S(2)}) collective-permute-start(bf16[256,7168]{1,0:T(8,128)(2,1)} %constant_dynamic-slice_fusion.2), channel_id=1, source_target_pairs={{0,8},{4,12},{8,0},{12,4},{16,24},{20,28},{24,16},{28,20},{1,9},{5... | collective-permute-start | bytes 11010056 | tf_op jit(solution)/shard_map/ppermute | solution.py:145
  274.7 1.9 copy-start.2
  279.6 164.8 %collective-permute-start.5 = (bf16[672,896]{1,0:T(8,128)(2,1)S(1)}, bf16[672,896]{1,0:T(8,128)(2,1)}, u32[]{:S(2)}, u32[]{:S(2)}) collective-permute-start(bf16[672,896]{1,0:T(8,128)(2,1)S(1)} %dynamic-slice_bitcast_fusion.2), channel_id=1, source_target_pairs={{0,24},{4,28},{8,16},{12,20},{16,8},{20,12},{24,0},{28,4},{1,25},{... | collective-permute-start | bytes 3612680 | tf_op jit(solution)/shard_map/ppermute | solution.py:145
  283.5 1.0 copy-start.10
  284.5 162.4 %collective-permute-start.6 = (bf16[672,896]{1,0:T(8,128)(2,1)}, bf16[672,896]{1,0:T(8,128)(2,1)}, u32[]{:S(2)}, u32[]{:S(2)}) collective-permute-start(bf16[672,896]{1,0:T(8,128)(2,1)} %dynamic-slice_bitcast_fusion.1), channel_id=1, source_target_pairs={{0,24},{4,28},{8,16},{12,20},{16,8},{20,12},{24,0},{28,4},{1,25},{... | collective-permute-start | bytes 3612680 | tf_op jit(solution)/shard_map/ppermute | solution.py:145
  289.7 152.2 %collective-permute-start.4 = (bf16[672,896]{1,0:T(8,128)(2,1)}, bf16[672,896]{1,0:T(8,128)(2,1)}, u32[]{:S(2)}, u32[]{:S(2)}) collective-permute-start(bf16[672,896]{1,0:T(8,128)(2,1)} %get-tuple-element.6), channel_id=1, source_target_pairs={{0,16},{4,20},{8,24},{12,28},{16,0},{20,4},{24,8},{28,12},{1,17},{... | collective-permute-start | bytes 3612680 | tf_op jit(solution)/shard_map/ppermute | solution.py:145
  293.3 14.7 %copy-start.11 = (bf16[672,896]{1,0:T(8,128)(2,1)S(1)}, bf16[672,896]{1,0:T(8,128)(2,1)}, u32[]{:S(2)}) copy-start(bf16[672,896]{1,0:T(8,128)(2,1)} %copy-done.10) | copy-start | bytes 3612676
  449.4 87.6 %collective-permute-start.8 = (bf16[256,7168]{1,0:T(8,128)(2,1)}, bf16[256,7168]{1,0:T(8,128)(2,1)S(1)}, u32[]{:S(2)}, u32[]{:S(2)}) collective-permute-start(bf16[256,7168]{1,0:T(8,128)(2,1)} %collective-permute-done.7), channel_id=1, source_target_pairs={{0,1},{1,0},{2,3},{3,2},{4,5},{5,4},{6,7},{7,6},{8,9},{9,8},{10,11... | collective-permute-start | bytes 11010056 | tf_op jit(solution)/shard_map/ppermute | solution.py:145
  449.4 82.3 %collective-permute-start.9 = (bf16[256,7168]{1,0:T(8,128)(2,1)}, bf16[256,7168]{1,0:T(8,128)(2,1)S(1)}, u32[]{:S(2)}, u32[]{:S(2)}) collective-permute-start(bf16[256,7168]{1,0:T(8,128)(2,1)} %collective-permute-done.7), channel_id=1, source_target_pairs={{0,2},{1,3},{2,0},{3,1},{4,6},{5,7},{6,4},{7,5},{8,10},{9,11},{10,... | collective-permute-start | bytes 11010056 | tf_op jit(solution)/shard_map/ppermute | solution.py:145
  450.9 159.7 %collective-permute-start.13 = (bf16[256,7168]{1,0:T(8,128)(2,1)}, bf16[256,7168]{1,0:T(8,128)(2,1)}, u32[]{:S(2)}, u32[]{:S(2)}) collective-permute-start(bf16[256,7168]{1,0:T(8,128)(2,1)} %collective-permute-done.11), channel_id=1, source_target_pairs={{0,2},{1,3},{2,0},{3,1},{4,6},{5,7},{6,4},{7,5},{8,10},{9,11},{10,... | collective-permute-start | bytes 11010056 | tf_op jit(solution)/shard_map/ppermute | solution.py:145
  451.5 81.5 %collective-permute-start.15 = (bf16[256,7168]{1,0:T(8,128)(2,1)}, bf16[256,7168]{1,0:T(8,128)(2,1)}, u32[]{:S(2)}, u32[]{:S(2)}) collective-permute-start(bf16[256,7168]{1,0:T(8,128)(2,1)} %collective-permute-done.11), channel_id=1, source_target_pairs={{0,4},{4,0},{8,12},{12,8},{16,20},{20,16},{24,28},{28,24},{1,5},{5... | collective-permute-start | bytes 11010056 | tf_op jit(solution)/shard_map/ppermute | solution.py:145
  469.6 145.1 %collective-permute-start.12 = (bf16[256,7168]{1,0:T(8,128)(2,1)}, bf16[256,7168]{1,0:T(8,128)(2,1)S(1)}, u32[]{:S(2)}, u32[]{:S(2)}) collective-permute-start(bf16[256,7168]{1,0:T(8,128)(2,1)} %collective-permute-done.11), channel_id=1, source_target_pairs={{0,1},{1,0},{2,3},{3,2},{4,5},{5,4},{6,7},{7,6},{8,9},{9,8},{10,11... | collective-permute-start | bytes 11010056 | tf_op jit(solution)/shard_map/ppermute | solution.py:145
  531.8 89.2 %collective-permute-start.10 = (bf16[256,7168]{1,0:T(8,128)(2,1)S(1)}, bf16[256,7168]{1,0:T(8,128)(2,1)S(1)}, u32[]{:S(2)}, u32[]{:S(2)}) collective-permute-start(bf16[256,7168]{1,0:T(8,128)(2,1)S(1)} %collective-permute-done.9), channel_id=1, source_target_pairs={{0,1},{1,0},{2,3},{3,2},{4,5},{5,4},{6,7},{7,6},{8,9},{9,8},{10,11... | collective-permute-start | bytes 11010056 | tf_op jit(solution)/shard_map/ppermute | solution.py:145
  537.0 169.6 %collective-permute-start.16 = (bf16[256,7168]{1,0:T(8,128)(2,1)}, bf16[256,7168]{1,0:T(8,128)(2,1)}, u32[]{:S(2)}, u32[]{:S(2)}) collective-permute-start(bf16[256,7168]{1,0:T(8,128)(2,1)} %collective-permute-done.15), channel_id=1, source_target_pairs={{0,1},{1,0},{2,3},{3,2},{4,5},{5,4},{6,7},{7,6},{8,9},{9,8},{10,11... | collective-permute-start | bytes 11010056 | tf_op jit(solution)/shard_map/ppermute | solution.py:145
  537.0 151.8 %collective-permute-start.17 = (bf16[256,7168]{1,0:T(8,128)(2,1)}, bf16[256,7168]{1,0:T(8,128)(2,1)}, u32[]{:S(2)}, u32[]{:S(2)}) collective-permute-start(bf16[256,7168]{1,0:T(8,128)(2,1)} %collective-permute-done.15), channel_id=1, source_target_pairs={{0,2},{1,3},{2,0},{3,1},{4,6},{5,7},{6,4},{7,5},{8,10},{9,11},{10,... | collective-permute-start | bytes 11010056 | tf_op jit(solution)/shard_map/ppermute | solution.py:145
  610.5 24.3 %collective-permute-start.14 = (bf16[256,7168]{1,0:T(8,128)(2,1)}, bf16[256,7168]{1,0:T(8,128)(2,1)}, u32[]{:S(2)}, u32[]{:S(2)}) collective-permute-start(bf16[256,7168]{1,0:T(8,128)(2,1)} %collective-permute-done.13), channel_id=1, source_target_pairs={{0,1},{1,0},{2,3},{3,2},{4,5},{5,4},{6,7},{7,6},{8,9},{9,8},{10,11... | collective-permute-start | bytes 11010056 | tf_op jit(solution)/shard_map/ppermute | solution.py:145
  620.9 2.2 copy-start.4
  688.8 46.4 %collective-permute-start.18 = (bf16[256,7168]{1,0:T(8,128)(2,1)}, bf16[256,7168]{1,0:T(8,128)(2,1)S(1)}, u32[]{:S(2)}, u32[]{:S(2)}) collective-permute-start(bf16[256,7168]{1,0:T(8,128)(2,1)} %collective-permute-done.17), channel_id=1, source_target_pairs={{0,1},{1,0},{2,3},{3,2},{4,5},{5,4},{6,7},{7,6},{8,9},{9,8},{10,11... | collective-permute-start | bytes 11010056 | tf_op jit(solution)/shard_map/ppermute | solution.py:145
  714.9 17.7 %copy-start.8 = (bf16[672,1024]{1,0:T(8,128)(2,1)S(1)}, bf16[672,1024]{1,0:T(8,128)(2,1)}, u32[]{:S(2)}) copy-start(bf16[672,1024]{1,0:T(8,128)(2,1)} %add_convert_fusion.3) | copy-start | bytes 4128772
  749.1 16.7 %copy-start.9 = (bf16[672,1024]{1,0:T(8,128)(2,1)S(1)}, bf16[672,1024]{1,0:T(8,128)(2,1)}, u32[]{:S(2)}) copy-start(bf16[672,1024]{1,0:T(8,128)(2,1)} %add_convert_fusion.1) | copy-start | bytes 4128772
  765.8 1.3 copy-start.6
  767.1 4.0 copy-start.3
  809.4 25.0 %collective-permute-start.26 = (bf16[224,2048]{1,0:T(8,128)(2,1)S(1)}, bf16[224,2048]{1,0:T(8,128)(2,1)}, u32[]{:S(2)}, u32[]{:S(2)}) collective-permute-start(bf16[224,2048]{1,0:T(8,128)(2,1)S(1)} %get-tuple-element.16), channel_id=1, source_target_pairs={{0,8},{4,12},{8,0},{12,4},{16,24},{20,28},{24,16},{28,20},{1,9},{5... | collective-permute-start | bytes 2752520 | tf_op jit(solution)/shard_map/ppermute | solution.py:145
  838.2 22.2 %collective-permute-start.27 = (bf16[2,224,1024]{2,1,0:T(8,128)(2,1)S(1)}, bf16[2,224,1024]{2,1,0:T(8,128)(2,1)S(1)}, u32[]{:S(2)}, u32[]{:S(2)}) collective-permute-start(bf16[2,224,1024]{2,1,0:T(8,128)(2,1)S(1)} %get-tuple-element.14), channel_id=1, source_target_pairs={{0,4},{4,0},{8,12},{12,8},{16,20},{20,16},{24,28},{28,24},{1,5},{5... | collective-permute-start | bytes 2752520 | tf_op jit(solution)/shard_map/ppermute | solution.py:145
  909.3 6.8 collective-permute-start.28
  920.9 2.9 copy-start.5
  924.0 42.2 %collective-permute-start.29 = (bf16[1024,896]{1,0:T(8,128)(2,1)S(1)}, bf16[1024,896]{1,0:T(8,128)(2,1)}, u32[]{:S(2)}, u32[]{:S(2)}) collective-permute-start(bf16[1024,896]{1,0:T(8,128)(2,1)S(1)} %fusion.4), channel_id=1, source_target_pairs={{0,2},{1,3},{2,0},{3,1},{4,6},{5,7},{6,4},{7,5},{8,10},{9,11},{10,... | collective-permute-start | bytes 5505032 | tf_op jit(solution)/shard_map/ppermute | solution.py:145
  925.6 44.8 %copy-start.1 = (bf16[896,128]{1,0:T(8,128)(2,1)S(1)}, bf16[896,128]{1,0:T(8,128)(2,1)}, u32[]{:S(2)}) copy-start(bf16[896,128]{1,0:T(8,128)(2,1)} %param.13) | copy-start | bytes 688132
Sparse Core Ops, SparseCore 0:
  10.2 74.3 all-gather.2
  86.8 154.3 all-gather.4

commit v2 on v0

--- a/solution.py
+++ b/solution.py
@@ -1,6 +1,10 @@
+import functools
+
 import jax
 import jax.numpy as jnp
 from jax import lax
+from jax.experimental import pallas as pl
+from jax.experimental.pallas import tpu as pltpu
 from jax.sharding import PartitionSpec as P
 
 HD = 224
@@ -134,20 +138,455 @@
     )
 
 
+CHUNK = 256
+GROUP = 128
+RANK = 128
+LOG2E = 1.4426950408889634
+
+
+def swap(array, axis, size, bit):
+    return lax.ppermute(array, axis, [(i, i ^ bit) for i in range(size)])
+
+
+def pick(array, index, axis=0):
+    return lax.dynamic_index_in_dim(array, index, axis, keepdims=False)
+
+
+def after(array, *earlier):
+    return lax.optimization_barrier((array, *earlier))[0]
+
+
+def fence(*arrays):
+    return lax.optimization_barrier(arrays)
+
+
+def norm_kernel(first, inputs_ref, gain_ref, out_ref):
+    widened = inputs_ref[...].astype(jnp.float32)
+    mean = jnp.mean(widened * widened, axis=-1, keepdims=True)
+    out_ref[...] = (widened * lax.rsqrt(mean + 1e-05) * gain_ref[...]).astype(jnp.bfloat16)
+
+
+def normalise(inputs, norm_gain, part, count):
+    width = inputs.shape[1]
+    rows = 64
+    steps = count // rows
+    return pl.pallas_call(
+        norm_kernel,
+        grid_spec=pltpu.PrefetchScalarGridSpec(
+            num_scalar_prefetch=1,
+            grid=(steps,),
+            in_specs=[
+                pl.BlockSpec((rows, width), lambda i, first: (first[0] * steps + i, 0)),
+                pl.BlockSpec((1, width), lambda i, first: (0, 0)),
+            ],
+            out_specs=pl.BlockSpec((rows, width), lambda i, first: (i, 0)),
+        ),
+        out_shape=jax.ShapeDtypeStruct((count, width), jnp.bfloat16),
+        compiler_params=pltpu.CompilerParams(vmem_limit_bytes=40 * 2**20),
+        cost_estimate=pl.CostEstimate(flops=1, bytes_accessed=1, transcendentals=0),
+    )(part.reshape(1), inputs, norm_gain.reshape(1, width))
+
+
+def project_kernel(sets, order, up_ref, down_ref, *refs):
+    token_refs, weight_refs = refs[: len(sets)], refs[len(sets) : -3]
+    turned_ref, keys_ref, held_ref = refs[-3:]
+    rows = weight_refs[0].shape[1]
+    main = 3 * HD
+    step = pl.program_id(0)
+
+    @pl.when(step == 0)
+    def fill():
+        for number, weight_ref in enumerate(weight_refs):
+            columns = pl.ds(pl.multiple_of(order[number] * rows, 128), rows)
+            held_ref[pl.ds(0, main), columns] = weight_ref[...]
+        held_ref[pl.ds(main, RANK), :] = down_ref[...]
+
+    def run(tokens_ref):
+        total = lax.dot_general(
+            held_ref[...],
+            tokens_ref[...],
+            (((1,), (1,)), ((), ())),
+            preferred_element_type=jnp.float32,
+        )
+        low_rank = total[main:].astype(jnp.bfloat16)
+        total = total[:main] + jnp.dot(up_ref[...], low_rank, preferred_element_type=jnp.float32)
+        for number in range(turned_ref.shape[0]):
+            columns = slice(number * CHUNK, (number + 1) * CHUNK)
+            turned_ref[number, pl.ds(0, HD), :] = total[:HD, columns].astype(jnp.bfloat16)
+            turned_ref[number, pl.ds(HD, HD), :] = total[2 * HD :, columns].astype(jnp.bfloat16)
+            keys_ref[number] = total[HD : 2 * HD, columns].T.astype(jnp.bfloat16)
+
+    for (first, count), tokens_ref in zip(sets, token_refs):
+        pl.when((step >= first) & (step < first + count))(functools.partial(run, tokens_ref))
+
+
+def project(token_sets, up, down, weight_blocks, order):
+    width = token_sets[0].shape[1]
+    per_step = 1 if len(token_sets) > 1 else 2
+    main = 3 * HD
+    sets, steps = [], 0
+    for tokens in token_sets:
+        sets.append((steps, tokens.shape[0] // (per_step * CHUNK)))
+        steps += sets[-1][1]
+    chunks = steps * per_step
+    whole = lambda array: pl.BlockSpec(array.shape, lambda i, *_: (0,) * array.ndim)
+
+    def token_spec(first, count):
+        return pl.BlockSpec(
+            (per_step * CHUNK, width), lambda i, *_: (jnp.clip(i - first, 0, count - 1), 0)
+        )
+
+    return pl.pallas_call(
+        functools.partial(project_kernel, tuple(sets)),
+        grid_spec=pltpu.PrefetchScalarGridSpec(
+            num_scalar_prefetch=1,
+            grid=(steps,),
+            in_specs=[whole(array) for array in (up, down)]
+            + [token_spec(*one) for one in sets]
+            + [
+                pl.BlockSpec(
+                    (main, array.shape[1]), lambda i, *_: (0, 0), pipeline_mode=pl.Buffered(1)
+                )
+                for array in weight_blocks
+            ],
+            out_specs=[
+                pl.BlockSpec((per_step, 2 * HD, CHUNK), lambda i, *_: (i, 0, 0)),
+                pl.BlockSpec((per_step, CHUNK, HD), lambda i, *_: (i, 0, 0)),
+            ],
+            scratch_shapes=[pltpu.VMEM((main + RANK, width), jnp.bfloat16)],
+        ),
+        out_shape=[
+            jax.ShapeDtypeStruct((chunks, 2 * HD, CHUNK), jnp.bfloat16),
+            jax.ShapeDtypeStruct((chunks, CHUNK, HD), jnp.bfloat16),
+        ],
+        compiler_params=pltpu.CompilerParams(vmem_limit_bytes=58 * 2**20),
+        cost_estimate=pl.CostEstimate(flops=1, bytes_accessed=1, transcendentals=0),
+    )(order, up, down, *token_sets, *weight_blocks)
+
+
+def attention_kernel(
+    half,
+    chunk_table,
+    cache_table,
+    length_ref,
+    turned_ref,
+    keys_ref,
+    *refs,
+):
+    block_refs, (out_ref, total_ref, cached_keys, cached_values) = refs[:-4], refs[-4:]
+    tile = 2 * pl.program_id(0) + half
+    factor = HD ** (-0.5) * LOG2E
+    width = 2 * CHUNK
+    length = length_ref[0]
+
+    @pl.when(pl.program_id(0) == 0)
+    def gather_cache():
+        for number in range(cache_table.shape[0]):
+            entry = cache_table[number]
+            for bit, block_ref in enumerate(block_refs):
+
+                @pl.when((number * CHUNK < length) & (entry // 4 == bit))
+                def take(number=number, entry=entry, block_ref=block_ref):
+                    other = (entry // 2) % 2
+                    columns = pl.ds(pl.multiple_of((entry % 2) * CHUNK, CHUNK), CHUNK)
+                    place = pl.ds(number * CHUNK, CHUNK)
+                    keys = block_ref[other, pl.ds(0, HD), columns].astype(jnp.float32)
+                    cached_keys[place, :] = keys.T.astype(jnp.bfloat16)
+                    cached_values[:, place] = block_ref[other, pl.ds(HD, HD), columns]
+
+    def joined(ref, first, rows):
+        pieces = [ref[chunk_table[first + place], rows, :] for place in range(2)]
+        return jnp.concatenate(pieces, axis=1)
+
+    query_rows, value_rows = pl.ds(0, HD), pl.ds(HD, HD)
+    queries = joined(turned_ref, 2 * tile, query_rows)
+
+    def step(state, keys, values, visible):
+        largest, weight_sum = state
+        scores = jnp.dot(keys, queries, preferred_element_type=jnp.float32)
+        if visible is not None:
+            scores = jnp.where(visible, scores, lowest)
+        new_largest = jnp.maximum(largest, jnp.max(scores, axis=0, keepdims=True))
+        weights = jnp.exp2((scores - new_largest) * factor)
+        fade = jnp.exp2((largest - new_largest) * factor)
+        weight_sum = weight_sum * fade + jnp.sum(weights, axis=0, keepdims=True)
+        total_ref[...] = total_ref[...] * fade + jnp.dot(
+            values, weights.astype(jnp.bfloat16), preferred_element_type=jnp.float32
+        )
+        return (new_largest, weight_sum)
+
+    def new_step(number, state, visible=None):
+        first = 2 * number
+        pieces = [keys_ref[chunk_table[first + place]] for place in range(2)]
+        keys = jnp.concatenate(pieces, axis=0)
+        return step(state, keys, joined(turned_ref, first, value_rows), visible)
+
+    def cache_step(number, state):
+        place = pl.ds(pl.multiple_of(number * CHUNK, CHUNK), CHUNK)
+        row = lax.broadcasted_iota(jnp.int32, (CHUNK, width), 0)
+        visible = row + number * CHUNK < length
+        return step(state, cached_keys[place, :], cached_values[:, place], visible)
+
+    total_ref[...] = jnp.zeros_like(total_ref)
+    state = (jnp.full((1, width), lowest, jnp.float32), jnp.zeros((1, width), jnp.float32))
+    key_row = lax.broadcasted_iota(jnp.int32, (width, width), 0)
+    query_column = lax.broadcasted_iota(jnp.int32, (width, width), 1)
+    state = new_step(tile, state, key_row <= query_column)
+    state = lax.fori_loop(0, tile, new_step, state)
+    state = lax.fori_loop(0, pl.cdiv(length, CHUNK), cache_step, state)
+    out_ref[...] = (total_ref[...] / state[1]).astype(jnp.bfloat16)
+
+
+def attention(half, turned, keys, cache_blocks, chunk_table, cache_table, length):
+    whole = lambda array: pl.BlockSpec(array.shape, lambda i, *_: (0, 0, 0))
+    cache_span = cache_table.shape[0] * CHUNK
+    return pl.pallas_call(
+        functools.partial(attention_kernel, half),
+        grid_spec=pltpu.PrefetchScalarGridSpec(
+            num_scalar_prefetch=3,
+            grid=(QLEN // (4 * CHUNK),),
+            in_specs=[whole(array) for array in (turned, keys, *cache_blocks)],
+            out_specs=pl.BlockSpec((HD, 2 * CHUNK), lambda i, *_: (0, i)),
+            scratch_shapes=[
+                pltpu.VMEM((HD, 2 * CHUNK), jnp.float32),
+                pltpu.VMEM((cache_span, HD), jnp.bfloat16),
+                pltpu.VMEM((HD, cache_span), jnp.bfloat16),
+            ],
+        ),
+        out_shape=jax.ShapeDtypeStruct((HD, QLEN // 2), jnp.bfloat16),
+        compiler_params=pltpu.CompilerParams(vmem_limit_bytes=48 * 2**20),
+        cost_estimate=pl.CostEstimate(flops=1, bytes_accessed=1, transcendentals=0),
+    )(chunk_table, cache_table, length, turned, keys, *cache_blocks)
+
+
+def per_device_paired(
+    inputs,
+    norm_gain,
+    qkv_weight,
+    adapter_down,
+    adapter_up,
+    out_weight,
+    cache_keys,
+    cache_values,
+    cache_lengths,
+    block_perm,
+):
+    tok_dev, width = inputs.shape
+    rows = qkv_weight.shape[0]
+    plane, side = lax.axis_index("z"), lax.axis_index("x")
+    row, core = lax.axis_index("y"), lax.axis_index("core")
+    seq, mp = 2 * plane + side, 2 * row + core
+    role = plane % 2
+
+    def over_z(array, bit):
+        return swap(array, "z", 4, bit)
+
+    def over_x(array):
+        return swap(array, "x", 2, 1)
+
+    def over_y(array):
+        return swap(array, "y", 2, 1)
+
+    def over_core(array):
+        return swap(array, "core", 2, 1)
+
+    part = normalise(inputs, norm_gain, mp, CHUNK)
+    plane_axes = ("x", "y", "core")
+    plane_axes = ("x", "y", "core")
+    part_z = over_z(part, 1)
+    part_x = over_x(part)
+
+    turned = qkv_weight.reshape(rows, 3, 4, HD).transpose(2, 1, 3, 0).reshape(2, 2, 3 * HD, rows)
+    kept = pick(turned, side, 1)
+    given = pick(turned, 1 - side, 1)
+    from_x = over_x(jnp.stack([pick(given, role), pick(given, 1 - role)]))
+    kept_near = pick(kept, 1 - role)
+    far = {bit: [over_z(pick(kept, role ^ (bit & 1)), bit)] for bit in (2, 3)}
+    share = lax.dynamic_slice_in_dim(adapter_down, mp * (rows // 4), rows // 4, 0)
+    down = lax.all_gather(share, ("z", "x", "y", "core"), axis=0, tiled=True)
+
+    def turned_cache(cache):
+        blocks, size, _ = cache.shape
+        return cache.reshape(blocks * size, 4, HD).transpose(1, 2, 0)
+
+    cached = jnp.concatenate([turned_cache(cache_keys), turned_cache(cache_values)], axis=1)
+    cached = cached.reshape(2, 2, 2 * HD, cached.shape[2])
+
+    part_z, part_x, from_x, far[2][0], far[3][0], kept_near, cached, down, inputs = fence(
+        part_z, part_x, from_x, far[2][0], far[3][0], kept_near, cached, down, inputs
+    )
+    pair_tokens = lax.all_gather(part_z, plane_axes, axis=0, tiled=True)
+    near = over_z(jnp.stack([kept_near, from_x[1]]), 1)
+    for bit in (2, 3):
+        far[bit].append(over_z(from_x[bit & 1], bit))
+    cache_from_x = over_x(pick(cached, 1 - side, 1))
+    part_y = over_y(part_x[:GROUP])
+    normed = normalise(inputs, norm_gain, jnp.int32(0), tok_dev)
+    down = down.T
+
+    near, far[2][1], far[3][1], cache_from_x, part_y, normed, part_x, down, cached = fence(
+        near, far[2][1], far[3][1], cache_from_x, part_y, normed, part_x, down, cached
+    )
+    cache_both = jnp.stack([pick(cached, side, 1), cache_from_x], axis=1)
+    cache_blocks = [pick(cache_both, role)]
+    for bit in (1, 2, 3):
+        cache_blocks.append(over_z(pick(cache_both, role ^ (bit & 1)), bit))
+    core_x = over_core(part_x)
+    start = (mp ^ 2) * CHUNK + GROUP
+    part_yx = over_x(lax.dynamic_slice_in_dim(normed, start, GROUP, 0))
+    weight_blocks = [pick(kept, role), from_x[0], near[0], near[1], *far[2], *far[3]]
+    order = jnp.arange(8, dtype=jnp.int32) ^ seq
+    up = adapter_up.reshape(3, RANK, 4, HD).transpose(2, 0, 3, 1).reshape(4, 3 * HD, RANK)
+    up = pick(up, 2 * role + side)
+
+    requests = jnp.stack([plane, plane ^ 1])
+    lengths = lookup(cache_lengths, requests)
+    logical = requests[:, None] * 4 + jnp.arange(4, dtype=jnp.int32)[None, :]
+    hits = logical[..., None] == block_perm
+    physical = jnp.sum(
+        jnp.where(hits, jnp.arange(block_perm.shape[0], dtype=jnp.int32), 0), axis=-1
+    )
+    cache_table = (((physical // 2) ^ seq) * 2 + physical % 2).astype(jnp.int32)
+
+    def attend(number, half, projected):
+        turned_rows, key_rows = projected
+        return attention(
+            half,
+            turned_rows,
+            key_rows,
+            cache_blocks,
+            chunk_tables[number],
+            cache_table[number],
+            lengths[number : number + 1],
+        )
+
+    half_dev = tok_dev // 2
+
+    place = jnp.arange(8, dtype=jnp.int32)
+    moved = (place % 4) ^ mp
+    chunk_tables = (
+        jnp.where(place // 4 == side, place % 4, 4 + moved),
+        place,
+    )
+    local_projected = project((normed,), up, down, weight_blocks, order)
+
+    *cache_blocks, up, local_turned, local_keys, out_weight, core_x, part_y, part_yx = fence(
+        *cache_blocks, up, *local_projected, out_weight, core_x, part_y, part_yx
+    )
+    pair_projected = project((pair_tokens,), up, down, weight_blocks, order)
+    pair_first = attend(1, 0, pair_projected)
+    part_y, part_yx = fence(part_y, part_yx, pair_projected[0])[:2]
+    part_y = jnp.concatenate([part_y, part_yx])
+    core_y = over_core(part_y)
+    pair_first, core_y, part_y, up, pair_turned = fence(
+        pair_first, core_y, part_y, up, pair_projected[0]
+    )
+
+    out_rows = lax.all_gather(out_weight, ("z", "x"), axis=1, tiled=True)
+    out_cols = out_rows.shape[1] // 4
+
+    def out_columns(to_row, to_core):
+        return lax.dynamic_slice_in_dim(out_rows, (2 * to_row + to_core) * out_cols, out_cols, 1)
+
+    columns = {
+        "away_core": out_columns(1 - row, 1 - core),
+        "away": out_columns(1 - row, core),
+        "here_core": out_columns(row, 1 - core),
+        "here": out_columns(row, core),
+    }
+
+    def rounded(array):
+        return array.astype(jnp.bfloat16)
+
+    def out_part(heads, name):
+        return lax.dot_general(
+            heads, columns[name], (((0,), (0,)), ((), ())), preferred_element_type=jnp.float32
+        )
+
+    def crossing(attended):
+        return lax.dynamic_slice_in_dim(attended, (1 - side) * half_dev, half_dev, 1)
+
+    def both_sides(attended, theirs):
+        mine = lax.dynamic_slice_in_dim(attended, side * half_dev, half_dev, 1)
+        return jnp.where(side == 0, jnp.stack([mine, theirs]), jnp.stack([theirs, mine]))
+
+    def all_heads(own, own_theirs, pair, pair_theirs):
+        own_heads, pair_heads = both_sides(own, own_theirs), both_sides(pair, pair_theirs)
+        return jnp.where(
+            role == 0,
+            jnp.concatenate([own_heads, pair_heads]),
+            jnp.concatenate([pair_heads, own_heads]),
+        ).reshape(4 * HD, half_dev)
+
+    def summed(heads):
+        away = over_core(rounded(out_part(heads, "away_core")))
+        here = over_core(rounded(out_part(heads, "here_core")))
+        away = rounded(out_part(heads, "away") + away.astype(jnp.float32))
+        return away, out_part(heads, "here") + here.astype(jnp.float32)
+
+    pair_first = over_z(pair_first, 1)
+    parts_projected = project((part_x, core_x, part_y, core_y), up, down, weight_blocks, order)
+    pair_first, parts_turned, parts_keys = fence(pair_first, *parts_projected)
+    pair_first_crossed = over_x(crossing(pair_first))
+    own_projected = (
+        jnp.concatenate([local_turned, parts_turned]),
+        jnp.concatenate([local_keys, parts_keys]),
+    )
+    own_first = attend(0, 0, own_projected)
+    pair_first_crossed, own_first, pair_turned, own_turned = fence(
+        pair_first_crossed, own_first, pair_turned, own_projected[0]
+    )
+    own_first_crossed = over_x(crossing(own_first))
+    pair_second = attend(1, 1, (pair_turned, pair_projected[1]))
+    own_first_crossed, pair_second = fence(own_first_crossed, pair_second)
+    pair_second = over_z(pair_second, 1)
+    first_sent, first_here = summed(
+        all_heads(own_first, own_first_crossed, pair_first, pair_first_crossed)
+    )
+    pair_second, first_sent, first_here, own_turned = fence(
+        pair_second, first_sent, first_here, own_turned
+    )
+    first_received = over_y(first_sent)
+    pair_second_crossed = over_x(crossing(pair_second))
+    own_second = attend(0, 1, (own_turned, own_projected[1]))
+    pair_second_crossed, own_second = fence(pair_second_crossed, own_second)
+    own_second_crossed = over_x(crossing(own_second))
+    own_second_crossed, first_received = fence(own_second_crossed, first_received)
+    second_sent, second_here = summed(
+        all_heads(own_second, own_second_crossed, pair_second, pair_second_crossed)
+    )
+    second_received = over_y(second_sent)
+    return jnp.concatenate(
+        [
+            rounded(first_here + first_received.astype(jnp.float32)),
+            rounded(second_here + second_received.astype(jnp.float32)),
+        ]
+    )
+
+
 def solution(mesh):
+    paired = mesh.shape["seq"] == 8 and mesh.shape["mp"] == 4
+    if paired:
+        seq, mp = ("z", "x"), ("y", "core")
+        mesh = jax.sharding.Mesh(mesh.devices.reshape(4, 2, 2, 2), seq + mp)
+    else:
+        seq, mp = "seq", "mp"
     in_specs = (
-        P("seq", None),
+        P(seq, None),
         P(),
-        P("seq", None, "mp"),
-        P("seq", None),
-        P(None, None, "mp"),
-        P("mp", "seq"),
-        P("seq", None, "mp"),
-        P("seq", None, "mp"),
+        P(seq, None, mp),
+        P(seq, None),
+        P(None, None, mp),
+        P(mp, seq),
+        P(seq, None, mp),
+        P(seq, None, mp),
         P(),
         P(),
     )
-    out_specs = P("seq", "mp")
     return jax.shard_map(
-        per_device, mesh=mesh, in_specs=in_specs, out_specs=out_specs, check_vma=False
-    )
+        per_device_paired if paired else per_device,
+        mesh=mesh,
+        in_specs=in_specs,
+        out_specs=P(seq, mp),
+        check_vma=False,
+    )

time: 1870 us -> 587 us (0.31)
  waiting for transfers between devices: 1490 us -> 282 us
  matrix products: 241 us -> 20 us
  Pallas kernels: 0 us -> 148 us
  other arithmetic: 90.8 us -> 13.8 us
  starting transfers between devices: 0.42 us -> 37 us
  local copies, waits for them, and re-layouts: 28.5 us -> 64.6 us
    all_gather x5 -> x3, waiting for transfers between devices: 1430 us -> 19.9 us  [the longest x1 19.9 us: per_device_paired(): pair_tokens = lax.all_gather(part_z, plane_axes, axis=0, tiled=True)]
    ppermute x0 -> x28, waiting for transfers between devices: none -> 262 us  [swap(): return lax.ppermute(array, axis, [(i, i ^ bit) for i in range(size)])]
    dot_general x5 -> x8, matrix products: 241 us -> 20 us  [out_part(): lax.dot_general(heads, columns[name], (((0,), (0,)), ((), ())), preferred...]
    pallas_call x0 -> x9, Pallas kernels: none -> 148 us  [the longest x3 82.7 us: project(): pl.pallas_call(functools.partial(project_kernel, tuple(sets)), grid_spec=...]
    reduce_sum x2 -> x1, other arithmetic: 73.2 us -> 0.22 us  [per_device_paired(): jnp.sum(jnp.where(hits, jnp.arange(block_perm.shape[0], dtype=jnp.int32),...]
    unnamed x7 -> x3, waiting for transfers between devices: 65 us -> 0.05 us
    ppermute x0 -> x28, starting transfers between devices: none -> 36.6 us  [swap(): return lax.ppermute(array, axis, [(i, i ^ bit) for i in range(size)])]
  transfers between devices with their start and end apart: 6 -> 31, of which waited for: 5 -> 15; matrix products, arithmetic and copies ran while one was open for 16% -> 15% of each run, Pallas kernels for 0% -> 25%
where the time goes in v2:
time: 587 us; the launch traced here: 580 us
  waiting for transfers between devices  282 us (48%)
  Pallas kernels  148 us (25%)
  local copies, waits for them, and re-layouts  64.6 us (11%)
  starting transfers between devices  37 us (6%)
  matrix products  20 us (3%)
  between operations  14 us (2%)
  other arithmetic  13.8 us (2%)
    ppermute x28, waiting for transfers between devices, swap(): return lax.ppermute(array, axis, [(i, i ^ bit) for i in range(size)])  262 us
    pallas_call x3, Pallas kernels, project(): pl.pallas_call(functools.partial(project_kernel, tuple(sets)), grid_spec=...  82.7 us
    pallas_call x4, Pallas kernels, attention(): pl.pallas_call(functools.partial(attention_kernel, half), grid_spec=pltpu...  41.7 us
    ppermute x28, starting transfers between devices, swap(): return lax.ppermute(array, axis, [(i, i ^ bit) for i in range(size)])  36.6 us
    pallas_call x2, Pallas kernels, normalise(): pl.pallas_call(norm_kernel, grid_spec=pltpu.PrefetchScalarGridSpec(num_sc...  23.6 us
    unnamed x59, local copies, waits for them, and re-layouts  20.4 us
    dot_general x8, matrix products, out_part(): lax.dot_general(heads, columns[name], (((0,), (0,)), ((), ())), preferred...  20 us
    all_gather x1, waiting for transfers between devices, per_device_paired(): pair_tokens = lax.all_gather(part_z, plane_axes, axis=0, tiled=True)  19.9 us
  transfers between devices with their start and end apart: 31, of which 15 were waited for; matrix products, arithmetic and copies ran while one was open for 15% of the time, Pallas kernels for 25%

profile of v2, /device:TPU:0, one launch (start us, length us, event | category | flops | bytes accessed | tf_op | source)
XLA Modules:
  0.0 580.0 jit_solution(16398707651792014307)
XLA Ops:
  7.3 5.5 shard_map.100
  12.8 3.0 collective-permute-start
  15.8 1.5 collective-permute-start.1
  18.1 7.5 %copy.34 = bf16[896,3,896]{0,2,1:T(8,128)(2,1)} copy(bf16[896,3,896]{2,0,1:T(8,128)(2,1)} %param.12) | data formatting | bytes 9633792 | tf_op args[2]
  25.6 2.8 copy.35
  28.4 1.9 dynamic-slice_bitcast_fusion
  30.3 1.6 pad_maximum_fusion
  32.5 2.6 collective-permute-start.3
  35.1 1.8 reshape.95
  36.9 1.6 copy.41
  38.5 3.8 reshape.96
  42.4 2.4 copy.42
  44.8 2.6 pad_maximum_fusion.2
  47.4 82.9 %collective-permute-done.3.refs_5_.refs_8_ = bf16[672,896]{1,0:T(8,128)(2,1)S(1)} collective-permute-done((bf16[672,896]{1,0:T(8,128)(2,1)S(1)}, bf16[672,896]{1,0:T(8,128)(2,1)S(1)}, u32[]{:S(2)}, u32[]{:S(2)}) %collective-permute-start.3) | collective-permute-done | bytes 1204256 | tf_op jit(solution)/shard_map/ppermute | solution.py:148
  130.3 27.7 %collective-permute-done.4.refs_7_.refs_10_ = bf16[672,896]{1,0:T(8,128)(2,1)} collective-permute-done((bf16[672,896]{1,0:T(8,128)(2,1)}, bf16[672,896]{1,0:T(8,128)(2,1)}, u32[]{:S(2)}, u32[]{:S(2)}) %collective-permute-start.4) | collective-permute-done | bytes 1204256 | tf_op jit(solution)/shard_map/ppermute | solution.py:148
  158.4 3.0 slice_bitcast_fusion.5
  161.4 1.8 pad_maximum_fusion.1
  163.3 3.4 slice.37
  166.7 1.5 collective-permute-start.9
  168.2 1.9 collective-permute-start.6
  170.1 2.4 collective-permute-start.7
  172.5 1.6 collective-permute-start.8
  174.1 18.2 %shard_map.101.refs_0_ = bf16[1024,7168]{1,0:T(8,128)(2,1)} custom-call(s32[1]{0:T(128)} %constant.234.clone.1.first, bf16[1024,7168]{1,0:T(8,128)(2,1)} %inputs_ref.2, f32[1,7168]{1,0:T(1,128)S(1)} %bitcast.71), custom_call_target="tpu_custom_call" | custom-call | flops 1 | bytes 1 | tf_op jit(solution)/shard_map/pallas_call | solution.py:173
  192.2 3.9 copy.38
  196.1 18.2 %collective-permute-done.8 = bf16[2,448,512]{2,1,0:T(8,128)(2,1)} collective-permute-done((bf16[2,448,512]{2,1,0:T(8,128)(2,1)S(1)}, bf16[2,448,512]{2,1,0:T(8,128)(2,1)}, u32[]{:S(2)}, u32[]{:S(2)}) %collective-permute-start.8) | collective-permute-done | bytes 917536 | tf_op jit(solution)/shard_map/ppermute | solution.py:148
  214.3 27.8 %collective-permute-done.6.refs_6_.refs_9_ = bf16[672,896]{1,0:T(8,128)(2,1)S(1)} collective-permute-done((bf16[672,896]{1,0:T(8,128)(2,1)S(1)}, bf16[672,896]{1,0:T(8,128)(2,1)S(1)}, u32[]{:S(2)}, u32[]{:S(2)}) %collective-permute-start.6) | collective-permute-done | bytes 1204256 | tf_op jit(solution)/shard_map/ppermute | solution.py:148
  242.1 26.1 %collective-permute-done.7.refs_8_.refs_11_ = bf16[672,896]{1,0:T(8,128)(2,1)} collective-permute-done((bf16[672,896]{1,0:T(8,128)(2,1)}, bf16[672,896]{1,0:T(8,128)(2,1)}, u32[]{:S(2)}, u32[]{:S(2)}) %collective-permute-start.7) | collective-permute-done | bytes 1204256 | tf_op jit(solution)/shard_map/ppermute | solution.py:148
  268.4 3.0 constant_dynamic-slice_fusion.4
  271.4 1.5 collective-permute-start.14
  272.9 2.3 fusion.19
  275.2 5.6 collective-permute-start.10
  280.8 2.4 collective-permute-start.12
  283.2 2.2 copy.39
  285.4 2.0 copy.40
  287.8 1.6 dynamic-slice_bitcast_fusion.10.up_ref
  289.5 3.3 slice_bitcast_fusion
  292.7 22.0 %shard_map.102 = (bf16[4,448,256]{2,1,0:T(8,128)(2,1)}, bf16[4,256,224]{2,1,0:T(8,128)(2,1)}) custom-call(s32[8]{0:T(128)} %iota_xor_fusion.order, bf16[672,128]{1,0:T(8,128)(2,1)} %dynamic-slice_bitcast_fusion.10.up_ref, bf16[128,7168]{1,0:T(8,128)(2,1)} %bitcast.72, bf16[1024,7168]{1,0:T(8,128)(2,1)} %shard_map.101.refs_0_, bf16[672,896]{1,0:T(8,128)(2,1)} %copy-done.8, ...), custom_call_target="tpu_custom_call" | custom-call | flops 1 | bytes 1 | tf_op jit(solution)/shard_map/pallas_call | solution.py:239
  314.7 5.6 collective-permute-done.10.refs_1_
  320.3 23.9 %collective-permute-done.11.refs_2_ = bf16[2,448,512]{2,1,0:T(8,128)(2,1)S(1)} collective-permute-done((bf16[2,448,512]{2,1,0:T(8,128)(2,1)S(1)}, bf16[2,448,512]{2,1,0:T(8,128)(2,1)S(1)}, u32[]{:S(2)}, u32[]{:S(2)}) %collective-permute-start.11) | collective-permute-done | bytes 917536 | tf_op jit(solution)/shard_map/ppermute | solution.py:148
  344.3 9.4 %collective-permute-done.14 = bf16[128,7168]{1,0:T(8,128)(2,1)} collective-permute-done((bf16[128,7168]{1,0:T(8,128)(2,1)}, bf16[128,7168]{1,0:T(8,128)(2,1)}, u32[]{:S(2)}, u32[]{:S(2)}) %collective-permute-start.14) | collective-permute-done | bytes 1835040 | tf_op jit(solution)/shard_map/ppermute | solution.py:148
  353.7 19.9 %all-gather.6.cloned.1.call-done.refs_0_ = bf16[2048,7168]{1,0:T(8,128)(2,1)} async-done(((bf16[256,7168]{1,0:T(8,128)(2,1)}), bf16[2048,7168]{1,0:T(8,128)(2,1)}) %all-gather.6.cloned.1.call-update) | async-done | bytes 29360144 | tf_op jit(solution)/shard_map/all_gather | solution.py:418
  373.7 35.3 %shard_map.103 = (bf16[8,448,256]{2,1,0:T(8,128)(2,1)}, bf16[8,256,224]{2,1,0:T(8,128)(2,1)}) custom-call(s32[8]{0:T(128)} %iota_xor_fusion.order, bf16[672,128]{1,0:T(8,128)(2,1)} %dynamic-slice_bitcast_fusion.10.up_ref, bf16[128,7168]{1,0:T(8,128)(2,1)} %bitcast.73, bf16[2048,7168]{1,0:T(8,128)(2,1)} %all-gather.6.cloned.1.call-done.refs_0_, ...), custom_call_target="tpu_custom_call" | custom-call | flops 1 | bytes 1 | tf_op jit(solution)/shard_map/pallas_call | solution.py:239
  408.9 2.9 constant_dynamic-update-slice_fusion.1
  411.8 2.9 constant_dynamic-update-slice_fusion.refs_2_
  417.3 8.7 %shard_map.104 = bf16[224,1024]{1,0:T(8,128)(2,1)S(1)} custom-call(s32[8]{0:T(128)S(1)} %iota.25.chunk_table, s32[4]{0:T(128)S(1)} %get-tuple-element.146.cache_table, s32[1]{0:T(128)} %get-tuple-element.148.length_ref, bf16[8,448,256]{2,1,0:T(8,128)(2,1)} %get-tuple-element.109.turned_ref, bf16[8,256,224]{2,1,0:T(8,128)(2,1)S(1)} %copy-done.4, ...), custom_call_target="tpu_custom_call" | custom-call | flops 1 | bytes 1 | tf_op jit(solution)/shard_map/pallas_call | solution.py:343
  426.0 4.0 collective-permute-start.16
  431.1 2.2 constant_dynamic-update-slice_fusion.3
  433.3 25.5 %shard_map.105 = (bf16[4,448,256]{2,1,0:T(8,128)(2,1)}, bf16[4,256,224]{2,1,0:T(8,128)(2,1)}) custom-call(s32[8]{0:T(128)} %iota_xor_fusion.order, bf16[672,128]{1,0:T(8,128)(2,1)} %dynamic-slice_bitcast_fusion.10.up_ref, bf16[128,7168]{1,0:T(8,128)(2,1)} %bitcast.74, bf16[256,7168]{1,0:T(8,128)(2,1)} %collective-permute-done.1.refs_0_, ...), custom_call_target="tpu_custom_call" | custom-call | flops 1 | bytes 1 | tf_op jit(solution)/shard_map/pallas_call | solution.py:239
  458.8 8.8 %collective-permute-done.16 = bf16[224,1024]{1,0:T(8,128)(2,1)} collective-permute-done((bf16[224,1024]{1,0:T(8,128)(2,1)S(1)}, bf16[224,1024]{1,0:T(8,128)(2,1)}, u32[]{:S(2)}, u32[]{:S(2)}) %collective-permute-start.16) | collective-permute-done | bytes 458784 | tf_op jit(solution)/shard_map/ppermute | solution.py:148
  467.6 1.8 dynamic-slice_bitcast_fusion.8
  469.4 1.9 collective-permute-start.17
  472.4 1.6 constant_dynamic-update-slice_fusion.2.turned_ref
  475.3 10.8 %shard_map.106 = bf16[224,1024]{1,0:T(8,128)(2,1)S(1)} custom-call(s32[8]{0:T(128)S(1)} %compare_select_fusion.chunk_table, s32[4]{0:T(128)S(1)} %get-tuple-element.145.cache_table, s32[1]{0:T(128)} %get-tuple-element.147.length_ref, bf16[8,448,256]{2,1,0:T(8,128)(2,1)} %copy-done.11, bf16[8,256,224]{2,1,0:T(8,128)(2,1)S(1)} %constant_dynamic-update-slice_fusion.4.keys_ref, ...), custom_call_target="tpu_custom_call" | custom-call | flops 1 | bytes 1 | tf_op jit(solution)/shard_map/pallas_call | solution.py:343
  488.4 9.8 %shard_map.107 = bf16[224,1024]{1,0:T(8,128)(2,1)S(1)} custom-call(s32[8]{0:T(128)S(1)} %iota.28.chunk_table, s32[4]{0:T(128)S(1)} %get-tuple-element.146.cache_table, s32[1]{0:T(128)} %get-tuple-element.148.length_ref, bf16[8,448,256]{2,1,0:T(8,128)(2,1)} %get-tuple-element.109.turned_ref, bf16[8,256,224]{2,1,0:T(8,128)(2,1)S(1)} %copy-done.5, ...), custom_call_target="tpu_custom_call" | custom-call | flops 1 | bytes 1 | tf_op jit(solution)/shard_map/pallas_call | solution.py:343
  500.5 3.9 convolution_convert_fusion.3
  504.4 3.9 convolution_convert_fusion.2
  508.8 4.2 add_convert_fusion.3
  513.1 3.0 convert_add_fusion
  516.1 5.2 collective-permute-done.19
  521.3 1.5 collective-permute-start.24
  522.8 2.0 collective-permute-start.22
  524.8 12.4 %shard_map.108 = bf16[224,1024]{1,0:T(8,128)(2,1)S(1)} custom-call(s32[8]{0:T(128)S(1)} %compare_select_fusion.chunk_table, s32[4]{0:T(128)S(1)} %get-tuple-element.145.cache_table, s32[1]{0:T(128)} %get-tuple-element.147.length_ref, bf16[8,448,256]{2,1,0:T(8,128)(2,1)} %copy-done.11, bf16[8,256,224]{2,1,0:T(8,128)(2,1)S(1)} %copy-done.3, ...), custom_call_target="tpu_custom_call" | custom-call | flops 1 | bytes 1 | tf_op jit(solution)/shard_map/pallas_call | solution.py:343
  537.6 5.9 %collective-permute-done.23 = bf16[224,512]{1,0:T(8,128)(2,1)S(1)} collective-permute-done((bf16[224,512]{1,0:T(8,128)(2,1)S(1)}, bf16[224,512]{1,0:T(8,128)(2,1)S(1)}, u32[]{:S(2)}, u32[]{:S(2)}) %collective-permute-start.23) | collective-permute-done | bytes 229408 | tf_op jit(solution)/shard_map/ppermute | solution.py:148
  551.2 20.1 %collective-permute-done.27 = bf16[512,896]{1,0:T(8,128)(2,1)S(1)} collective-permute-done((bf16[512,896]{1,0:T(8,128)(2,1)S(1)}, bf16[512,896]{1,0:T(8,128)(2,1)S(1)}, u32[]{:S(2)}, u32[]{:S(2)}) %collective-permute-start.27) | collective-permute-done | bytes 917536 | tf_op jit(solution)/shard_map/ppermute | solution.py:148
  (124 shorter events, 24.0 us)
Async XLA Ops:
  6.5 10.8 %copy-start = (bf16[896,128]{1,0:T(8,128)(2,1)S(1)}, bf16[896,128]{1,0:T(8,128)(2,1)}, u32[]{:S(2)}) copy-start(bf16[896,128]{1,0:T(8,128)(2,1)} %param.13) | copy-start | bytes 688132
  6.5 151.4 %all-gather.4.cloned.1.call-start = ((), (), s32[]{:S(2)}) async-start(), calls=%async_computation | async-start | bytes 1892352 | tf_op jit(solution)/shard_map/all_gather | solution.py:406
  6.5 0.8 copy-start.6
  12.8 145.2 %collective-permute-start = (bf16[256,7168]{1,0:T(8,128)(2,1)}, bf16[256,7168]{1,0:T(8,128)(2,1)}, u32[]{:S(2)}, u32[]{:S(2)}) collective-permute-start(bf16[256,7168]{1,0:T(8,128)(2,1)} %shard_map.100), channel_id=1, source_target_pairs={{0,8},{8,0},{16,24},{24,16},{1,9},{9,1},{17,25},{25,17},{2,10},{10... | collective-permute-start | bytes 11010056 | tf_op jit(solution)/shard_map/ppermute | solution.py:148
  15.8 142.2 %collective-permute-start.1 = (bf16[256,7168]{1,0:T(8,128)(2,1)}, bf16[256,7168]{1,0:T(8,128)(2,1)}, u32[]{:S(2)}, u32[]{:S(2)}) collective-permute-start(bf16[256,7168]{1,0:T(8,128)(2,1)} %shard_map.100), channel_id=1, source_target_pairs={{0,4},{4,0},{1,5},{5,1},{2,6},{6,2},{3,7},{7,3},{8,12},{12,8},{9,1... | collective-permute-start | bytes 11010056 | tf_op jit(solution)/shard_map/ppermute | solution.py:148
  18.0 355.7 %all-gather.6.cloned.1.call-start = ((), (), s32[]{:S(2)}) async-start(), calls=%async_computation.1 | async-start | bytes 33030144 | tf_op jit(solution)/shard_map/all_gather | solution.py:418
  30.3 2.2 copy-start.8
  30.3 4.8 copy-start.17
  31.9 126.1 %collective-permute-start.2 = (bf16[2,672,896]{2,1,0:T(8,128)(2,1)}, bf16[2,672,896]{2,1,0:T(8,128)(2,1)}, u32[]{:S(2)}, u32[]{:S(2)}) collective-permute-start(bf16[2,672,896]{2,1,0:T(8,128)(2,1)} %pad_maximum_fusion), channel_id=1, source_target_pairs={{0,4},{4,0},{1,5},{5,1},{2,6},{6,2},{3,7},{7,3},{8,12},{12,8},{9,1... | collective-permute-start | bytes 7225352 | tf_op jit(solution)/shard_map/ppermute | solution.py:148
  32.5 97.8 %collective-permute-start.3 = (bf16[672,896]{1,0:T(8,128)(2,1)S(1)}, bf16[672,896]{1,0:T(8,128)(2,1)S(1)}, u32[]{:S(2)}, u32[]{:S(2)}) collective-permute-start(bf16[672,896]{1,0:T(8,128)(2,1)S(1)} %get-tuple-element.127.refs_1_.refs_4_), channel_id=1, source_target_pairs={{0,16},{8,24},{16,0},{24,8},{1,17},{9,25},{17,1},{25,9},{2,18},{10... | collective-permute-start | bytes 3612680 | tf_op jit(solution)/shard_map/ppermute | solution.py:148
  35.1 122.9 %collective-permute-start.4 = (bf16[672,896]{1,0:T(8,128)(2,1)}, bf16[672,896]{1,0:T(8,128)(2,1)}, u32[]{:S(2)}, u32[]{:S(2)}) collective-permute-start(bf16[672,896]{1,0:T(8,128)(2,1)} %get-tuple-element.126), channel_id=1, source_target_pairs={{0,24},{8,16},{16,8},{24,0},{1,25},{9,17},{17,9},{25,1},{2,26},{10... | collective-permute-start | bytes 3612680 | tf_op jit(solution)/shard_map/ppermute | solution.py:148
  130.3 27.7 %copy-start.12 = (bf16[672,896]{1,0:T(8,128)(2,1)}, bf16[672,896]{1,0:T(8,128)(2,1)S(1)}, u32[]{:S(2)}) copy-start(bf16[672,896]{1,0:T(8,128)(2,1)S(1)} %collective-permute-done.3.refs_5_.refs_8_) | copy-start | bytes 3612676
  158.0 342.5 %all-gather.8.cloned.1.call-start = ((), (), s32[]{:S(2)}) async-start(), calls=%async_computation.2 | async-start | bytes 7225344 | tf_op jit(solution)/shard_map/all_gather | solution.py:485
  158.4 3.0 copy-start.16
  161.4 6.8 %copy-start.9 = (bf16[672,896]{1,0:T(8,128)(2,1)}, bf16[672,896]{1,0:T(8,128)(2,1)S(1)}, u32[]{:S(2)}) copy-start(bf16[672,896]{1,0:T(8,128)(2,1)S(1)} %get-tuple-element.133.refs_2_.refs_5_) | copy-start | bytes 3612676
  163.2 9.2 %copy-start.14 = (bf16[4,448,512]{2,1,0:T(8,128)(2,1)S(1)}, bf16[4,448,512]{2,1,0:T(8,128)(2,1)}, u32[]{:S(2)}) copy-start(bf16[4,448,512]{2,1,0:T(8,128)(2,1)} %pad_maximum_fusion.2) | copy-start | bytes 5505028
  163.2 105.1 %collective-permute-start.5 = (bf16[2,672,896]{2,1,0:T(8,128)(2,1)}, bf16[2,672,896]{2,1,0:T(8,128)(2,1)}, u32[]{:S(2)}, u32[]{:S(2)}) collective-permute-start(bf16[2,672,896]{2,1,0:T(8,128)(2,1)} %pad_maximum_fusion.1), channel_id=1, source_target_pairs={{0,8},{8,0},{16,24},{24,16},{1,9},{9,1},{17,25},{25,17},{2,10},{10... | collective-permute-start | bytes 7225352 | tf_op jit(solution)/shard_map/ppermute | solution.py:148
  166.6 7.4 %copy-start.7 = (f32[7168]{0:T(1024)S(1)}, f32[7168]{0:T(1024)}, u32[]{:S(2)}) copy-start(f32[7168]{0:T(1024)} %param.11) | copy-start | bytes 86020
  166.7 101.5 %collective-permute-start.9 = (bf16[128,7168]{1,0:T(8,128)(2,1)}, bf16[128,7168]{1,0:T(8,128)(2,1)}, u32[]{:S(2)}, u32[]{:S(2)}) collective-permute-start(bf16[128,7168]{1,0:T(8,128)(2,1)} %slice.37), channel_id=1, source_target_pairs={{0,2},{2,0},{1,3},{3,1},{4,6},{6,4},{5,7},{7,5},{8,10},{10,8},{9,1... | collective-permute-start | bytes 5505032 | tf_op jit(solution)/shard_map/ppermute | solution.py:148
  168.2 73.9 %collective-permute-start.6 = (bf16[672,896]{1,0:T(8,128)(2,1)S(1)}, bf16[672,896]{1,0:T(8,128)(2,1)S(1)}, u32[]{:S(2)}, u32[]{:S(2)}) collective-permute-start(bf16[672,896]{1,0:T(8,128)(2,1)S(1)} %get-tuple-element.133.refs_2_.refs_5_), channel_id=1, source_target_pairs={{0,16},{8,24},{16,0},{24,8},{1,17},{9,25},{17,1},{25,9},{2,18},{10... | collective-permute-start | bytes 3612680 | tf_op jit(solution)/shard_map/ppermute | solution.py:148
  170.1 98.1 %collective-permute-start.7 = (bf16[672,896]{1,0:T(8,128)(2,1)}, bf16[672,896]{1,0:T(8,128)(2,1)}, u32[]{:S(2)}, u32[]{:S(2)}) collective-permute-start(bf16[672,896]{1,0:T(8,128)(2,1)} %get-tuple-element.132), channel_id=1, source_target_pairs={{0,24},{8,16},{16,8},{24,0},{1,25},{9,17},{17,9},{25,1},{2,26},{10... | collective-permute-start | bytes 3612680 | tf_op jit(solution)/shard_map/ppermute | solution.py:148
  172.5 41.8 %collective-permute-start.8 = (bf16[2,448,512]{2,1,0:T(8,128)(2,1)S(1)}, bf16[2,448,512]{2,1,0:T(8,128)(2,1)}, u32[]{:S(2)}, u32[]{:S(2)}) collective-permute-start(bf16[2,448,512]{2,1,0:T(8,128)(2,1)S(1)} %dynamic-slice_bitcast_fusion.5), channel_id=1, source_target_pairs={{0,4},{4,0},{1,5},{5,1},{2,6},{6,2},{3,7},{7,3},{8,12},{12,8},{9,1... | collective-permute-start | bytes 2752520 | tf_op jit(solution)/shard_map/ppermute | solution.py:148
  242.1 29.3 %copy-start.13 = (bf16[672,896]{1,0:T(8,128)(2,1)}, bf16[672,896]{1,0:T(8,128)(2,1)S(1)}, u32[]{:S(2)}) copy-start(bf16[672,896]{1,0:T(8,128)(2,1)S(1)} %collective-permute-done.6.refs_6_.refs_9_) | copy-start | bytes 3612676
  268.3 85.3 %collective-permute-start.13 = (bf16[256,7168]{1,0:T(8,128)(2,1)}, bf16[256,7168]{1,0:T(8,128)(2,1)}, u32[]{:S(2)}, u32[]{:S(2)}) collective-permute-start(bf16[256,7168]{1,0:T(8,128)(2,1)} %collective-permute-done.1.refs_0_), channel_id=1, source_target_pairs={{0,1},{1,0},{2,3},{3,2},{4,5},{5,4},{6,7},{7,6},{8,9},{9,8},{10,11... | collective-permute-start | bytes 11010056 | tf_op jit(solution)/shard_map/ppermute | solution.py:148
  268.3 4.5 copy-start.15
  271.4 82.3 %collective-permute-start.14 = (bf16[128,7168]{1,0:T(8,128)(2,1)}, bf16[128,7168]{1,0:T(8,128)(2,1)}, u32[]{:S(2)}, u32[]{:S(2)}) collective-permute-start(bf16[128,7168]{1,0:T(8,128)(2,1)} %constant_dynamic-slice_fusion.4), channel_id=1, source_target_pairs={{0,4},{4,0},{1,5},{5,1},{2,6},{6,2},{3,7},{7,3},{8,12},{12,8},{9,1... | collective-permute-start | bytes 5505032 | tf_op jit(solution)/shard_map/ppermute | solution.py:148
  275.2 45.1 %collective-permute-start.10 = (bf16[2,448,512]{2,1,0:T(8,128)(2,1)}, bf16[2,448,512]{2,1,0:T(8,128)(2,1)S(1)}, u32[]{:S(2)}, u32[]{:S(2)}) collective-permute-start(bf16[2,448,512]{2,1,0:T(8,128)(2,1)} %get-tuple-element.135), channel_id=1, source_target_pairs={{0,8},{8,0},{16,24},{24,16},{1,9},{9,1},{17,25},{25,17},{2,10},{10... | collective-permute-start | bytes 2752520 | tf_op jit(solution)/shard_map/ppermute | solution.py:148
  280.8 63.5 %collective-permute-start.11 = (bf16[2,448,512]{2,1,0:T(8,128)(2,1)S(1)}, bf16[2,448,512]{2,1,0:T(8,128)(2,1)S(1)}, u32[]{:S(2)}, u32[]{:S(2)}) collective-permute-start(bf16[2,448,512]{2,1,0:T(8,128)(2,1)S(1)} %get-tuple-element.87.refs_0_), channel_id=1, source_target_pairs={{0,16},{8,24},{16,0},{24,8},{1,17},{9,25},{17,1},{25,9},{2,18},{10... | collective-permute-start | bytes 2752520 | tf_op jit(solution)/shard_map/ppermute | solution.py:148
  280.8 63.5 %collective-permute-start.12 = (bf16[2,448,512]{2,1,0:T(8,128)(2,1)}, bf16[2,448,512]{2,1,0:T(8,128)(2,1)}, u32[]{:S(2)}, u32[]{:S(2)}) collective-permute-start(bf16[2,448,512]{2,1,0:T(8,128)(2,1)} %get-tuple-element.135), channel_id=1, source_target_pairs={{0,24},{8,16},{16,8},{24,0},{1,25},{9,17},{17,9},{25,1},{2,26},{10... | collective-permute-start | bytes 2752520 | tf_op jit(solution)/shard_map/ppermute | solution.py:148
  411.8 3.2 copy-start.24
  411.8 4.0 copy-start.23
  414.7 11.3 %collective-permute-start.15 = (bf16[256,7168]{1,0:T(8,128)(2,1)}, bf16[256,7168]{1,0:T(8,128)(2,1)}, u32[]{:S(2)}, u32[]{:S(2)}) collective-permute-start(bf16[256,7168]{1,0:T(8,128)(2,1)} %constant_dynamic-update-slice_fusion.refs_2_), channel_id=1, source_target_pairs={{0,1},{1,0},{2,3},{3,2},{4,5},{5,4},{6,7},{7,6},{8,9},{9,8},{10,11... | collective-permute-start | bytes 11010056 | tf_op jit(solution)/shard_map/ppermute | solution.py:148
  416.1 1.2 copy-start.4
  426.0 41.6 %collective-permute-start.16 = (bf16[224,1024]{1,0:T(8,128)(2,1)S(1)}, bf16[224,1024]{1,0:T(8,128)(2,1)}, u32[]{:S(2)}, u32[]{:S(2)}) collective-permute-start(bf16[224,1024]{1,0:T(8,128)(2,1)S(1)} %shard_map.104), channel_id=1, source_target_pairs={{0,8},{8,0},{16,24},{24,16},{1,9},{9,1},{17,25},{25,17},{2,10},{10... | collective-permute-start | bytes 1376264 | tf_op jit(solution)/shard_map/ppermute | solution.py:148
  458.8 13.6 %copy-start.10 = (bf16[8,448,256]{2,1,0:T(8,128)(2,1)S(1)}, bf16[8,448,256]{2,1,0:T(8,128)(2,1)}, u32[]{:S(2)}) copy-start(bf16[8,448,256]{2,1,0:T(8,128)(2,1)} %constant_dynamic-update-slice_fusion.3) | copy-start | bytes 5505028
  469.4 16.8 %collective-permute-start.17 = (bf16[224,512]{1,0:T(8,128)(2,1)S(1)}, bf16[224,512]{1,0:T(8,128)(2,1)S(1)}, u32[]{:S(2)}, u32[]{:S(2)}) collective-permute-start(bf16[224,512]{1,0:T(8,128)(2,1)S(1)} %get-tuple-element.144), channel_id=1, source_target_pairs={{0,4},{4,0},{1,5},{5,1},{2,6},{6,2},{3,7},{7,3},{8,12},{12,8},{9,1... | collective-permute-start | bytes 688136 | tf_op jit(solution)/shard_map/ppermute | solution.py:148
  472.4 13.7 %copy-start.2 = (bf16[8,256,224]{2,1,0:T(8,128)(2,1)}, bf16[8,256,224]{2,1,0:T(8,128)(2,1)S(1)}, u32[]{:S(2)}) copy-start(bf16[8,256,224]{2,1,0:T(8,128)(2,1)S(1)} %constant_dynamic-update-slice_fusion.4.keys_ref) | copy-start | bytes 2752516
  474.0 1.2 copy-start.11
  486.2 0.9 copy-start.21
  487.0 11.3 %collective-permute-start.18 = (bf16[224,512]{1,0:T(8,128)(2,1)}, bf16[224,512]{1,0:T(8,128)(2,1)}, u32[]{:S(2)}, u32[]{:S(2)}) collective-permute-start(bf16[224,512]{1,0:T(8,128)(2,1)} %get-tuple-element.142), channel_id=1, source_target_pairs={{0,4},{4,0},{1,5},{5,1},{2,6},{6,2},{3,7},{7,3},{8,12},{12,8},{9,1... | collective-permute-start | bytes 688136 | tf_op jit(solution)/shard_map/ppermute | solution.py:148
  487.1 1.2 copy-start.5
  488.4 9.8 %copy-start.19 = (bf16[1,224,512]{2,1,0:T(8,128)(2,1)S(1)}, bf16[1,224,512]{2,1,0:T(8,128)(2,1)}, u32[]{:S(2)}) copy-start(bf16[1,224,512]{2,1,0:T(8,128)(2,1)} %get-tuple-element.143) | copy-start | bytes 688132
  488.4 9.8 %copy-start.22 = (bf16[224,512]{1,0:T(8,128)(2,1)S(1)}, bf16[224,512]{1,0:T(8,128)(2,1)}, u32[]{:S(2)}) copy-start(bf16[224,512]{1,0:T(8,128)(2,1)} %copy-done.21) | copy-start | bytes 688132
  488.4 9.9 %copy-start.20 = (bf16[1,224,512]{2,1,0:T(8,128)(2,1)S(1)}, bf16[1,224,512]{2,1,0:T(8,128)(2,1)}, u32[]{:S(2)}) copy-start(bf16[1,224,512]{2,1,0:T(8,128)(2,1)} %get-tuple-element.141) | copy-start | bytes 688132
  504.4 4.4 collective-permute-start.20
  508.3 4.7 collective-permute-start.21
  508.8 4.2 copy-start.18
  508.8 12.4 %collective-permute-start.19 = (bf16[224,1024]{1,0:T(8,128)(2,1)S(1)}, bf16[224,1024]{1,0:T(8,128)(2,1)S(1)}, u32[]{:S(2)}, u32[]{:S(2)}) collective-permute-start(bf16[224,1024]{1,0:T(8,128)(2,1)S(1)} %shard_map.107), channel_id=1, source_target_pairs={{0,8},{8,0},{16,24},{24,16},{1,9},{9,1},{17,25},{25,17},{2,10},{10... | collective-permute-start | bytes 1376264 | tf_op jit(solution)/shard_map/ppermute | solution.py:148
  513.0 11.7 %copy-start.3 = (bf16[8,256,224]{2,1,0:T(8,128)(2,1)S(1)}, bf16[8,256,224]{2,1,0:T(8,128)(2,1)}, u32[]{:S(2)}) copy-start(bf16[8,256,224]{2,1,0:T(8,128)(2,1)} %copy-done.2) | copy-start | bytes 2752516
  521.3 22.2 %collective-permute-start.24 = (bf16[512,896]{1,0:T(8,128)(2,1)}, bf16[512,896]{1,0:T(8,128)(2,1)S(1)}, u32[]{:S(2)}, u32[]{:S(2)}) collective-permute-start(bf16[512,896]{1,0:T(8,128)(2,1)} %add_convert_fusion.3), channel_id=1, source_target_pairs={{0,2},{2,0},{1,3},{3,1},{4,6},{6,4},{5,7},{7,5},{8,10},{10,8},{9,1... | collective-permute-start | bytes 2752520 | tf_op jit(solution)/shard_map/ppermute | solution.py:148
  522.7 21.0 %slice-start = ((s8[6422528]{0:T(1024)(128)(4,1)}), s8[4194304]{0:T(1024)(128)(4,1)S(1)}, s32[]{:S(2)}) async-start(s8[6422528]{0:T(1024)(128)(4,1)} %bitcast.95), calls=%async_computation.3 | async-start | bytes 8388608
  522.8 21.0 %slice-start.1 = ((s8[6422528]{0:T(1024)(128)(4,1)}), s8[2228224]{0:T(1024)(128)(4,1)S(1)}, s32[]{:S(2)}) async-start(s8[6422528]{0:T(1024)(128)(4,1)} %bitcast.95), calls=%async_computation.4 | async-start | bytes 4456448
  522.8 14.4 %collective-permute-start.22 = (bf16[224,512]{1,0:T(8,128)(2,1)S(1)}, bf16[224,512]{1,0:T(8,128)(2,1)S(1)}, u32[]{:S(2)}, u32[]{:S(2)}) collective-permute-start(bf16[224,512]{1,0:T(8,128)(2,1)S(1)} %get-tuple-element.140), channel_id=1, source_target_pairs={{0,4},{4,0},{1,5},{5,1},{2,6},{6,2},{3,7},{7,3},{8,12},{12,8},{9,1... | collective-permute-start | bytes 688136 | tf_op jit(solution)/shard_map/ppermute | solution.py:148
  537.2 6.3 %collective-permute-start.23 = (bf16[224,512]{1,0:T(8,128)(2,1)S(1)}, bf16[224,512]{1,0:T(8,128)(2,1)S(1)}, u32[]{:S(2)}, u32[]{:S(2)}) collective-permute-start(bf16[224,512]{1,0:T(8,128)(2,1)S(1)} %get-tuple-element.138), channel_id=1, source_target_pairs={{0,4},{4,0},{1,5},{5,1},{2,6},{6,2},{3,7},{7,3},{8,12},{12,8},{9,1... | collective-permute-start | bytes 688136 | tf_op jit(solution)/shard_map/ppermute | solution.py:148
  545.0 2.5 collective-permute-start.26
  546.4 4.8 collective-permute-start.25
  548.8 22.5 %collective-permute-start.27 = (bf16[512,896]{1,0:T(8,128)(2,1)S(1)}, bf16[512,896]{1,0:T(8,128)(2,1)S(1)}, u32[]{:S(2)}, u32[]{:S(2)}) collective-permute-start(bf16[512,896]{1,0:T(8,128)(2,1)S(1)} %add_convert_fusion.1), channel_id=1, source_target_pairs={{0,2},{2,0},{1,3},{3,1},{4,6},{6,4},{5,7},{7,5},{8,10},{10,8},{9,1... | collective-permute-start | bytes 2752520 | tf_op jit(solution)/shard_map/ppermute | solution.py:148
  571.3 1.7 copy-start.1
Sparse Core Ops, SparseCore 0:
  18.1 83.1 all-gather.3
  158.1 215.4 all-gather.5
  375.8 106.8 all-gather.7

commit v3 on v2

--- a/solution.py
+++ b/solution.py
@@ -283,6 +283,12 @@
     def gather_cache():
         for number in range(cache_table.shape[0]):
             entry = cache_table[number]
+
+            @pl.when(number * CHUNK >= length)
+            def clear(number=number):
+                place = pl.ds(number * CHUNK, CHUNK)
+                cached_values[:, place] = jnp.zeros((HD, CHUNK), jnp.bfloat16)
+
             for bit, block_ref in enumerate(block_refs):
 
                 @pl.when((number * CHUNK < length) & (entry // 4 == bit))
@@ -322,9 +328,8 @@
         return step(state, keys, joined(turned_ref, first, value_rows), visible)
 
     def cache_step(number, state):
-        place = pl.ds(pl.multiple_of(number * CHUNK, CHUNK), CHUNK)
-        row = lax.broadcasted_iota(jnp.int32, (CHUNK, width), 0)
-        visible = row + number * CHUNK < length
+        place = pl.ds(pl.multiple_of(number * width, width), width)
+        visible = key_row + number * width < length
         return step(state, cached_keys[place, :], cached_values[:, place], visible)
 
     total_ref[...] = jnp.zeros_like(total_ref)
@@ -333,7 +338,7 @@
     query_column = lax.broadcasted_iota(jnp.int32, (width, width), 1)
     state = new_step(tile, state, key_row <= query_column)
     state = lax.fori_loop(0, tile, new_step, state)
-    state = lax.fori_loop(0, pl.cdiv(length, CHUNK), cache_step, state)
+    state = lax.fori_loop(0, pl.cdiv(length, width), cache_step, state)
     out_ref[...] = (total_ref[...] / state[1]).astype(jnp.bfloat16)
 
 
@@ -412,29 +417,61 @@
     cached = jnp.concatenate([turned_cache(cache_keys), turned_cache(cache_values)], axis=1)
     cached = cached.reshape(2, 2, 2 * HD, cached.shape[2])
 
-    part_z, part_x, from_x, far[2][0], far[3][0], kept_near, cached, down, inputs = fence(
-        part_z, part_x, from_x, far[2][0], far[3][0], kept_near, cached, down, inputs
+    near_rows = jnp.stack([kept_near, from_x[1]])
+    same_rows, other_rows = from_x[0], from_x[1]
+    cache_own, cache_given = pick(cached, side, 1), pick(cached, 1 - side, 1)
+    (
+        part_z,
+        part_x,
+        near_rows,
+        same_rows,
+        other_rows,
+        far[2][0],
+        far[3][0],
+        cache_own,
+        cache_given,
+        down,
+        inputs,
+    ) = fence(
+        part_z,
+        part_x,
+        near_rows,
+        same_rows,
+        other_rows,
+        far[2][0],
+        far[3][0],
+        cache_own,
+        cache_given,
+        down,
+        inputs,
     )
     pair_tokens = lax.all_gather(part_z, plane_axes, axis=0, tiled=True)
-    near = over_z(jnp.stack([kept_near, from_x[1]]), 1)
-    for bit in (2, 3):
-        far[bit].append(over_z(from_x[bit & 1], bit))
-    cache_from_x = over_x(pick(cached, 1 - side, 1))
-    part_y = over_y(part_x[:GROUP])
+    near = over_z(near_rows, 1)
+    far[2].append(over_z(same_rows, 2))
+    far[3].append(over_z(other_rows, 3))
+    cache_from_x = over_x(cache_given)
+    core_x = over_core(part_x)
     normed = normalise(inputs, norm_gain, jnp.int32(0), tok_dev)
     down = down.T
 
-    near, far[2][1], far[3][1], cache_from_x, part_y, normed, part_x, down, cached = fence(
-        near, far[2][1], far[3][1], cache_from_x, part_y, normed, part_x, down, cached
-    )
-    cache_both = jnp.stack([pick(cached, side, 1), cache_from_x], axis=1)
-    cache_blocks = [pick(cache_both, role)]
-    for bit in (1, 2, 3):
-        cache_blocks.append(over_z(pick(cache_both, role ^ (bit & 1)), bit))
-    core_x = over_core(part_x)
     start = (mp ^ 2) * CHUNK + GROUP
-    part_yx = over_x(lax.dynamic_slice_in_dim(normed, start, GROUP, 0))
-    weight_blocks = [pick(kept, role), from_x[0], near[0], near[1], *far[2], *far[3]]
+    given_x = lax.dynamic_slice_in_dim(normed, start, GROUP, 0)
+    given_y = part_x[:GROUP]
+    cache_both = jnp.stack([cache_own, cache_from_x], axis=1)
+    cache_same, cache_other = pick(cache_both, role), pick(cache_both, 1 - role)
+    near, far[2][1], far[3][1], cache_same, cache_other, core_x, normed, part_x = fence(
+        near, far[2][1], far[3][1], cache_same, cache_other, core_x, normed, part_x
+    )
+    given_x, given_y, down, part_x = fence(given_x, given_y, down, part_x)
+    cache_blocks = [
+        cache_same,
+        over_z(cache_other, 1),
+        over_z(cache_same, 2),
+        over_z(cache_other, 3),
+    ]
+    part_y = over_y(given_y)
+    part_yx = over_x(given_x)
+    weight_blocks = [pick(kept, role), same_rows, near[0], near[1], *far[2], *far[3]]
     order = jnp.arange(8, dtype=jnp.int32) ^ seq
     up = adapter_up.reshape(3, RANK, 4, HD).transpose(2, 0, 3, 1).reshape(4, 3 * HD, RANK)
     up = pick(up, 2 * role + side)
@@ -468,19 +505,16 @@
         jnp.where(place // 4 == side, place % 4, 4 + moved),
         place,
     )
-    local_projected = project((normed,), up, down, weight_blocks, order)
-
-    *cache_blocks, up, local_turned, local_keys, out_weight, core_x, part_y, part_yx = fence(
-        *cache_blocks, up, *local_projected, out_weight, core_x, part_y, part_yx
-    )
+    local_projected = project((normed, part_x, core_x), up, down, weight_blocks, order)
+
+    *cache_blocks, up, local_turned, local_keys, out_weight, part_y, part_yx = fence(
+        *cache_blocks, up, *local_projected, out_weight, part_y, part_yx
+    )
+    part_y = jnp.concatenate([part_y, part_yx])
+    core_y = over_core(part_y)
     pair_projected = project((pair_tokens,), up, down, weight_blocks, order)
     pair_first = attend(1, 0, pair_projected)
-    part_y, part_yx = fence(part_y, part_yx, pair_projected[0])[:2]
-    part_y = jnp.concatenate([part_y, part_yx])
-    core_y = over_core(part_y)
-    pair_first, core_y, part_y, up, pair_turned = fence(
-        pair_first, core_y, part_y, up, pair_projected[0]
-    )
+    pair_first, pair_turned, core_y, up = fence(pair_first, pair_projected[0], core_y, up)
 
     out_rows = lax.all_gather(out_weight, ("z", "x"), axis=1, tiled=True)
     out_cols = out_rows.shape[1] // 4
@@ -502,6 +536,12 @@
         return lax.dot_general(
             heads, columns[name], (((0,), (0,)), ((), ())), preferred_element_type=jnp.float32
         )
+
+    def summed(heads):
+        away = over_core(rounded(out_part(heads, "away_core")))
+        here = over_core(rounded(out_part(heads, "here_core")))
+        away = rounded(out_part(heads, "away") + away.astype(jnp.float32))
+        return away, out_part(heads, "here") + here.astype(jnp.float32)
 
     def crossing(attended):
         return lax.dynamic_slice_in_dim(attended, (1 - side) * half_dev, half_dev, 1)
@@ -518,23 +558,15 @@
             jnp.concatenate([pair_heads, own_heads]),
         ).reshape(4 * HD, half_dev)
 
-    def summed(heads):
-        away = over_core(rounded(out_part(heads, "away_core")))
-        here = over_core(rounded(out_part(heads, "here_core")))
-        away = rounded(out_part(heads, "away") + away.astype(jnp.float32))
-        return away, out_part(heads, "here") + here.astype(jnp.float32)
-
     pair_first = over_z(pair_first, 1)
-    parts_projected = project((part_x, core_x, part_y, core_y), up, down, weight_blocks, order)
-    pair_first, parts_turned, parts_keys = fence(pair_first, *parts_projected)
+    parts_turned, parts_keys = project((part_y, core_y), up, down, weight_blocks, order)
+    own_keys = jnp.concatenate([local_keys, parts_keys])
+    own_turned = jnp.concatenate([local_turned, parts_turned])
+    pair_first, own_turned, own_keys = fence(pair_first, own_turned, own_keys)
     pair_first_crossed = over_x(crossing(pair_first))
-    own_projected = (
-        jnp.concatenate([local_turned, parts_turned]),
-        jnp.concatenate([local_keys, parts_keys]),
-    )
-    own_first = attend(0, 0, own_projected)
+    own_first = attend(0, 0, (own_turned, own_keys))
     pair_first_crossed, own_first, pair_turned, own_turned = fence(
-        pair_first_crossed, own_first, pair_turned, own_projected[0]
+        pair_first_crossed, own_first, pair_turned, own_turned
     )
     own_first_crossed = over_x(crossing(own_first))
     pair_second = attend(1, 1, (pair_turned, pair_projected[1]))
@@ -548,7 +580,7 @@
     )
     first_received = over_y(first_sent)
     pair_second_crossed = over_x(crossing(pair_second))
-    own_second = attend(0, 1, (own_turned, own_projected[1]))
+    own_second = attend(0, 1, (own_turned, own_keys))
     pair_second_crossed, own_second = fence(pair_second_crossed, own_second)
     own_second_crossed = over_x(crossing(own_second))
     own_second_crossed, first_received = fence(own_second_crossed, first_received)

time: 587 us -> 556 us (0.947)
  waiting for transfers between devices: 282 us -> 262 us
    all_gather x1, waiting for transfers between devices: 19.9 us -> 0.02 us  [per_device_paired(): pair_tokens = lax.all_gather(part_z, plane_axes, axis=0, tiled=True)]
    unnamed x59 -> x55, local copies, waits for them, and re-layouts: 20.4 us -> 16.5 us
  transfers between devices with their start and end apart: 31 -> 31, of which waited for: 15 -> 13; matrix products, arithmetic and copies ran while one was open for 15% -> 15% of each run, Pallas kernels for 25% -> 26%
where the time goes in v3:
time: 556 us; the launch traced here: 549 us
  waiting for transfers between devices  262 us (47%)
  Pallas kernels  146 us (26%)
  local copies, waits for them, and re-layouts  59.6 us (11%)
  starting transfers between devices  33.2 us (6%)
  matrix products  20 us (4%)
  other arithmetic  15.2 us (3%)
  between operations  13.8 us (2%)
    ppermute x28, waiting for transfers between devices, swap(): return lax.ppermute(array, axis, [(i, i ^ bit) for i in range(size)])  262 us
    pallas_call x3, Pallas kernels, project(): pl.pallas_call(functools.partial(project_kernel, tuple(sets)), grid_spec=...  83.6 us
    pallas_call x4, Pallas kernels, attention(): pl.pallas_call(functools.partial(attention_kernel, half), grid_spec=pltpu...  37.4 us
    ppermute x28, starting transfers between devices, swap(): return lax.ppermute(array, axis, [(i, i ^ bit) for i in range(size)])  32.9 us
    pallas_call x2, Pallas kernels, normalise(): pl.pallas_call(norm_kernel, grid_spec=pltpu.PrefetchScalarGridSpec(num_sc...  24.9 us
    dot_general x8, matrix products, out_part(): lax.dot_general(heads, columns[name], (((0,), (0,)), ((), ())), preferred...  20 us
    unnamed x55, local copies, waits for them, and re-layouts  16.5 us
  transfers between devices with their start and end apart: 31, of which 13 were waited for; matrix products, arithmetic and copies ran while one was open for 15% of the time, Pallas kernels for 26%

profile of v3, /device:TPU:0, one launch (start us, length us, event | category | flops | bytes accessed | tf_op | source)
XLA Modules:
  0.0 549.3 jit_solution(17225493037656142849)
XLA Ops:
  7.3 5.4 shard_map.100
  12.7 3.0 collective-permute-start
  15.8 1.5 collective-permute-start.1
  18.0 7.6 %copy.35 = bf16[896,3,896]{0,2,1:T(8,128)(2,1)} copy(bf16[896,3,896]{2,0,1:T(8,128)(2,1)} %param.12) | data formatting | bytes 9633792 | tf_op args[2]
  25.6 5.0 copy.36
  30.6 4.6 dynamic-slice_bitcast_fusion
  35.2 1.7 pad_maximum_fusion
  37.4 2.6 collective-permute-start.3
  41.6 3.0 reshape.94
  44.6 1.5 copy.42
  46.1 1.3 pad_maximum_fusion.2
  48.5 105.3 %collective-permute-done.2 = bf16[2,672,896]{2,1,0:T(8,128)(2,1)} collective-permute-done((bf16[2,672,896]{2,1,0:T(8,128)(2,1)}, bf16[2,672,896]{2,1,0:T(8,128)(2,1)}, u32[]{:S(2)}, u32[]{:S(2)}) %collective-permute-start.2) | collective-permute-done | bytes 2408480 | tf_op jit(solution)/shard_map/ppermute | solution.py:148
  153.8 3.0 slice_bitcast_fusion.5
  156.8 1.9 pad_maximum_fusion.1
  159.4 2.8 collective-permute-start.6
  162.2 1.3 collective-permute-start.7
  163.5 1.5 collective-permute-start.8
  165.0 19.5 %shard_map.101.refs_0_ = bf16[1024,7168]{1,0:T(8,128)(2,1)} custom-call(s32[1]{0:T(128)} %constant.230.clone.1.first, bf16[1024,7168]{1,0:T(8,128)(2,1)} %inputs_ref.2, f32[1,7168]{1,0:T(1,128)S(1)} %bitcast.73), custom_call_target="tpu_custom_call" | custom-call | flops 1 | bytes 1 | tf_op jit(solution)/shard_map/pallas_call | solution.py:173
  184.5 2.9 slice.36
  187.4 3.9 copy.41
  191.3 2.9 constant_dynamic-slice_fusion.4
  194.2 5.4 collective-permute-done.8
  199.6 2.3 fusion.19
  201.8 36.3 %collective-permute-done.6.refs_8_.refs_6_.refs_7_ = bf16[672,896]{1,0:T(8,128)(2,1)} collective-permute-done((bf16[672,896]{1,0:T(8,128)(2,1)S(1)}, bf16[672,896]{1,0:T(8,128)(2,1)}, u32[]{:S(2)}, u32[]{:S(2)}) %collective-permute-start.6) | collective-permute-done | bytes 1204256 | tf_op jit(solution)/shard_map/ppermute | solution.py:148
  238.1 29.6 %collective-permute-done.7.refs_10_.refs_8_.refs_9_ = bf16[672,896]{1,0:T(8,128)(2,1)} collective-permute-done((bf16[672,896]{1,0:T(8,128)(2,1)S(1)}, bf16[672,896]{1,0:T(8,128)(2,1)}, u32[]{:S(2)}, u32[]{:S(2)}) %collective-permute-start.7) | collective-permute-done | bytes 1204256 | tf_op jit(solution)/shard_map/ppermute | solution.py:148
  267.8 1.5 collective-permute-start.13
  269.3 1.5 collective-permute-start.14
  270.8 1.6 collective-permute-start.11
  272.4 2.8 collective-permute-start.12
  275.2 2.2 copy.39
  277.4 2.0 copy.40
  279.9 1.6 dynamic-slice_bitcast_fusion.11.up_ref
  281.5 3.3 slice_bitcast_fusion.1
  284.8 31.5 %shard_map.102 = (bf16[6,448,256]{2,1,0:T(8,128)(2,1)}, bf16[6,256,224]{2,1,0:T(8,128)(2,1)}) custom-call(s32[8]{0:T(128)} %iota_xor_fusion.order, bf16[672,128]{1,0:T(8,128)(2,1)} %dynamic-slice_bitcast_fusion.11.up_ref, bf16[128,7168]{1,0:T(8,128)(2,1)} %bitcast.74, bf16[1024,7168]{1,0:T(8,128)(2,1)} %shard_map.101.refs_0_, ...), custom_call_target="tpu_custom_call" | custom-call | flops 1 | bytes 1 | tf_op jit(solution)/shard_map/pallas_call | solution.py:239
  316.2 18.0 %collective-permute-done.11.refs_2_ = bf16[2,448,512]{2,1,0:T(8,128)(2,1)S(1)} collective-permute-done((bf16[2,448,512]{2,1,0:T(8,128)(2,1)S(1)}, bf16[2,448,512]{2,1,0:T(8,128)(2,1)S(1)}, u32[]{:S(2)}, u32[]{:S(2)}) %collective-permute-start.11) | collective-permute-done | bytes 917536 | tf_op jit(solution)/shard_map/ppermute | solution.py:148
  334.3 15.5 %collective-permute-done.13 = bf16[128,7168]{1,0:T(8,128)(2,1)} collective-permute-done((bf16[128,7168]{1,0:T(8,128)(2,1)}, bf16[128,7168]{1,0:T(8,128)(2,1)}, u32[]{:S(2)}, u32[]{:S(2)}) %collective-permute-start.13) | collective-permute-done | bytes 1835040 | tf_op jit(solution)/shard_map/ppermute | solution.py:148
  350.6 3.2 constant_dynamic-update-slice_fusion.1
  353.8 2.9 constant_dynamic-update-slice_fusion.refs_0_
  357.9 35.6 %shard_map.103 = (bf16[8,448,256]{2,1,0:T(8,128)(2,1)}, bf16[8,256,224]{2,1,0:T(8,128)(2,1)}) custom-call(s32[8]{0:T(128)} %iota_xor_fusion.order, bf16[672,128]{1,0:T(8,128)(2,1)} %dynamic-slice_bitcast_fusion.11.up_ref, bf16[128,7168]{1,0:T(8,128)(2,1)} %bitcast.75, bf16[2048,7168]{1,0:T(8,128)(2,1)} %all-gather.6.cloned.1.call-done.refs_0_, ...), custom_call_target="tpu_custom_call" | custom-call | flops 1 | bytes 1 | tf_op jit(solution)/shard_map/pallas_call | solution.py:239
  394.7 7.6 %shard_map.104 = bf16[224,1024]{1,0:T(8,128)(2,1)S(1)} custom-call(s32[8]{0:T(128)S(1)} %iota.25.chunk_table, s32[4]{0:T(128)S(1)} %get-tuple-element.150.cache_table, s32[1]{0:T(128)} %get-tuple-element.152.length_ref, bf16[8,448,256]{2,1,0:T(8,128)(2,1)} %get-tuple-element.111.turned_ref, bf16[8,256,224]{2,1,0:T(8,128)(2,1)S(1)} %copy-done.4, ...), custom_call_target="tpu_custom_call" | custom-call | flops 1 | bytes 1 | tf_op jit(solution)/shard_map/pallas_call | solution.py:348
  402.4 3.9 collective-permute-start.16
  406.2 16.5 %shard_map.105 = (bf16[2,448,256]{2,1,0:T(8,128)(2,1)}, bf16[2,256,224]{2,1,0:T(8,128)(2,1)}) custom-call(s32[8]{0:T(128)} %iota_xor_fusion.order, bf16[672,128]{1,0:T(8,128)(2,1)} %dynamic-slice_bitcast_fusion.11.up_ref, bf16[128,7168]{1,0:T(8,128)(2,1)} %bitcast.76, bf16[256,7168]{1,0:T(8,128)(2,1)} %constant_dynamic-update-slice_fusion.refs_0_, ...), custom_call_target="tpu_custom_call" | custom-call | flops 1 | bytes 1 | tf_op jit(solution)/shard_map/pallas_call | solution.py:239
  422.8 1.3 pad_maximum_fusion.5.keys_ref
  424.2 1.4 pad_maximum_fusion.3.turned_ref
  425.6 18.1 %collective-permute-done.16 = bf16[224,1024]{1,0:T(8,128)(2,1)} collective-permute-done((bf16[224,1024]{1,0:T(8,128)(2,1)S(1)}, bf16[224,1024]{1,0:T(8,128)(2,1)}, u32[]{:S(2)}, u32[]{:S(2)}) %collective-permute-start.16) | collective-permute-done | bytes 458784 | tf_op jit(solution)/shard_map/ppermute | solution.py:148
  443.7 1.8 dynamic-slice_bitcast_fusion.9
  445.5 1.7 collective-permute-start.17
  447.2 9.3 %shard_map.106 = bf16[224,1024]{1,0:T(8,128)(2,1)S(1)} custom-call(s32[8]{0:T(128)S(1)} %compare_select_fusion.chunk_table, s32[4]{0:T(128)S(1)} %get-tuple-element.149.cache_table, s32[1]{0:T(128)} %get-tuple-element.151.length_ref, bf16[8,448,256]{2,1,0:T(8,128)(2,1)} %pad_maximum_fusion.3.turned_ref, bf16[8,256,224]{2,1,0:T(8,128)(2,1)S(1)} %pad_maximum_fusion.5.keys_ref, ...), custom_call_target="tpu_custom_call" | custom-call | flops 1 | bytes 1 | tf_op jit(solution)/shard_map/pallas_call | solution.py:348
  457.7 1.2 copy-done.5
  459.0 9.4 %shard_map.107 = bf16[224,1024]{1,0:T(8,128)(2,1)S(1)} custom-call(s32[8]{0:T(128)S(1)} %iota.28.chunk_table, s32[4]{0:T(128)S(1)} %get-tuple-element.150.cache_table, s32[1]{0:T(128)} %get-tuple-element.152.length_ref, bf16[8,448,256]{2,1,0:T(8,128)(2,1)} %get-tuple-element.111.turned_ref, bf16[8,256,224]{2,1,0:T(8,128)(2,1)S(1)} %copy-done.5, ...), custom_call_target="tpu_custom_call" | custom-call | flops 1 | bytes 1 | tf_op jit(solution)/shard_map/pallas_call | solution.py:348
  470.7 3.9 convolution_convert_fusion.3
  474.6 3.9 convolution_convert_fusion.2
  479.0 4.2 add_convert_fusion.3
  483.2 3.0 convert_add_fusion
  486.2 5.2 collective-permute-done.19
  492.6 1.9 collective-permute-start.22
  494.5 11.0 %shard_map.108 = bf16[224,1024]{1,0:T(8,128)(2,1)S(1)} custom-call(s32[8]{0:T(128)S(1)} %compare_select_fusion.chunk_table, s32[4]{0:T(128)S(1)} %get-tuple-element.149.cache_table, s32[1]{0:T(128)} %get-tuple-element.151.length_ref, bf16[8,448,256]{2,1,0:T(8,128)(2,1)} %pad_maximum_fusion.3.turned_ref, bf16[8,256,224]{2,1,0:T(8,128)(2,1)S(1)} %copy-done.3, ...), custom_call_target="tpu_custom_call" | custom-call | flops 1 | bytes 1 | tf_op jit(solution)/shard_map/pallas_call | solution.py:348
  506.3 5.7 %collective-permute-done.23 = bf16[224,512]{1,0:T(8,128)(2,1)S(1)} collective-permute-done((bf16[224,512]{1,0:T(8,128)(2,1)S(1)}, bf16[224,512]{1,0:T(8,128)(2,1)S(1)}, u32[]{:S(2)}, u32[]{:S(2)}) %collective-permute-start.23) | collective-permute-done | bytes 229408 | tf_op jit(solution)/shard_map/ppermute | solution.py:148
  513.3 1.2 convolution_convert_fusion
  514.6 1.3 convolution_convert_fusion.1
  517.1 1.3 add_convert_fusion.1
  519.5 1.2 fusion.2
  521.0 19.8 %collective-permute-done.27 = bf16[512,896]{1,0:T(8,128)(2,1)S(1)} collective-permute-done((bf16[512,896]{1,0:T(8,128)(2,1)S(1)}, bf16[512,896]{1,0:T(8,128)(2,1)S(1)}, u32[]{:S(2)}, u32[]{:S(2)}) %collective-permute-start.27) | collective-permute-done | bytes 917536 | tf_op jit(solution)/shard_map/ppermute | solution.py:148
  541.1 1.4 pad_maximum_fusion.4
  (119 shorter events, 19.5 us)
Async XLA Ops:
  6.5 10.7 %copy-start = (bf16[896,128]{1,0:T(8,128)(2,1)S(1)}, bf16[896,128]{1,0:T(8,128)(2,1)}, u32[]{:S(2)}) copy-start(bf16[896,128]{1,0:T(8,128)(2,1)} %param.13) | copy-start | bytes 688132
  6.5 152.1 %all-gather.4.cloned.1.call-start = ((), (), s32[]{:S(2)}) async-start(), calls=%async_computation | async-start | bytes 1892352 | tf_op jit(solution)/shard_map/all_gather | solution.py:411
  6.5 0.8 copy-start.6
  12.7 145.9 %collective-permute-start = (bf16[256,7168]{1,0:T(8,128)(2,1)}, bf16[256,7168]{1,0:T(8,128)(2,1)}, u32[]{:S(2)}, u32[]{:S(2)}) collective-permute-start(bf16[256,7168]{1,0:T(8,128)(2,1)} %shard_map.100), channel_id=1, source_target_pairs={{0,8},{8,0},{16,24},{24,16},{1,9},{9,1},{17,25},{25,17},{2,10},{10... | collective-permute-start | bytes 11010056 | tf_op jit(solution)/shard_map/ppermute | solution.py:148
  15.8 142.9 %collective-permute-start.1 = (bf16[256,7168]{1,0:T(8,128)(2,1)}, bf16[256,7168]{1,0:T(8,128)(2,1)}, u32[]{:S(2)}, u32[]{:S(2)}) collective-permute-start(bf16[256,7168]{1,0:T(8,128)(2,1)} %shard_map.100), channel_id=1, source_target_pairs={{0,4},{4,0},{1,5},{5,1},{2,6},{6,2},{3,7},{7,3},{8,12},{12,8},{9,1... | collective-permute-start | bytes 11010056 | tf_op jit(solution)/shard_map/ppermute | solution.py:148
  17.9 340.0 %all-gather.6.cloned.1.call-start = ((), (), s32[]{:S(2)}) async-start(), calls=%async_computation.1 | async-start | bytes 33030144 | tf_op jit(solution)/shard_map/all_gather | solution.py:448
  35.2 2.3 copy-start.8
  35.2 4.8 copy-start.14
  36.9 116.9 %collective-permute-start.2 = (bf16[2,672,896]{2,1,0:T(8,128)(2,1)}, bf16[2,672,896]{2,1,0:T(8,128)(2,1)}, u32[]{:S(2)}, u32[]{:S(2)}) collective-permute-start(bf16[2,672,896]{2,1,0:T(8,128)(2,1)} %pad_maximum_fusion), channel_id=1, source_target_pairs={{0,4},{4,0},{1,5},{5,1},{2,6},{6,2},{3,7},{7,3},{8,12},{12,8},{9,1... | collective-permute-start | bytes 7225352 | tf_op jit(solution)/shard_map/ppermute | solution.py:148
  37.4 121.2 %collective-permute-start.3 = (bf16[672,896]{1,0:T(8,128)(2,1)S(1)}, bf16[672,896]{1,0:T(8,128)(2,1)}, u32[]{:S(2)}, u32[]{:S(2)}) collective-permute-start(bf16[672,896]{1,0:T(8,128)(2,1)S(1)} %get-tuple-element.128.refs_3_.refs_1_.refs_2_), channel_id=1, source_target_pairs={{0,16},{8,24},{16,0},{24,8},{1,17},{9,25},{17,1},{25,9},{2,18},{10... | collective-permute-start | bytes 3612680 | tf_op jit(solution)/shard_map/ppermute | solution.py:148
  40.0 118.6 %collective-permute-start.4 = (bf16[672,896]{1,0:T(8,128)(2,1)}, bf16[672,896]{1,0:T(8,128)(2,1)}, u32[]{:S(2)}, u32[]{:S(2)}) collective-permute-start(bf16[672,896]{1,0:T(8,128)(2,1)} %get-tuple-element.127), channel_id=1, source_target_pairs={{0,24},{8,16},{16,8},{24,0},{1,25},{9,17},{17,9},{25,1},{2,26},{10... | collective-permute-start | bytes 3612680 | tf_op jit(solution)/shard_map/ppermute | solution.py:148
  48.5 108.3 %copy-start.10 = (bf16[1,672,896]{2,1,0:T(8,128)(2,1)S(1)}, bf16[1,672,896]{2,1,0:T(8,128)(2,1)}, u32[]{:S(2)}) copy-start(bf16[1,672,896]{2,1,0:T(8,128)(2,1)} %get-tuple-element.131) | copy-start | bytes 3612676
  156.8 2.7 copy-start.9
  158.7 3.5 copy-start.13
  158.7 6.3 %copy-start.7 = (f32[7168]{0:T(1024)S(1)}, f32[7168]{0:T(1024)}, u32[]{:S(2)}) copy-start(f32[7168]{0:T(1024)} %param.11) | copy-start | bytes 86020
  158.7 311.9 %all-gather.8.cloned.1.call-start = ((), (), s32[]{:S(2)}) async-start(), calls=%async_computation.2 | async-start | bytes 7225344 | tf_op jit(solution)/shard_map/all_gather | solution.py:519
  159.0 108.8 %collective-permute-start.9 = (bf16[256,7168]{1,0:T(8,128)(2,1)}, bf16[256,7168]{1,0:T(8,128)(2,1)}, u32[]{:S(2)}, u32[]{:S(2)}) collective-permute-start(bf16[256,7168]{1,0:T(8,128)(2,1)} %collective-permute-done.1.refs_1_), channel_id=1, source_target_pairs={{0,1},{1,0},{2,3},{3,2},{4,5},{5,4},{6,7},{7,6},{8,9},{9,8},{10,11... | collective-permute-start | bytes 11010056 | tf_op jit(solution)/shard_map/ppermute | solution.py:148
  159.1 108.7 %collective-permute-start.5 = (bf16[2,672,896]{2,1,0:T(8,128)(2,1)}, bf16[2,672,896]{2,1,0:T(8,128)(2,1)}, u32[]{:S(2)}, u32[]{:S(2)}) collective-permute-start(bf16[2,672,896]{2,1,0:T(8,128)(2,1)} %pad_maximum_fusion.1), channel_id=1, source_target_pairs={{0,8},{8,0},{16,24},{24,16},{1,9},{9,1},{17,25},{25,17},{2,10},{10... | collective-permute-start | bytes 7225352 | tf_op jit(solution)/shard_map/ppermute | solution.py:148
  159.4 78.7 %collective-permute-start.6 = (bf16[672,896]{1,0:T(8,128)(2,1)S(1)}, bf16[672,896]{1,0:T(8,128)(2,1)}, u32[]{:S(2)}, u32[]{:S(2)}) collective-permute-start(bf16[672,896]{1,0:T(8,128)(2,1)S(1)} %get-tuple-element.66.refs_4_.refs_2_.refs_3_), channel_id=1, source_target_pairs={{0,16},{8,24},{16,0},{24,8},{1,17},{9,25},{17,1},{25,9},{2,18},{10... | collective-permute-start | bytes 3612680 | tf_op jit(solution)/shard_map/ppermute | solution.py:148
  162.2 105.6 %collective-permute-start.7 = (bf16[672,896]{1,0:T(8,128)(2,1)S(1)}, bf16[672,896]{1,0:T(8,128)(2,1)}, u32[]{:S(2)}, u32[]{:S(2)}) collective-permute-start(bf16[672,896]{1,0:T(8,128)(2,1)S(1)} %copy-done.13), channel_id=1, source_target_pairs={{0,24},{8,16},{16,8},{24,0},{1,25},{9,17},{17,9},{25,1},{2,26},{10... | collective-permute-start | bytes 3612680 | tf_op jit(solution)/shard_map/ppermute | solution.py:148
  163.5 36.0 %collective-permute-start.8 = (bf16[2,448,512]{2,1,0:T(8,128)(2,1)S(1)}, bf16[2,448,512]{2,1,0:T(8,128)(2,1)}, u32[]{:S(2)}, u32[]{:S(2)}) collective-permute-start(bf16[2,448,512]{2,1,0:T(8,128)(2,1)S(1)} %get-tuple-element.69), channel_id=1, source_target_pairs={{0,4},{4,0},{1,5},{5,1},{2,6},{6,2},{3,7},{7,3},{8,12},{12,8},{9,1... | collective-permute-start | bytes 2752520 | tf_op jit(solution)/shard_map/ppermute | solution.py:148
  191.3 8.3 %copy-start.11 = (bf16[2,448,512]{2,1,0:T(8,128)(2,1)S(1)}, bf16[2,448,512]{2,1,0:T(8,128)(2,1)}, u32[]{:S(2)}) copy-start(bf16[2,448,512]{2,1,0:T(8,128)(2,1)} %get-tuple-element.68) | copy-start | bytes 2752516
  267.8 82.1 %collective-permute-start.13 = (bf16[128,7168]{1,0:T(8,128)(2,1)}, bf16[128,7168]{1,0:T(8,128)(2,1)}, u32[]{:S(2)}, u32[]{:S(2)}) collective-permute-start(bf16[128,7168]{1,0:T(8,128)(2,1)} %slice.36), channel_id=1, source_target_pairs={{0,2},{2,0},{1,3},{3,1},{4,6},{6,4},{5,7},{7,5},{8,10},{10,8},{9,1... | collective-permute-start | bytes 5505032 | tf_op jit(solution)/shard_map/ppermute | solution.py:148
  269.3 81.3 %collective-permute-start.14 = (bf16[128,7168]{1,0:T(8,128)(2,1)}, bf16[128,7168]{1,0:T(8,128)(2,1)}, u32[]{:S(2)}, u32[]{:S(2)}) collective-permute-start(bf16[128,7168]{1,0:T(8,128)(2,1)} %constant_dynamic-slice_fusion.4), channel_id=1, source_target_pairs={{0,4},{4,0},{1,5},{5,1},{2,6},{6,2},{3,7},{7,3},{8,12},{12,8},{9,1... | collective-permute-start | bytes 5505032 | tf_op jit(solution)/shard_map/ppermute | solution.py:148
  270.8 45.5 %collective-permute-start.10 = (bf16[2,448,512]{2,1,0:T(8,128)(2,1)}, bf16[2,448,512]{2,1,0:T(8,128)(2,1)S(1)}, u32[]{:S(2)}, u32[]{:S(2)}) collective-permute-start(bf16[2,448,512]{2,1,0:T(8,128)(2,1)} %get-tuple-element.73), channel_id=1, source_target_pairs={{0,8},{8,0},{16,24},{24,16},{1,9},{9,1},{17,25},{25,17},{2,10},{10... | collective-permute-start | bytes 2752520 | tf_op jit(solution)/shard_map/ppermute | solution.py:148
  270.8 63.5 %collective-permute-start.11 = (bf16[2,448,512]{2,1,0:T(8,128)(2,1)S(1)}, bf16[2,448,512]{2,1,0:T(8,128)(2,1)S(1)}, u32[]{:S(2)}, u32[]{:S(2)}) collective-permute-start(bf16[2,448,512]{2,1,0:T(8,128)(2,1)S(1)} %get-tuple-element.93.refs_0_), channel_id=1, source_target_pairs={{0,16},{8,24},{16,0},{24,8},{1,17},{9,25},{17,1},{25,9},{2,18},{10... | collective-permute-start | bytes 2752520 | tf_op jit(solution)/shard_map/ppermute | solution.py:148
  272.4 61.9 %collective-permute-start.12 = (bf16[2,448,512]{2,1,0:T(8,128)(2,1)}, bf16[2,448,512]{2,1,0:T(8,128)(2,1)}, u32[]{:S(2)}, u32[]{:S(2)}) collective-permute-start(bf16[2,448,512]{2,1,0:T(8,128)(2,1)} %get-tuple-element.73), channel_id=1, source_target_pairs={{0,24},{8,16},{16,8},{24,0},{1,25},{9,17},{17,9},{25,1},{2,26},{10... | collective-permute-start | bytes 2752520 | tf_op jit(solution)/shard_map/ppermute | solution.py:148
  353.8 3.0 copy-start.23
  353.8 3.8 copy-start.22
  356.8 45.6 %collective-permute-start.15 = (bf16[256,7168]{1,0:T(8,128)(2,1)}, bf16[256,7168]{1,0:T(8,128)(2,1)}, u32[]{:S(2)}, u32[]{:S(2)}) collective-permute-start(bf16[256,7168]{1,0:T(8,128)(2,1)} %constant_dynamic-update-slice_fusion.refs_0_), channel_id=1, source_target_pairs={{0,1},{1,0},{2,3},{3,2},{4,5},{5,4},{6,7},{7,6},{8,9},{9,8},{10,11... | collective-permute-start | bytes 11010056 | tf_op jit(solution)/shard_map/ppermute | solution.py:148
  393.5 1.2 copy-start.4
  402.4 41.4 %collective-permute-start.16 = (bf16[224,1024]{1,0:T(8,128)(2,1)S(1)}, bf16[224,1024]{1,0:T(8,128)(2,1)}, u32[]{:S(2)}, u32[]{:S(2)}) collective-permute-start(bf16[224,1024]{1,0:T(8,128)(2,1)S(1)} %shard_map.104), channel_id=1, source_target_pairs={{0,8},{8,0},{16,24},{24,16},{1,9},{9,1},{17,25},{25,17},{2,10},{10... | collective-permute-start | bytes 1376264 | tf_op jit(solution)/shard_map/ppermute | solution.py:148
  406.2 16.5 %copy-start.18 = (bf16[6,256,224]{2,1,0:T(8,128)(2,1)S(1)}, bf16[6,256,224]{2,1,0:T(8,128)(2,1)}, u32[]{:S(2)}) copy-start(bf16[6,256,224]{2,1,0:T(8,128)(2,1)} %get-tuple-element.104) | copy-start | bytes 2064388
  422.7 1.4 copy-start.12
  422.7 1.5 copy-start.19
  424.0 23.2 %copy-start.2 = (bf16[8,256,224]{2,1,0:T(8,128)(2,1)}, bf16[8,256,224]{2,1,0:T(8,128)(2,1)S(1)}, u32[]{:S(2)}) copy-start(bf16[8,256,224]{2,1,0:T(8,128)(2,1)S(1)} %pad_maximum_fusion.5.keys_ref) | copy-start | bytes 2752516
  445.5 11.0 %collective-permute-start.17 = (bf16[224,512]{1,0:T(8,128)(2,1)S(1)}, bf16[224,512]{1,0:T(8,128)(2,1)S(1)}, u32[]{:S(2)}, u32[]{:S(2)}) collective-permute-start(bf16[224,512]{1,0:T(8,128)(2,1)S(1)} %get-tuple-element.148), channel_id=1, source_target_pairs={{0,4},{4,0},{1,5},{5,1},{2,6},{6,2},{3,7},{7,3},{8,12},{12,8},{9,1... | collective-permute-start | bytes 688136 | tf_op jit(solution)/shard_map/ppermute | solution.py:148
  456.5 0.9 copy-start.20
  457.4 11.0 %collective-permute-start.18 = (bf16[224,512]{1,0:T(8,128)(2,1)}, bf16[224,512]{1,0:T(8,128)(2,1)}, u32[]{:S(2)}, u32[]{:S(2)}) collective-permute-start(bf16[224,512]{1,0:T(8,128)(2,1)} %get-tuple-element.146), channel_id=1, source_target_pairs={{0,4},{4,0},{1,5},{5,1},{2,6},{6,2},{3,7},{7,3},{8,12},{12,8},{9,1... | collective-permute-start | bytes 688136 | tf_op jit(solution)/shard_map/ppermute | solution.py:148
  457.7 1.2 copy-start.5
  459.0 9.4 %copy-start.16 = (bf16[1,224,512]{2,1,0:T(8,128)(2,1)S(1)}, bf16[1,224,512]{2,1,0:T(8,128)(2,1)}, u32[]{:S(2)}) copy-start(bf16[1,224,512]{2,1,0:T(8,128)(2,1)} %get-tuple-element.147) | copy-start | bytes 688132
  459.0 9.4 %copy-start.21 = (bf16[224,512]{1,0:T(8,128)(2,1)S(1)}, bf16[224,512]{1,0:T(8,128)(2,1)}, u32[]{:S(2)}) copy-start(bf16[224,512]{1,0:T(8,128)(2,1)} %copy-done.20) | copy-start | bytes 688132
  459.0 9.5 %copy-start.17 = (bf16[1,224,512]{2,1,0:T(8,128)(2,1)S(1)}, bf16[1,224,512]{2,1,0:T(8,128)(2,1)}, u32[]{:S(2)}) copy-start(bf16[1,224,512]{2,1,0:T(8,128)(2,1)} %get-tuple-element.145) | copy-start | bytes 688132
  474.6 4.4 collective-permute-start.20
  478.5 4.7 collective-permute-start.21
  479.0 4.2 copy-start.15
  479.0 12.4 %collective-permute-start.19 = (bf16[224,1024]{1,0:T(8,128)(2,1)S(1)}, bf16[224,1024]{1,0:T(8,128)(2,1)S(1)}, u32[]{:S(2)}, u32[]{:S(2)}) collective-permute-start(bf16[224,1024]{1,0:T(8,128)(2,1)S(1)} %shard_map.107), channel_id=1, source_target_pairs={{0,8},{8,0},{16,24},{24,16},{1,9},{9,1},{17,25},{25,17},{2,10},{10... | collective-permute-start | bytes 1376264 | tf_op jit(solution)/shard_map/ppermute | solution.py:148
  483.2 11.3 %copy-start.3 = (bf16[8,256,224]{2,1,0:T(8,128)(2,1)S(1)}, bf16[8,256,224]{2,1,0:T(8,128)(2,1)}, u32[]{:S(2)}) copy-start(bf16[8,256,224]{2,1,0:T(8,128)(2,1)} %copy-done.2) | copy-start | bytes 2752516
  491.4 21.6 %collective-permute-start.24 = (bf16[512,896]{1,0:T(8,128)(2,1)}, bf16[512,896]{1,0:T(8,128)(2,1)S(1)}, u32[]{:S(2)}, u32[]{:S(2)}) collective-permute-start(bf16[512,896]{1,0:T(8,128)(2,1)} %add_convert_fusion.3), channel_id=1, source_target_pairs={{0,2},{2,0},{1,3},{3,1},{4,6},{6,4},{5,7},{7,5},{8,10},{10,8},{9,1... | collective-permute-start | bytes 2752520 | tf_op jit(solution)/shard_map/ppermute | solution.py:148
  492.5 20.7 %slice-start = ((s8[6422528]{0:T(1024)(128)(4,1)}), s8[4194304]{0:T(1024)(128)(4,1)S(1)}, s32[]{:S(2)}) async-start(s8[6422528]{0:T(1024)(128)(4,1)} %bitcast.96), calls=%async_computation.3 | async-start | bytes 8388608
  492.6 20.7 %slice-start.1 = ((s8[6422528]{0:T(1024)(128)(4,1)}), s8[2228224]{0:T(1024)(128)(4,1)S(1)}, s32[]{:S(2)}) async-start(s8[6422528]{0:T(1024)(128)(4,1)} %bitcast.96), calls=%async_computation.4 | async-start | bytes 4456448
  492.6 12.9 %collective-permute-start.22 = (bf16[224,512]{1,0:T(8,128)(2,1)S(1)}, bf16[224,512]{1,0:T(8,128)(2,1)S(1)}, u32[]{:S(2)}, u32[]{:S(2)}) collective-permute-start(bf16[224,512]{1,0:T(8,128)(2,1)S(1)} %get-tuple-element.144), channel_id=1, source_target_pairs={{0,4},{4,0},{1,5},{5,1},{2,6},{6,2},{3,7},{7,3},{8,12},{12,8},{9,1... | collective-permute-start | bytes 688136 | tf_op jit(solution)/shard_map/ppermute | solution.py:148
  505.6 6.4 %collective-permute-start.23 = (bf16[224,512]{1,0:T(8,128)(2,1)S(1)}, bf16[224,512]{1,0:T(8,128)(2,1)S(1)}, u32[]{:S(2)}, u32[]{:S(2)}) collective-permute-start(bf16[224,512]{1,0:T(8,128)(2,1)S(1)} %get-tuple-element.142), channel_id=1, source_target_pairs={{0,4},{4,0},{1,5},{5,1},{2,6},{6,2},{3,7},{7,3},{8,12},{12,8},{9,1... | collective-permute-start | bytes 688136 | tf_op jit(solution)/shard_map/ppermute | solution.py:148
  514.5 2.5 collective-permute-start.26
  515.9 5.1 collective-permute-start.25
  518.3 22.5 %collective-permute-start.27 = (bf16[512,896]{1,0:T(8,128)(2,1)S(1)}, bf16[512,896]{1,0:T(8,128)(2,1)S(1)}, u32[]{:S(2)}, u32[]{:S(2)}) collective-permute-start(bf16[512,896]{1,0:T(8,128)(2,1)S(1)} %add_convert_fusion.1), channel_id=1, source_target_pairs={{0,2},{2,0},{1,3},{3,1},{4,6},{6,4},{5,7},{7,5},{8,10},{10,8},{9,1... | collective-permute-start | bytes 2752520 | tf_op jit(solution)/shard_map/ppermute | solution.py:148
  540.8 1.7 copy-start.1
Sparse Core Ops, SparseCore 0:
  18.0 78.8 all-gather.3
  158.9 195.0 all-gather.5
  356.1 106.8 all-gather.7

commit v4 on v3

--- a/solution.py
+++ b/solution.py
@@ -562,16 +562,15 @@
     parts_turned, parts_keys = project((part_y, core_y), up, down, weight_blocks, order)
     own_keys = jnp.concatenate([local_keys, parts_keys])
     own_turned = jnp.concatenate([local_turned, parts_turned])
-    pair_first, own_turned, own_keys = fence(pair_first, own_turned, own_keys)
+    pair_second = attend(1, 1, (pair_turned, pair_projected[1]))
+    pair_first, pair_second, own_turned, own_keys = fence(
+        pair_first, pair_second, own_turned, own_keys
+    )
     pair_first_crossed = over_x(crossing(pair_first))
+    pair_second = over_z(pair_second, 1)
     own_first = attend(0, 0, (own_turned, own_keys))
-    pair_first_crossed, own_first, pair_turned, own_turned = fence(
-        pair_first_crossed, own_first, pair_turned, own_turned
-    )
+    pair_first_crossed, own_first, own_turned = fence(pair_first_crossed, own_first, own_turned)
     own_first_crossed = over_x(crossing(own_first))
-    pair_second = attend(1, 1, (pair_turned, pair_projected[1]))
-    own_first_crossed, pair_second = fence(own_first_crossed, pair_second)
-    pair_second = over_z(pair_second, 1)
     first_sent, first_here = summed(
         all_heads(own_first, own_first_crossed, pair_first, pair_first_crossed)
     )

time: 556 us -> 552 us (level)
    unnamed x55 -> x49, local copies, waits for them, and re-layouts: 16.5 us -> 16.5 us
  transfers between devices with their start and end apart: 31 -> 31, of which waited for: 13 -> 14; matrix products, arithmetic and copies ran while one was open for 15% -> 16% of each run, Pallas kernels for 26% -> 26%
where the time goes in v4:
time: 552 us; the launch traced here: 547 us
  waiting for transfers between devices  257 us (47%)
  Pallas kernels  146 us (26%)
  local copies, waits for them, and re-layouts  59.7 us (11%)
  starting transfers between devices  33.7 us (6%)
  matrix products  20 us (4%)
  other arithmetic  16.8 us (3%)
  between operations  14 us (3%)
    ppermute x28, waiting for transfers between devices, swap(): return lax.ppermute(array, axis, [(i, i ^ bit) for i in range(size)])  257 us
    pallas_call x3, Pallas kernels, project(): pl.pallas_call(functools.partial(project_kernel, tuple(sets)), grid_spec=...  83.2 us
    pallas_call x4, Pallas kernels, attention(): pl.pallas_call(functools.partial(attention_kernel, half), grid_spec=pltpu...  38.2 us
    ppermute x28, starting transfers between devices, swap(): return lax.ppermute(array, axis, [(i, i ^ bit) for i in range(size)])  33.1 us
    pallas_call x2, Pallas kernels, normalise(): pl.pallas_call(norm_kernel, grid_spec=pltpu.PrefetchScalarGridSpec(num_sc...  24.8 us
    dot_general x8, matrix products, out_part(): lax.dot_general(heads, columns[name], (((0,), (0,)), ((), ())), preferred...  20 us
    unnamed x49, local copies, waits for them, and re-layouts  16.5 us
  transfers between devices with their start and end apart: 31, of which 14 were waited for; matrix products, arithmetic and copies ran while one was open for 16% of the time, Pallas kernels for 26%

profile of v4, /device:TPU:0, one launch (start us, length us, event | category | flops | bytes accessed | tf_op | source)
XLA Modules:
  0.0 547.0 jit_solution(13384616325728155043)
XLA Ops:
  7.3 5.4 shard_map.100
  12.7 3.0 collective-permute-start
  15.8 1.5 collective-permute-start.1
  18.0 7.6 %copy.35 = bf16[896,3,896]{0,2,1:T(8,128)(2,1)} copy(bf16[896,3,896]{2,0,1:T(8,128)(2,1)} %param.12) | data formatting | bytes 9633792 | tf_op args[2]
  25.6 5.0 copy.36
  30.6 4.6 dynamic-slice_bitcast_fusion
  35.2 1.7 pad_maximum_fusion
  37.4 2.6 collective-permute-start.3
  41.6 3.0 reshape.94
  44.6 1.5 copy.42
  46.1 1.3 pad_maximum_fusion.2
  48.5 105.3 %collective-permute-done.2 = bf16[2,672,896]{2,1,0:T(8,128)(2,1)} collective-permute-done((bf16[2,672,896]{2,1,0:T(8,128)(2,1)}, bf16[2,672,896]{2,1,0:T(8,128)(2,1)}, u32[]{:S(2)}, u32[]{:S(2)}) %collective-permute-start.2) | collective-permute-done | bytes 2408480 | tf_op jit(solution)/shard_map/ppermute | solution.py:148
  153.8 3.0 slice_bitcast_fusion.5
  156.8 1.9 pad_maximum_fusion.1
  159.7 2.8 collective-permute-start.6
  162.5 1.3 collective-permute-start.7
  163.8 1.5 collective-permute-start.8
  165.3 19.4 %shard_map.101.refs_0_ = bf16[1024,7168]{1,0:T(8,128)(2,1)} custom-call(s32[1]{0:T(128)} %constant.230.clone.1.first, bf16[1024,7168]{1,0:T(8,128)(2,1)} %inputs_ref.2, f32[1,7168]{1,0:T(1,128)S(1)} %bitcast.73), custom_call_target="tpu_custom_call" | custom-call | flops 1 | bytes 1 | tf_op jit(solution)/shard_map/pallas_call | solution.py:173
  184.7 2.9 slice.36
  187.5 3.9 copy.41
  191.4 2.9 constant_dynamic-slice_fusion.4
  194.3 5.8 %collective-permute-done.8 = bf16[2,448,512]{2,1,0:T(8,128)(2,1)} collective-permute-done((bf16[2,448,512]{2,1,0:T(8,128)(2,1)S(1)}, bf16[2,448,512]{2,1,0:T(8,128)(2,1)}, u32[]{:S(2)}, u32[]{:S(2)}) %collective-permute-start.8) | collective-permute-done | bytes 917536 | tf_op jit(solution)/shard_map/ppermute | solution.py:148
  200.2 2.3 fusion.19
  202.4 36.0 %collective-permute-done.6.refs_8_.refs_6_.refs_7_ = bf16[672,896]{1,0:T(8,128)(2,1)} collective-permute-done((bf16[672,896]{1,0:T(8,128)(2,1)S(1)}, bf16[672,896]{1,0:T(8,128)(2,1)}, u32[]{:S(2)}, u32[]{:S(2)}) %collective-permute-start.6) | collective-permute-done | bytes 1204256 | tf_op jit(solution)/shard_map/ppermute | solution.py:148
  238.4 29.6 %collective-permute-done.7.refs_10_.refs_8_.refs_9_ = bf16[672,896]{1,0:T(8,128)(2,1)} collective-permute-done((bf16[672,896]{1,0:T(8,128)(2,1)S(1)}, bf16[672,896]{1,0:T(8,128)(2,1)}, u32[]{:S(2)}, u32[]{:S(2)}) %collective-permute-start.7) | collective-permute-done | bytes 1204256 | tf_op jit(solution)/shard_map/ppermute | solution.py:148
  268.0 1.5 collective-permute-start.13
  269.6 1.5 collective-permute-start.14
  271.1 1.6 collective-permute-start.11
  272.6 2.8 collective-permute-start.12
  275.4 2.2 copy.39
  277.7 2.0 copy.40
  280.2 1.6 dynamic-slice_bitcast_fusion.11.up_ref
  281.8 3.3 slice_bitcast_fusion.1
  285.1 31.5 %shard_map.102 = (bf16[6,448,256]{2,1,0:T(8,128)(2,1)}, bf16[6,256,224]{2,1,0:T(8,128)(2,1)}) custom-call(s32[8]{0:T(128)} %iota_xor_fusion.order, bf16[672,128]{1,0:T(8,128)(2,1)} %dynamic-slice_bitcast_fusion.11.up_ref, bf16[128,7168]{1,0:T(8,128)(2,1)} %bitcast.74, bf16[1024,7168]{1,0:T(8,128)(2,1)} %shard_map.101.refs_0_, ...), custom_call_target="tpu_custom_call" | custom-call | flops 1 | bytes 1 | tf_op jit(solution)/shard_map/pallas_call | solution.py:239
  316.6 18.0 %collective-permute-done.11.refs_2_ = bf16[2,448,512]{2,1,0:T(8,128)(2,1)S(1)} collective-permute-done((bf16[2,448,512]{2,1,0:T(8,128)(2,1)S(1)}, bf16[2,448,512]{2,1,0:T(8,128)(2,1)S(1)}, u32[]{:S(2)}, u32[]{:S(2)}) %collective-permute-start.11) | collective-permute-done | bytes 917536 | tf_op jit(solution)/shard_map/ppermute | solution.py:148
  334.6 15.5 %collective-permute-done.13 = bf16[128,7168]{1,0:T(8,128)(2,1)} collective-permute-done((bf16[128,7168]{1,0:T(8,128)(2,1)}, bf16[128,7168]{1,0:T(8,128)(2,1)}, u32[]{:S(2)}, u32[]{:S(2)}) %collective-permute-start.13) | collective-permute-done | bytes 1835040 | tf_op jit(solution)/shard_map/ppermute | solution.py:148
  350.9 3.2 constant_dynamic-update-slice_fusion.1
  354.1 2.9 constant_dynamic-update-slice_fusion.refs_0_
  358.2 35.5 %shard_map.103 = (bf16[8,448,256]{2,1,0:T(8,128)(2,1)}, bf16[8,256,224]{2,1,0:T(8,128)(2,1)}) custom-call(s32[8]{0:T(128)} %iota_xor_fusion.order, bf16[672,128]{1,0:T(8,128)(2,1)} %dynamic-slice_bitcast_fusion.11.up_ref, bf16[128,7168]{1,0:T(8,128)(2,1)} %bitcast.75, bf16[2048,7168]{1,0:T(8,128)(2,1)} %all-gather.6.cloned.1.call-done.refs_0_, ...), custom_call_target="tpu_custom_call" | custom-call | flops 1 | bytes 1 | tf_op jit(solution)/shard_map/pallas_call | solution.py:239
  394.9 8.2 %shard_map.104 = bf16[224,1024]{1,0:T(8,128)(2,1)} custom-call(s32[8]{0:T(128)S(1)} %iota.25.chunk_table, s32[4]{0:T(128)S(1)} %get-tuple-element.146.cache_table, s32[1]{0:T(128)} %get-tuple-element.148.length_ref, bf16[8,448,256]{2,1,0:T(8,128)(2,1)} %get-tuple-element.98.turned_ref, bf16[8,256,224]{2,1,0:T(8,128)(2,1)S(1)} %copy-done.4, ...), custom_call_target="tpu_custom_call" | custom-call | flops 1 | bytes 1 | tf_op jit(solution)/shard_map/pallas_call | solution.py:348
  403.1 3.9 collective-permute-start.16
  408.2 9.0 %shard_map.105 = bf16[224,1024]{1,0:T(8,128)(2,1)S(1)} custom-call(s32[8]{0:T(128)S(1)} %iota.27.chunk_table, s32[4]{0:T(128)S(1)} %get-tuple-element.146.cache_table, s32[1]{0:T(128)} %get-tuple-element.148.length_ref, bf16[8,448,256]{2,1,0:T(8,128)(2,1)} %get-tuple-element.98.turned_ref, bf16[8,256,224]{2,1,0:T(8,128)(2,1)S(1)} %copy-done.5, ...), custom_call_target="tpu_custom_call" | custom-call | flops 1 | bytes 1 | tf_op jit(solution)/shard_map/pallas_call | solution.py:348
  417.2 16.2 %shard_map.106 = (bf16[2,448,256]{2,1,0:T(8,128)(2,1)}, bf16[2,256,224]{2,1,0:T(8,128)(2,1)}) custom-call(s32[8]{0:T(128)} %iota_xor_fusion.order, bf16[672,128]{1,0:T(8,128)(2,1)} %dynamic-slice_bitcast_fusion.11.up_ref, bf16[128,7168]{1,0:T(8,128)(2,1)} %bitcast.76, bf16[256,7168]{1,0:T(8,128)(2,1)} %constant_dynamic-update-slice_fusion.refs_0_, ...), custom_call_target="tpu_custom_call" | custom-call | flops 1 | bytes 1 | tf_op jit(solution)/shard_map/pallas_call | solution.py:239
  434.9 1.4 pad_maximum_fusion.3.turned_ref
  436.3 8.4 %collective-permute-done.16 = bf16[224,1024]{1,0:T(8,128)(2,1)} collective-permute-done((bf16[224,1024]{1,0:T(8,128)(2,1)}, bf16[224,1024]{1,0:T(8,128)(2,1)}, u32[]{:S(2)}, u32[]{:S(2)}) %collective-permute-start.16) | collective-permute-done | bytes 458784 | tf_op jit(solution)/shard_map/ppermute | solution.py:148
  444.7 1.8 dynamic-slice_bitcast_fusion.9
  447.5 9.6 %shard_map.107 = bf16[224,1024]{1,0:T(8,128)(2,1)S(1)} custom-call(s32[8]{0:T(128)S(1)} %compare_select_fusion.chunk_table, s32[4]{0:T(128)S(1)} %get-tuple-element.145.cache_table, s32[1]{0:T(128)} %get-tuple-element.147.length_ref, bf16[8,448,256]{2,1,0:T(8,128)(2,1)} %pad_maximum_fusion.3.turned_ref, bf16[8,256,224]{2,1,0:T(8,128)(2,1)S(1)} %pad_maximum_fusion.5.keys_ref, ...), custom_call_target="tpu_custom_call" | custom-call | flops 1 | bytes 1 | tf_op jit(solution)/shard_map/pallas_call | solution.py:348
  459.0 1.4 maximum_select_fusion.3
  460.3 5.3 collective-permute-done.19
  465.6 1.4 maximum_select_fusion.2
  468.1 3.9 convolution_convert_fusion.3
  472.0 3.9 convolution_convert_fusion.2
  476.5 4.2 add_convert_fusion.3
  480.7 3.0 convert_add_fusion
  483.7 5.2 collective-permute-done.17
  488.9 1.5 collective-permute-start.24
  490.8 11.4 %shard_map.108 = bf16[224,1024]{1,0:T(8,128)(2,1)S(1)} custom-call(s32[8]{0:T(128)S(1)} %compare_select_fusion.chunk_table, s32[4]{0:T(128)S(1)} %get-tuple-element.145.cache_table, s32[1]{0:T(128)} %get-tuple-element.147.length_ref, bf16[8,448,256]{2,1,0:T(8,128)(2,1)} %pad_maximum_fusion.3.turned_ref, bf16[8,256,224]{2,1,0:T(8,128)(2,1)S(1)} %copy-done.3, ...), custom_call_target="tpu_custom_call" | custom-call | flops 1 | bytes 1 | tf_op jit(solution)/shard_map/pallas_call | solution.py:348
  502.3 1.5 collective-permute-start.23
  503.9 4.8 collective-permute-done.23
  508.7 1.7 collective-permute-done.24
  514.5 1.3 add_convert_fusion.1
  515.8 1.6 collective-permute-start.27
  518.8 19.4 %collective-permute-done.27 = bf16[512,896]{1,0:T(8,128)(2,1)S(1)} collective-permute-done((bf16[512,896]{1,0:T(8,128)(2,1)S(1)}, bf16[512,896]{1,0:T(8,128)(2,1)S(1)}, u32[]{:S(2)}, u32[]{:S(2)}) %collective-permute-start.27) | collective-permute-done | bytes 917536 | tf_op jit(solution)/shard_map/ppermute | solution.py:148
  538.6 1.4 pad_maximum_fusion.4
  (113 shorter events, 22.9 us)
Async XLA Ops:
  6.5 10.7 %copy-start = (bf16[896,128]{1,0:T(8,128)(2,1)S(1)}, bf16[896,128]{1,0:T(8,128)(2,1)}, u32[]{:S(2)}) copy-start(bf16[896,128]{1,0:T(8,128)(2,1)} %param.13) | copy-start | bytes 688132
  6.5 152.1 %all-gather.4.cloned.1.call-start = ((), (), s32[]{:S(2)}) async-start(), calls=%async_computation | async-start | bytes 1892352 | tf_op jit(solution)/shard_map/all_gather | solution.py:411
  6.5 0.8 copy-start.6
  12.7 145.9 %collective-permute-start = (bf16[256,7168]{1,0:T(8,128)(2,1)}, bf16[256,7168]{1,0:T(8,128)(2,1)}, u32[]{:S(2)}, u32[]{:S(2)}) collective-permute-start(bf16[256,7168]{1,0:T(8,128)(2,1)} %shard_map.100), channel_id=1, source_target_pairs={{0,8},{8,0},{16,24},{24,16},{1,9},{9,1},{17,25},{25,17},{2,10},{10... | collective-permute-start | bytes 11010056 | tf_op jit(solution)/shard_map/ppermute | solution.py:148
  15.8 142.9 %collective-permute-start.1 = (bf16[256,7168]{1,0:T(8,128)(2,1)}, bf16[256,7168]{1,0:T(8,128)(2,1)}, u32[]{:S(2)}, u32[]{:S(2)}) collective-permute-start(bf16[256,7168]{1,0:T(8,128)(2,1)} %shard_map.100), channel_id=1, source_target_pairs={{0,4},{4,0},{1,5},{5,1},{2,6},{6,2},{3,7},{7,3},{8,12},{12,8},{9,1... | collective-permute-start | bytes 11010056 | tf_op jit(solution)/shard_map/ppermute | solution.py:148
  17.9 340.3 %all-gather.6.cloned.1.call-start = ((), (), s32[]{:S(2)}) async-start(), calls=%async_computation.1 | async-start | bytes 33030144 | tf_op jit(solution)/shard_map/all_gather | solution.py:448
  35.2 2.2 copy-start.8
  35.2 4.8 copy-start.14
  36.9 116.9 %collective-permute-start.2 = (bf16[2,672,896]{2,1,0:T(8,128)(2,1)}, bf16[2,672,896]{2,1,0:T(8,128)(2,1)}, u32[]{:S(2)}, u32[]{:S(2)}) collective-permute-start(bf16[2,672,896]{2,1,0:T(8,128)(2,1)} %pad_maximum_fusion), channel_id=1, source_target_pairs={{0,4},{4,0},{1,5},{5,1},{2,6},{6,2},{3,7},{7,3},{8,12},{12,8},{9,1... | collective-permute-start | bytes 7225352 | tf_op jit(solution)/shard_map/ppermute | solution.py:148
  37.4 121.2 %collective-permute-start.3 = (bf16[672,896]{1,0:T(8,128)(2,1)S(1)}, bf16[672,896]{1,0:T(8,128)(2,1)}, u32[]{:S(2)}, u32[]{:S(2)}) collective-permute-start(bf16[672,896]{1,0:T(8,128)(2,1)S(1)} %get-tuple-element.124.refs_3_.refs_1_.refs_2_), channel_id=1, source_target_pairs={{0,16},{8,24},{16,0},{24,8},{1,17},{9,25},{17,1},{25,9},{2,18},{10... | collective-permute-start | bytes 3612680 | tf_op jit(solution)/shard_map/ppermute | solution.py:148
  40.0 118.6 %collective-permute-start.4 = (bf16[672,896]{1,0:T(8,128)(2,1)}, bf16[672,896]{1,0:T(8,128)(2,1)}, u32[]{:S(2)}, u32[]{:S(2)}) collective-permute-start(bf16[672,896]{1,0:T(8,128)(2,1)} %get-tuple-element.123), channel_id=1, source_target_pairs={{0,24},{8,16},{16,8},{24,0},{1,25},{9,17},{17,9},{25,1},{2,26},{10... | collective-permute-start | bytes 3612680 | tf_op jit(solution)/shard_map/ppermute | solution.py:148
  48.5 108.3 %copy-start.10 = (bf16[1,672,896]{2,1,0:T(8,128)(2,1)S(1)}, bf16[1,672,896]{2,1,0:T(8,128)(2,1)}, u32[]{:S(2)}) copy-start(bf16[1,672,896]{2,1,0:T(8,128)(2,1)} %get-tuple-element.127) | copy-start | bytes 3612676
  156.8 2.9 copy-start.9
  158.7 3.8 copy-start.13
  158.7 6.6 %copy-start.7 = (f32[7168]{0:T(1024)S(1)}, f32[7168]{0:T(1024)}, u32[]{:S(2)}) copy-start(f32[7168]{0:T(1024)} %param.11) | copy-start | bytes 86020
  158.7 309.4 %all-gather.8.cloned.1.call-start = ((), (), s32[]{:S(2)}) async-start(), calls=%async_computation.2 | async-start | bytes 7225344 | tf_op jit(solution)/shard_map/all_gather | solution.py:519
  159.3 108.8 %collective-permute-start.9 = (bf16[256,7168]{1,0:T(8,128)(2,1)}, bf16[256,7168]{1,0:T(8,128)(2,1)}, u32[]{:S(2)}, u32[]{:S(2)}) collective-permute-start(bf16[256,7168]{1,0:T(8,128)(2,1)} %collective-permute-done.1.refs_1_), channel_id=1, source_target_pairs={{0,1},{1,0},{2,3},{3,2},{4,5},{5,4},{6,7},{7,6},{8,9},{9,8},{10,11... | collective-permute-start | bytes 11010056 | tf_op jit(solution)/shard_map/ppermute | solution.py:148
  159.4 108.7 %collective-permute-start.5 = (bf16[2,672,896]{2,1,0:T(8,128)(2,1)}, bf16[2,672,896]{2,1,0:T(8,128)(2,1)}, u32[]{:S(2)}, u32[]{:S(2)}) collective-permute-start(bf16[2,672,896]{2,1,0:T(8,128)(2,1)} %pad_maximum_fusion.1), channel_id=1, source_target_pairs={{0,8},{8,0},{16,24},{24,16},{1,9},{9,1},{17,25},{25,17},{2,10},{10... | collective-permute-start | bytes 7225352 | tf_op jit(solution)/shard_map/ppermute | solution.py:148
  159.7 78.7 %collective-permute-start.6 = (bf16[672,896]{1,0:T(8,128)(2,1)S(1)}, bf16[672,896]{1,0:T(8,128)(2,1)}, u32[]{:S(2)}, u32[]{:S(2)}) collective-permute-start(bf16[672,896]{1,0:T(8,128)(2,1)S(1)} %get-tuple-element.64.refs_4_.refs_2_.refs_3_), channel_id=1, source_target_pairs={{0,16},{8,24},{16,0},{24,8},{1,17},{9,25},{17,1},{25,9},{2,18},{10... | collective-permute-start | bytes 3612680 | tf_op jit(solution)/shard_map/ppermute | solution.py:148
  162.5 105.6 %collective-permute-start.7 = (bf16[672,896]{1,0:T(8,128)(2,1)S(1)}, bf16[672,896]{1,0:T(8,128)(2,1)}, u32[]{:S(2)}, u32[]{:S(2)}) collective-permute-start(bf16[672,896]{1,0:T(8,128)(2,1)S(1)} %copy-done.13), channel_id=1, source_target_pairs={{0,24},{8,16},{16,8},{24,0},{1,25},{9,17},{17,9},{25,1},{2,26},{10... | collective-permute-start | bytes 3612680 | tf_op jit(solution)/shard_map/ppermute | solution.py:148
  163.8 36.3 %collective-permute-start.8 = (bf16[2,448,512]{2,1,0:T(8,128)(2,1)S(1)}, bf16[2,448,512]{2,1,0:T(8,128)(2,1)}, u32[]{:S(2)}, u32[]{:S(2)}) collective-permute-start(bf16[2,448,512]{2,1,0:T(8,128)(2,1)S(1)} %get-tuple-element.67), channel_id=1, source_target_pairs={{0,4},{4,0},{1,5},{5,1},{2,6},{6,2},{3,7},{7,3},{8,12},{12,8},{9,1... | collective-permute-start | bytes 2752520 | tf_op jit(solution)/shard_map/ppermute | solution.py:148
  191.4 8.7 %copy-start.11 = (bf16[2,448,512]{2,1,0:T(8,128)(2,1)S(1)}, bf16[2,448,512]{2,1,0:T(8,128)(2,1)}, u32[]{:S(2)}) copy-start(bf16[2,448,512]{2,1,0:T(8,128)(2,1)} %get-tuple-element.66) | copy-start | bytes 2752516
  268.0 82.1 %collective-permute-start.13 = (bf16[128,7168]{1,0:T(8,128)(2,1)}, bf16[128,7168]{1,0:T(8,128)(2,1)}, u32[]{:S(2)}, u32[]{:S(2)}) collective-permute-start(bf16[128,7168]{1,0:T(8,128)(2,1)} %slice.36), channel_id=1, source_target_pairs={{0,2},{2,0},{1,3},{3,1},{4,6},{6,4},{5,7},{7,5},{8,10},{10,8},{9,1... | collective-permute-start | bytes 5505032 | tf_op jit(solution)/shard_map/ppermute | solution.py:148
  269.6 81.3 %collective-permute-start.14 = (bf16[128,7168]{1,0:T(8,128)(2,1)}, bf16[128,7168]{1,0:T(8,128)(2,1)}, u32[]{:S(2)}, u32[]{:S(2)}) collective-permute-start(bf16[128,7168]{1,0:T(8,128)(2,1)} %constant_dynamic-slice_fusion.4), channel_id=1, source_target_pairs={{0,4},{4,0},{1,5},{5,1},{2,6},{6,2},{3,7},{7,3},{8,12},{12,8},{9,1... | collective-permute-start | bytes 5505032 | tf_op jit(solution)/shard_map/ppermute | solution.py:148
  271.1 45.6 %collective-permute-start.10 = (bf16[2,448,512]{2,1,0:T(8,128)(2,1)}, bf16[2,448,512]{2,1,0:T(8,128)(2,1)S(1)}, u32[]{:S(2)}, u32[]{:S(2)}) collective-permute-start(bf16[2,448,512]{2,1,0:T(8,128)(2,1)} %get-tuple-element.71), channel_id=1, source_target_pairs={{0,8},{8,0},{16,24},{24,16},{1,9},{9,1},{17,25},{25,17},{2,10},{10... | collective-permute-start | bytes 2752520 | tf_op jit(solution)/shard_map/ppermute | solution.py:148
  271.1 63.5 %collective-permute-start.11 = (bf16[2,448,512]{2,1,0:T(8,128)(2,1)S(1)}, bf16[2,448,512]{2,1,0:T(8,128)(2,1)S(1)}, u32[]{:S(2)}, u32[]{:S(2)}) collective-permute-start(bf16[2,448,512]{2,1,0:T(8,128)(2,1)S(1)} %get-tuple-element.91.refs_0_), channel_id=1, source_target_pairs={{0,16},{8,24},{16,0},{24,8},{1,17},{9,25},{17,1},{25,9},{2,18},{10... | collective-permute-start | bytes 2752520 | tf_op jit(solution)/shard_map/ppermute | solution.py:148
  272.6 61.9 %collective-permute-start.12 = (bf16[2,448,512]{2,1,0:T(8,128)(2,1)}, bf16[2,448,512]{2,1,0:T(8,128)(2,1)}, u32[]{:S(2)}, u32[]{:S(2)}) collective-permute-start(bf16[2,448,512]{2,1,0:T(8,128)(2,1)} %get-tuple-element.71), channel_id=1, source_target_pairs={{0,24},{8,16},{16,8},{24,0},{1,25},{9,17},{17,9},{25,1},{2,26},{10... | collective-permute-start | bytes 2752520 | tf_op jit(solution)/shard_map/ppermute | solution.py:148
  354.1 3.0 copy-start.20
  354.1 3.8 copy-start.19
  357.0 46.0 %collective-permute-start.15 = (bf16[256,7168]{1,0:T(8,128)(2,1)}, bf16[256,7168]{1,0:T(8,128)(2,1)}, u32[]{:S(2)}, u32[]{:S(2)}) collective-permute-start(bf16[256,7168]{1,0:T(8,128)(2,1)} %constant_dynamic-update-slice_fusion.refs_0_), channel_id=1, source_target_pairs={{0,1},{1,0},{2,3},{3,2},{4,5},{5,4},{6,7},{7,6},{8,9},{9,8},{10,11... | collective-permute-start | bytes 11010056 | tf_op jit(solution)/shard_map/ppermute | solution.py:148
  393.7 1.2 copy-start.4
  403.1 41.6 %collective-permute-start.16 = (bf16[224,1024]{1,0:T(8,128)(2,1)}, bf16[224,1024]{1,0:T(8,128)(2,1)}, u32[]{:S(2)}, u32[]{:S(2)}) collective-permute-start(bf16[224,1024]{1,0:T(8,128)(2,1)} %shard_map.104), channel_id=1, source_target_pairs={{0,8},{8,0},{16,24},{24,16},{1,9},{9,1},{17,25},{25,17},{2,10},{10... | collective-permute-start | bytes 1376264 | tf_op jit(solution)/shard_map/ppermute | solution.py:148
  407.0 1.2 copy-start.5
  417.2 16.2 %copy-start.16 = (bf16[6,256,224]{2,1,0:T(8,128)(2,1)S(1)}, bf16[6,256,224]{2,1,0:T(8,128)(2,1)}, u32[]{:S(2)}) copy-start(bf16[6,256,224]{2,1,0:T(8,128)(2,1)} %get-tuple-element.103) | copy-start | bytes 2064388
  433.4 1.4 copy-start.12
  433.4 1.5 copy-start.17
  434.7 12.8 %copy-start.2 = (bf16[8,256,224]{2,1,0:T(8,128)(2,1)}, bf16[8,256,224]{2,1,0:T(8,128)(2,1)S(1)}, u32[]{:S(2)}) copy-start(bf16[8,256,224]{2,1,0:T(8,128)(2,1)S(1)} %pad_maximum_fusion.5.keys_ref) | copy-start | bytes 2752516
  446.5 10.6 %collective-permute-start.18 = (bf16[224,512]{1,0:T(8,128)(2,1)S(1)}, bf16[224,512]{1,0:T(8,128)(2,1)S(1)}, u32[]{:S(2)}, u32[]{:S(2)}) collective-permute-start(bf16[224,512]{1,0:T(8,128)(2,1)S(1)} %get-tuple-element.144), channel_id=1, source_target_pairs={{0,4},{4,0},{1,5},{5,1},{2,6},{6,2},{3,7},{7,3},{8,12},{12,8},{9,1... | collective-permute-start | bytes 688136 | tf_op jit(solution)/shard_map/ppermute | solution.py:148
  457.1 0.9 copy-start.18
  458.0 7.6 %collective-permute-start.19 = (bf16[224,512]{1,0:T(8,128)(2,1)}, bf16[224,512]{1,0:T(8,128)(2,1)}, u32[]{:S(2)}, u32[]{:S(2)}) collective-permute-start(bf16[224,512]{1,0:T(8,128)(2,1)} %get-tuple-element.142), channel_id=1, source_target_pairs={{0,4},{4,0},{1,5},{5,1},{2,6},{6,2},{3,7},{7,3},{8,12},{12,8},{9,1... | collective-permute-start | bytes 688136 | tf_op jit(solution)/shard_map/ppermute | solution.py:148
  472.0 4.4 collective-permute-start.20
  475.9 4.7 collective-permute-start.21
  476.4 4.2 copy-start.15
  476.5 12.4 %collective-permute-start.17 = (bf16[224,1024]{1,0:T(8,128)(2,1)S(1)}, bf16[224,1024]{1,0:T(8,128)(2,1)S(1)}, u32[]{:S(2)}, u32[]{:S(2)}) collective-permute-start(bf16[224,1024]{1,0:T(8,128)(2,1)S(1)} %shard_map.105), channel_id=1, source_target_pairs={{0,8},{8,0},{16,24},{24,16},{1,9},{9,1},{17,25},{25,17},{2,10},{10... | collective-permute-start | bytes 1376264 | tf_op jit(solution)/shard_map/ppermute | solution.py:148
  480.7 10.1 %copy-start.3 = (bf16[8,256,224]{2,1,0:T(8,128)(2,1)S(1)}, bf16[8,256,224]{2,1,0:T(8,128)(2,1)}, u32[]{:S(2)}) copy-start(bf16[8,256,224]{2,1,0:T(8,128)(2,1)} %copy-done.2) | copy-start | bytes 2752516
  488.9 21.6 %collective-permute-start.24 = (bf16[512,896]{1,0:T(8,128)(2,1)}, bf16[512,896]{1,0:T(8,128)(2,1)S(1)}, u32[]{:S(2)}, u32[]{:S(2)}) collective-permute-start(bf16[512,896]{1,0:T(8,128)(2,1)} %add_convert_fusion.3), channel_id=1, source_target_pairs={{0,2},{2,0},{1,3},{3,1},{4,6},{6,4},{5,7},{7,5},{8,10},{10,8},{9,1... | collective-permute-start | bytes 2752520 | tf_op jit(solution)/shard_map/ppermute | solution.py:148
  490.4 20.3 %slice-start = ((s8[6422528]{0:T(1024)(128)(4,1)}), s8[4194304]{0:T(1024)(128)(4,1)S(1)}, s32[]{:S(2)}) async-start(s8[6422528]{0:T(1024)(128)(4,1)} %bitcast.96), calls=%async_computation.3 | async-start | bytes 8388608
  490.4 20.3 %slice-start.1 = ((s8[6422528]{0:T(1024)(128)(4,1)}), s8[2228224]{0:T(1024)(128)(4,1)S(1)}, s32[]{:S(2)}) async-start(s8[6422528]{0:T(1024)(128)(4,1)} %bitcast.96), calls=%async_computation.4 | async-start | bytes 4456448
  490.5 11.8 %collective-permute-start.22 = (bf16[224,512]{1,0:T(8,128)(2,1)S(1)}, bf16[224,512]{1,0:T(8,128)(2,1)S(1)}, u32[]{:S(2)}, u32[]{:S(2)}) collective-permute-start(bf16[224,512]{1,0:T(8,128)(2,1)S(1)} %get-tuple-element.140), channel_id=1, source_target_pairs={{0,4},{4,0},{1,5},{5,1},{2,6},{6,2},{3,7},{7,3},{8,12},{12,8},{9,1... | collective-permute-start | bytes 688136 | tf_op jit(solution)/shard_map/ppermute | solution.py:148
  502.3 6.4 %collective-permute-start.23 = (bf16[224,512]{1,0:T(8,128)(2,1)S(1)}, bf16[224,512]{1,0:T(8,128)(2,1)S(1)}, u32[]{:S(2)}, u32[]{:S(2)}) collective-permute-start(bf16[224,512]{1,0:T(8,128)(2,1)S(1)} %get-tuple-element.138), channel_id=1, source_target_pairs={{0,4},{4,0},{1,5},{5,1},{2,6},{6,2},{3,7},{7,3},{8,12},{12,8},{9,1... | collective-permute-start | bytes 688136 | tf_op jit(solution)/shard_map/ppermute | solution.py:148
  512.0 2.5 collective-permute-start.26
  513.3 5.5 %collective-permute-start.25 = (bf16[512,896]{1,0:T(8,128)(2,1)S(1)}, bf16[512,896]{1,0:T(8,128)(2,1)S(1)}, u32[]{:S(2)}, u32[]{:S(2)}) collective-permute-start(bf16[512,896]{1,0:T(8,128)(2,1)S(1)} %convolution_convert_fusion.1), channel_id=1, source_target_pairs={{0,1},{1,0},{2,3},{3,2},{4,5},{5,4},{6,7},{7,6},{8,9},{9,8},{10,11... | collective-permute-start | bytes 2752520 | tf_op jit(solution)/shard_map/ppermute | solution.py:148
  515.8 22.5 %collective-permute-start.27 = (bf16[512,896]{1,0:T(8,128)(2,1)S(1)}, bf16[512,896]{1,0:T(8,128)(2,1)S(1)}, u32[]{:S(2)}, u32[]{:S(2)}) collective-permute-start(bf16[512,896]{1,0:T(8,128)(2,1)S(1)} %add_convert_fusion.1), channel_id=1, source_target_pairs={{0,2},{2,0},{1,3},{3,1},{4,6},{6,4},{5,7},{7,5},{8,10},{10,8},{9,1... | collective-permute-start | bytes 2752520 | tf_op jit(solution)/shard_map/ppermute | solution.py:148
  538.3 1.7 copy-start.1
Sparse Core Ops, SparseCore 0:
  18.0 78.8 all-gather.3
  158.8 195.3 all-gather.5
  356.4 106.8 all-gather.7
